TPU v7x, 512 devices: a whole 4x4x16 slice. The times are simulated.
512 devices in a mesh: dp: 16 (over z_lo, core), fsdp: 32 (over x, z_hi, y).
Axes of the slice: x: 4, y: 4, z: 16 (z_hi: 2, z_lo: 8; z = z_hi * 8 + z_lo), core: 2. Of those that a mesh axis runs over, the one named last changes fastest.
Arguments:
- hidden_input: bfloat16 [16, 2, 4096, 8192], P('dp', None, 'fsdp'), may hold values from -6 to 6
- readout: bfloat16 [16, 2, 4096, 512], P('dp', None, 'fsdp'), may hold values from -0.26367188 to 0.26367188
- response: int32 [16, 2, 4096], P('dp', None, 'fsdp'), may hold values from 0 to 1, as said below
- value_matrix: bfloat16 [8192, 512], P('fsdp'), may hold values from -0.0625 to 0.0625
- adapter_down: bfloat16 [8192, 64], P('fsdp'), may hold values from -0.0625 to 0.0625
- adapter_up: bfloat16 [64, 512], replicated, may hold values from -0.037353516 to 0.037353516
Outputs:
- down_gradient: float32 [8192, 64], P('fsdp')
- grad_b_t: float32 [512, 64], P('fsdp')
- losses: float32 [16], P('dp')
- margins: float32 [16], P('dp')
Inputs may be any that keep to these rules, and one draw needn't show every extreme that they name: `response`: each sequence's 1s form one contiguous run of tokens that starts between 512 and 2048 and ends between 3072 and 4096.
All inputs are finite; a program needn't handle non-finite values.
Results may differ from a plain program's by a relative error of at most 0.0055.
Values may be sent and summed in bfloat16 or wider, within the bound.
No kernel may reach another device: no remote copies, remote signals or barrier semaphores. Data moves between devices by JAX's collectives and lax.ppermute only.
A program may use at most 64 MiB of HBM per device.

v0:
```python
import jax
import jax.numpy as jnp
from jax import lax
from jax.sharding import PartitionSpec as P

DPO_BETA = 0.5
ADAPTER_SCALE = 2.0


def shards(hidden_input, readout, response, value_matrix, adapter_down, adapter_up):
    seq_rows = hidden_input.shape[2]
    width = hidden_input.shape[3]
    kv_width = value_matrix.shape[1]
    token_row_block = hidden_input.reshape(2 * seq_rows, width)
    base_output = jnp.dot(
        token_row_block,
        lax.all_gather(value_matrix, "fsdp", axis=0, tiled=True),
        preferred_element_type=jnp.float32,
    )
    low_sum = jnp.dot(
        token_row_block,
        lax.all_gather(adapter_down, "fsdp", axis=0, tiled=True),
        preferred_element_type=jnp.float32,
    )
    lowrank_output = low_sum.astype(jnp.bfloat16)
    policy_score = base_output + ADAPTER_SCALE * jnp.dot(
        lowrank_output, adapter_up, preferred_element_type=jnp.float32
    )
    read_f = readout.reshape(2 * seq_rows, kv_width).astype(jnp.float32)
    mask_f = response.reshape(2 * seq_rows).astype(jnp.float32)
    t_pol = jnp.tanh(policy_score)
    t_ref = jnp.tanh(base_output)
    scores = jnp.sum(read_f * (t_pol - t_ref), axis=1) * mask_f
    partial_value = jnp.sum(scores.reshape(2, seq_rows), axis=1)
    ratio = lax.psum(partial_value, "fsdp")
    reward_margin = DPO_BETA * (ratio[0] - ratio[1])
    pair_loss_total = jax.nn.softplus(-reward_margin)
    gate = jax.nn.sigmoid(-reward_margin)
    coef = DPO_BETA * gate * jnp.array([-1.0, 1.0], jnp.float32)
    coef_rows = jnp.repeat(coef, seq_rows)
    hidden_gradient = (
        coef_rows[:, None] * mask_f[:, None] * read_f * (1.0 - t_pol * t_pol)
    ).astype(jnp.bfloat16)
    up_gradient_flipped = ADAPTER_SCALE * lax.dot_general(
        hidden_gradient,
        lowrank_output,
        (((0,), (0,)), ((), ())),
        preferred_element_type=jnp.float32,
    )
    lowrank_gradient = (
        ADAPTER_SCALE
        * lax.dot_general(
            hidden_gradient,
            adapter_up,
            (((1,), (1,)), ((), ())),
            preferred_element_type=jnp.float32,
        )
    ).astype(jnp.bfloat16)
    down_gradient = lax.dot_general(
        token_row_block,
        lowrank_gradient,
        (((0,), (0,)), ((), ())),
        preferred_element_type=jnp.float32,
    )
    summed_a, summed_b = lax.psum((down_gradient, up_gradient_flipped), "dp")
    part_a, part_b = (
        lax.psum_scatter(summed_a, "fsdp", scatter_dimension=0, tiled=True),
        lax.psum_scatter(summed_b, "fsdp", scatter_dimension=0, tiled=True),
    )
    return (part_a, part_b, pair_loss_total.reshape(1), reward_margin.reshape(1))


def solution(mesh):
    placed = (
        P("dp", None, "fsdp", None),
        P("dp", None, "fsdp", None),
        P("dp", None, "fsdp"),
        P("fsdp", None),
        P("fsdp", None),
        P(),
    )
    return jax.shard_map(
        shards,
        mesh=mesh,
        in_specs=placed,
        out_specs=(P("fsdp", None), P("fsdp", None), P("dp"), P("dp")),
        check_vma=False,
    )
```

profile of v0, /device:TPU:1, one launch (start us, length us, event | category | flops | bytes accessed | tf_op | source)
XLA Modules:
  0.0 1336.3 jit_solution(9350286569051517849)
XLA Ops:
  7.2 0.0 copy-start
  7.2 0.0 all-gather.5.cloned.1.call-start
  7.2 0.7 all-gather.5.cloned.1.call-update
  7.9 0.0 all-gather.3.cloned.1.call-start
  8.0 0.7 all-gather.3.cloned.1.call-update
  8.7 0.0 reduce-scatter.3.cloned.1.call-start
  8.7 124.5 %all-gather.5.cloned.1.call-done = bf16[8192,64]{0,1:T(8,128)(2,1)} async-done(((bf16[256,64]{0,1:T(8,128)(2,1)}), bf16[8192,64]{0,1:T(8,128)(2,1)}) %all-gather.5.cloned.1.call-update) | async-done | bytes 1048592 | tf_op jit(solution)/shard_map/all_gather | solution.py:22
  133.2 3.9 convolution_convert_fusion
  137.1 0.0 copy-start.2
  137.1 0.0 copy-start.3
  137.1 232.1 %all-gather.3.cloned.1.call-done = bf16[8192,512]{1,0:T(8,128)(2,1)} async-done(((bf16[256,512]{1,0:T(8,128)(2,1)}), bf16[8192,512]{1,0:T(8,128)(2,1)}) %all-gather.3.cloned.1.call-update) | async-done | bytes 8388624 | tf_op jit(solution)/shard_map/all_gather | solution.py:17
  369.2 7.0 fusion.10
  376.2 0.0 copy-done
  376.2 0.0 copy-done.1
  376.2 0.4 fusion.3
  376.6 0.1 fusion.7
  376.7 134.6 %psum.21 = f32[2]{0:T(128)S(1)} all-reduce(f32[2]{0:T(128)S(1)} %fusion.7), channel_id=1, replica_groups=mesh['dp'=16,'fsdp'=32] {'fsdp'}, use_global_device_ids=true, to_apply=%region_2.0 | all-reduce | flops 2 | bytes 16 | tf_op jit(solution)/shard_map/psum | solution.py:35
  511.4 0.6 fusion.9
  513.4 0.1 bitcast_multiply_fusion
  513.4 0.1 fusion.5
  513.6 4.7 convolution_bitcast_fusion
  518.3 0.0 reduce-scatter.3.cloned.1.call-update
  518.3 0.0 reduce-scatter.5.cloned.1.call-start
  518.4 1.0 convolution_multiply_fusion.1
  519.4 0.0 reduce-scatter.5.cloned.1.call-update
  519.4 0.0 all-reduce.2.cloned.1.call-start
  519.5 309.4 %reduce-scatter.3.cloned.1.call-done = f32[256,64]{0,1:T(8,128)} async-done(((f32[8192,64]{0,1:T(8,128)}), f32[256,64]{0,1:T(8,128)}) %reduce-scatter.3.cloned.1.call-update) | async-done | bytes 65552 | tf_op jit(solution)/shard_map/reduce_scatter | solution.py:67
  828.8 0.0 all-reduce.2.cloned.1.call-update
  828.9 297.9 %reduce-scatter.5.cloned.1.call-done = f32[16,64]{1,0:T(8,128)} async-done(((f32[512,64]{1,0:T(8,128)}), f32[16,64]{1,0:T(8,128)}) %reduce-scatter.5.cloned.1.call-update) | async-done | bytes 4112 | tf_op jit(solution)/shard_map/reduce_scatter | solution.py:68
  1126.8 72.3 %psum.25 = f32[16,64]{1,0:T(8,128)} all-reduce(f32[16,64]{1,0:T(8,128)} %reduce-scatter.5.cloned.1.call-done), channel_id=1, replica_groups=mesh['dp'=16,'fsdp'=32] {'dp'}, use_global_device_ids=true, to_apply=%region_5.6 | all-reduce | flops 1024 | bytes 8192 | tf_op jit(solution)/shard_map/psum | solution.py:65
  1199.1 126.9 %all-reduce.2.cloned.1.call-done = f32[256,64]{0,1:T(8,128)} async-done(((f32[256,64]{0,1:T(8,128)}), f32[256,64]{0,1:T(8,128)}) %all-reduce.2.cloned.1.call-update) | async-done | bytes 65552 | tf_op jit(solution)/shard_map/psum | solution.py:65
  1326.1 1.5 copy.12
  (4 shorter events, 0.0 us)
Async XLA Ops:
  7.2 369.1 %copy-start = (bf16[64,512]{1,0:T(8,128)(2,1)S(1)}, bf16[64,512]{1,0:T(8,128)(2,1)}, u32[]{:S(2)}) copy-start(bf16[64,512]{1,0:T(8,128)(2,1)} %param.12) | copy-start | bytes 196612
  7.2 126.1 %all-gather.5.cloned.1.call-start = ((), (), s32[]{:S(2)}) async-start(), calls=%async_computation.3 | async-start | bytes 1081344 | tf_op jit(solution)/shard_map/all_gather | solution.py:22
  7.9 361.3 %all-gather.3.cloned.1.call-start = ((), (), s32[]{:S(2)}) async-start(), calls=%async_computation.2 | async-start | bytes 8650752 | tf_op jit(solution)/shard_map/all_gather | solution.py:17
  8.7 820.2 %reduce-scatter.3.cloned.1.call-start = ((), (), s32[]{:S(2)}) async-start(), calls=%async_computation.4 | async-start | bytes 2162688 | tf_op jit(solution)/shard_map/reduce_scatter | solution.py:67
  137.1 239.1 %copy-start.1 = (bf16[1,2,128,512]{3,2,1,0:T(8,128)(2,1)S(1)}, bf16[1,2,128,512]{3,2,1,0:T(8,128)(2,1)}, u32[]{:S(2)}) copy-start(bf16[1,2,128,512]{3,2,1,0:T(8,128)(2,1)} %param.8) | copy-start | bytes 786436
  137.1 239.5 %copy-start.2 = (s32[1,2,128]{2,1,0:T(2,128)S(1)}, s32[1,2,128]{2,1,0:T(2,128)}, u32[]{:S(2)}) copy-start(s32[1,2,128]{2,1,0:T(2,128)} %param.9) | copy-start | bytes 3076
  137.1 376.2 %copy-start.3 = (f32[2]{0:T(128)S(1)}, f32[2]{0:T(128)}, u32[]{:S(2)}) copy-start(f32[2]{0:T(128)} %constant.19.clone) | copy-start | bytes 28
  518.3 608.5 %reduce-scatter.5.cloned.1.call-start = ((), (), s32[]{:S(2)}) async-start(), calls=%async_computation.6 | async-start | bytes 270336 | tf_op jit(solution)/shard_map/reduce_scatter | solution.py:68
  519.4 806.6 %all-reduce.2.cloned.1.call-start = ((), (), s32[]{:S(2)}) async-start(), calls=%async_computation.5 | async-start | bytes 131072 | tf_op jit(solution)/shard_map/psum | solution.py:65
Sparse Core Ops, SparseCore 0:
  12.1 121.0 all-gather.4
  137.6 231.5 all-gather.2
  518.5 310.3 reduce-scatter.2
  831.7 295.0 reduce-scatter.4
  1129.6 196.4 all-reduce.1
where the time goes:
time: 1340 us
  waiting for transfers between devices  1090 us (81%)
  blocking collectives  207 us (15%)
  between operations  17.6 us (1%)
  matrix products  17 us (1%)
    reduce_scatter x1, waiting for transfers between devices, shards(): lax.psum_scatter(summed_a, 'fsdp', scatter_dimension=0, tiled=True)  309 us
    reduce_scatter x1, waiting for transfers between devices, shards(): lax.psum_scatter(summed_b, 'fsdp', scatter_dimension=0, tiled=True)  298 us
    all_gather x1, waiting for transfers between devices, shards(): lax.all_gather(value_matrix, 'fsdp', axis=0, tiled=True)  232 us
    psum x1, blocking collectives, shards(): ratio = lax.psum(partial_value, 'fsdp')  135 us
    psum x1, waiting for transfers between devices, shards(): summed_a, summed_b = lax.psum((down_gradient, up_gradient_flipped), 'dp')  127 us
    all_gather x1, waiting for transfers between devices, shards(): lax.all_gather(adapter_down, 'fsdp', axis=0, tiled=True)  125 us
    psum x1, blocking collectives, shards(): summed_a, summed_b = lax.psum((down_gradient, up_gradient_flipped), 'dp')  72.3 us
  transfers between devices with their start and end apart: 5, of which 5 were waited for; matrix products, arithmetic and copies ran while one was open for 0% of the time, Pallas kernels for 0%

commit v1 on v0

v1 whole, which is shorter than its diff:
```python
import jax
import jax.numpy as jnp
import numpy as np
from jax import lax
from jax.experimental import pallas as pl
from jax.experimental.pallas import tpu as pltpu
from jax.sharding import Mesh, PartitionSpec as P

DPO_BETA = 0.5
ADAPTER_SCALE = 2.0
BF16 = jnp.bfloat16
F32 = jnp.float32
LANES = 128
X, Y, ZH, ZL = 4, 4, 2, 8
XY = ("x", "y")
ZZ = ("zl", "zh")
EXTRA = 16


def vmem():
    return pl.BlockSpec(memory_space=pltpu.VMEM)


def params():
    return pltpu.CompilerParams(vmem_limit_bytes=50 * 1024 * 1024)


def pieces(total, shape):
    full = jnp.broadcast_to(total, shape)
    high = full.astype(BF16).astype(F32)
    rest = full - high
    middle = rest.astype(BF16).astype(F32)
    low = rest - middle
    lane = lax.broadcasted_iota(jnp.int32, shape, 1)
    zero = jnp.zeros(shape, F32)
    return jnp.where(lane == 0, high, jnp.where(lane == 1, middle, jnp.where(lane == 2, low, zero)))


def order_kernel(where_ref, hidden_ref, out_ref):
    core, zh = where_ref[0], where_ref[1]
    at = 0
    for core_rel in range(2):
        for zh_rel in range(ZH):
            for x in range(X):
                for y in range(Y):
                    own_core = jnp.where(core_rel == 0, core, 1 - core)
                    own_zh = jnp.where(zh_rel == 0, zh, 1 - zh)
                    start = (((x * ZH + own_zh) * Y + y) * 2 + own_core) * LANES
                    out_ref[core_rel, :, at * LANES : (at + 1) * LANES] = hidden_ref[
                        :, pl.ds(pl.multiple_of(start, LANES), LANES)
                    ]
                    at = (at + 1) % (ZH * X * Y)


def forward_kernel(first, *refs):
    if first:
        mine_ref, other_ref, weight_ref, out_ref = refs
    else:
        mine_ref, other_ref, weight_ref, before_ref, out_ref = refs
    step = pl.program_id(0)
    tokens = mine_ref.shape[0]
    features = weight_ref.shape[2]
    sources = weight_ref.shape[0]
    value = weight_ref[:, :LANES, :].reshape(sources * LANES, features)
    down_t = jnp.concatenate(
        [
            jnp.concatenate(
                [weight_ref[s, LANES:, g * LANES : (g + 1) * LANES] for g in range(features // LANES)], axis=0
            )
            for s in range(sources)
        ],
        axis=1,
    )
    down_t = jnp.concatenate([down_t, jnp.zeros_like(down_t)], axis=0)
    for at, ref in enumerate((mine_ref, other_ref)):
        rows = slice(at * tokens, (at + 1) * tokens)
        base = jnp.dot(ref[...], value, preferred_element_type=F32)
        low = lax.dot_general(ref[...], down_t, (((1,), (1,)), ((), ())), preferred_element_type=F32)

        @pl.when(step == 0)
        def _():
            if first:
                out_ref[rows, :features] = base
                out_ref[rows, features:] = low
            else:
                out_ref[rows, :features] = before_ref[rows, :features] + base
                out_ref[rows, features:] = before_ref[rows, features:] + low

        @pl.when(step != 0)
        def _():
            out_ref[rows, :features] += base
            out_ref[rows, features:] += low


def forward(mine, other, weights, part, before=None):
    tokens = mine.shape[0]
    features = weights.shape[2]
    steps = 4
    sources = X * Y // steps
    wide = sources * LANES
    specs = [
        pl.BlockSpec((tokens, wide), lambda i: (0, part * steps + i)),
        pl.BlockSpec((tokens, wide), lambda i: (0, part * steps + i)),
        pl.BlockSpec((sources,) + weights.shape[1:], lambda i: (i, 0, 0)),
    ]
    given = [mine, other, weights]
    whole = pl.BlockSpec((2 * tokens, features + LANES), lambda i: (0, 0))
    if before is not None:
        specs.append(whole)
        given.append(before)
    return pl.pallas_call(
        lambda *refs: forward_kernel(before is None, *refs),
        grid=(steps,),
        in_specs=specs,
        out_specs=whole,
        out_shape=jax.ShapeDtypeStruct((2 * tokens, features + LANES), F32),
        compiler_params=params(),
        name="forward",
    )(*given)


def middle_kernel(mine_ref, other_ref, hidden_ref, read_ref, mask_ref, up_ref, out_ref):
    tokens, features = read_ref.shape
    rank = up_ref.shape[0] // 2
    base = mine_ref[:tokens, :features] + other_ref[:, :features]
    low = mine_ref[:tokens, features:] + other_ref[:, features:]
    low_b = low.astype(BF16)
    policy = base + ADAPTER_SCALE * jnp.dot(low_b, up_ref[...], preferred_element_type=F32)
    read = read_ref[...].astype(F32)
    sign = jnp.where(lax.broadcasted_iota(jnp.int32, (tokens, 1), 0) < tokens // 2, 1.0, -1.0)
    signed = mask_ref[...] * sign
    t_pol = jnp.tanh(policy)
    t_ref = jnp.tanh(base)
    scores = jnp.sum(read * (t_pol - t_ref), axis=1, keepdims=True) * signed
    total = jnp.sum(scores, axis=0, keepdims=True)
    grad = ((-DPO_BETA * signed) * read * (1.0 - t_pol * t_pol)).astype(BF16)
    low_grad_t = (
        ADAPTER_SCALE
        * lax.dot_general(up_ref[:rank, :], grad, (((1,), (1,)), ((), ())), preferred_element_type=F32)
    ).astype(BF16)
    twice = (low + pltpu.roll(low, rank, 1)).astype(BF16)
    up_grad = ADAPTER_SCALE * lax.dot_general(
        grad, twice, (((0,), (0,)), ((), ())), preferred_element_type=F32
    )
    wide = 2 * LANES
    part = features // (X * ZH * Y)
    lane = lax.broadcasted_iota(jnp.int32, (EXTRA, LANES), 1)
    sent = pieces(total, (EXTRA, LANES)).astype(BF16)
    for x in range(X):
        for y in range(Y):
            to = x * Y + y
            places = [(x * ZH + zh) * Y + y for zh in range(ZH)]
            for zh, s in enumerate(places):
                out_ref[to, zh * rank : (zh + 1) * rank, :] = jnp.dot(
                    low_grad_t, hidden_ref[:, s * wide : (s + 1) * wide], preferred_element_type=F32
                ).astype(BF16)
            both = jnp.where(
                lane < rank,
                up_grad[places[0] * part : (places[0] + 1) * part, :],
                up_grad[places[1] * part : (places[1] + 1) * part, :],
            )
            out_ref[to, ZH * rank :, :LANES] = both.astype(BF16)
            out_ref[to, ZH * rank :, LANES:] = sent


def plane_kernel(got_ref, out_ref):
    rank = (got_ref.shape[1] - EXTRA) // ZH
    rows = rank // ZL
    total = got_ref[0].astype(F32)
    for s in range(1, got_ref.shape[0]):
        total = total + got_ref[s].astype(F32)
    first = ZH * rank
    margin = jnp.sum(total[first : first + 1, LANES:], axis=1, keepdims=True)
    sent = pieces(margin, (8, LANES))
    lane = lax.broadcasted_iota(jnp.int32, (8, LANES), 1)
    upper = total[first : first + 8, :LANES]
    lower = total[first + 8 : first + 16, :LANES]
    packed = [
        jnp.where(lane < rank, upper, pltpu.roll(lower, rank, 1)),
        jnp.where(lane < rank, pltpu.roll(upper, rank, 1), lower),
    ]
    for zl in range(ZL):
        for zh in range(ZH):
            start = zh * rank + zl * rows
            tail = jnp.concatenate([packed[zh], sent], axis=1)
            out_ref[zl * ZH + zh] = jnp.concatenate(
                [total[start : start + rows, :], tail], axis=0
            ).astype(BF16)


def gate_kernel(got_ref, out_ref, diff_ref):
    total = None
    for zl in range(ZL):
        pair = got_ref[zl * ZH].astype(F32) + got_ref[zl * ZH + 1].astype(F32)
        diff = jnp.sum(pair[8:9, LANES:], axis=1, keepdims=True)
        gate = 1.0 / (1.0 + jnp.exp(DPO_BETA * diff))
        total = gate * pair if total is None else total + gate * pair
        diff_ref[zl : zl + 1, :] = jnp.broadcast_to(diff, (1, LANES))
    out_ref[...] = total


def shards(hidden_input, readout, response, value_matrix, adapter_down, adapter_up):
    seq_rows, width = hidden_input.shape[2:]
    tokens = 2 * seq_rows
    features = value_matrix.shape[1]
    rank = adapter_down.shape[1]
    core, zh, zl = lax.axis_index("core"), lax.axis_index("zh"), lax.axis_index("zl")
    hidden = hidden_input.reshape(tokens, width)

    value_half = lax.dynamic_slice_in_dim(value_matrix, core * LANES, LANES, 0)
    down_half = lax.dynamic_slice_in_dim(adapter_down, core * LANES, LANES, 0)
    packed = down_half.T.reshape(features // LANES, EXTRA, LANES).transpose(1, 0, 2).reshape(EXTRA, features)
    weights = jnp.concatenate([value_half, packed], axis=0)
    spots = [(a, c, b, e, d) for a in range(ZL) for c in range(2) for b in range(X) for e in range(ZH) for d in range(Y)]
    sizes = (ZL, 2, X, ZH, Y)
    axes = ("zl", "core", "x", "zh", "y")
    flat = lambda p: int(np.ravel_multi_index(p, sizes))
    swap_zh = [(flat(p), flat((p[0], p[1], p[2], 1 - p[3], p[4]))) for p in spots]
    swap_core = [(0, 1), (1, 0)]

    weights_far = lax.ppermute(weights, axes, swap_zh)
    spread = lambda w: lax.all_to_all(jnp.broadcast_to(w[None], (X * Y,) + w.shape), XY, 0, 0)
    near = spread(weights)

    halves = pl.pallas_call(
        order_kernel,
        in_specs=[pl.BlockSpec(memory_space=pltpu.SMEM), vmem()],
        out_specs=vmem(),
        out_shape=jax.ShapeDtypeStruct((2, tokens, width // 2), BF16),
        compiler_params=params(),
        name="order",
    )(jnp.stack([core, zh]).astype(jnp.int32), hidden)
    mine = halves[0]
    other = lax.ppermute(halves[1], "core", swap_core)

    far = spread(weights_far)
    part = forward(mine, other, near, 0)
    part = forward(mine, other, far, 1, part)
    from_other = lax.ppermute(part[tokens:], "core", swap_core)

    read = readout.reshape(tokens, features)
    mask = response.reshape(tokens, 1).astype(F32)
    up = jnp.pad(adapter_up, ((0, rank), (0, 0)))
    wide = width // (X * ZH * Y)
    sends = pl.pallas_call(
        middle_kernel,
        in_specs=[vmem()] * 6,
        out_specs=vmem(),
        out_shape=jax.ShapeDtypeStruct((X * Y, ZH * rank + EXTRA, wide), BF16),
        compiler_params=params(),
        name="middle",
    )(part, from_other, hidden, read, mask, up)
    got = lax.all_to_all(sends, XY, 0, 0)
    along = pl.pallas_call(
        plane_kernel,
        in_specs=[vmem()],
        out_specs=vmem(),
        out_shape=jax.ShapeDtypeStruct((ZL * ZH, 16, wide), BF16),
        compiler_params=params(),
        name="plane",
    )(got)
    got = lax.all_to_all(along, ZZ, 0, 0)
    gated, diffs = pl.pallas_call(
        gate_kernel,
        in_specs=[vmem()],
        out_specs=[vmem(), vmem()],
        out_shape=[jax.ShapeDtypeStruct((16, wide), F32), jax.ShapeDtypeStruct((ZL, LANES), F32)],
        compiler_params=params(),
        name="gate",
    )(got)
    summed = lax.psum(gated, "core")
    rows = rank // ZL
    all_rows = lax.all_to_all(jnp.broadcast_to(summed[None, :rows], (ZL, rows, wide)), "zl", 0, 0)
    down_gradient = all_rows.reshape(rank, wide).T
    up_part = jnp.concatenate([summed[8:16, :rank], summed[8:16, rank : 2 * rank]], axis=0)
    margin = DPO_BETA * lax.dynamic_slice(diffs, (zl, 0), (1, 1)).reshape(1)
    return down_gradient, up_part, jax.nn.softplus(-margin), margin


def solution(mesh):
    fine = Mesh(np.asarray(mesh.devices).reshape(ZL, 2, X, ZH, Y), ("zl", "core", "x", "zh", "y"))
    dp, fsdp = ("zl", "core"), ("x", "zh", "y")
    placed = (
        P(dp, None, fsdp, None),
        P(dp, None, fsdp, None),
        P(dp, None, fsdp),
        P(fsdp, None),
        P(fsdp, None),
        P(),
    )
    return jax.shard_map(
        shards,
        mesh=fine,
        in_specs=placed,
        out_specs=(P(fsdp, None), P(fsdp, None), P(dp), P(dp)),
        check_vma=False,
    )
```

time: 1340 us -> 172 us (0.13)
  waiting for transfers between devices: 1090 us -> 42.9 us
  blocking collectives: 207 us -> 27.8 us
  starting transfers between devices: 0.2 us -> 62.5 us
  Pallas kernels: 0 us -> 20.7 us
  matrix products: 17 us -> 0 us
  between operations: 17.6 us -> 2.71 us
    reduce_scatter x2 -> x0, waiting for transfers between devices: 607 us -> none  [the longest x1 309 us: shards(): lax.psum_scatter(summed_a, 'fsdp', scatter_dimension=0, tiled=True)]
    all_gather x2 -> x0, waiting for transfers between devices: 357 us -> none  [the longest x1 232 us: shards(): lax.all_gather(value_matrix, 'fsdp', axis=0, tiled=True)]
    psum x2 -> x1, blocking collectives: 207 us -> 6.63 us  [shards(): summed = lax.psum(gated, 'core')]
    psum x1 -> x0, waiting for transfers between devices: 127 us -> none  [shards(): summed_a, summed_b = lax.psum((down_gradient, up_gradient_flipped), 'dp')]
    all_to_all x0 -> x4, waiting for transfers between devices: none -> 37.7 us  [the longest x2 15.6 us: shards(): lax.all_to_all(jnp.broadcast_to(w[None], (X * Y,) + w.shape), XY, 0, 0)]
    all_to_all x0 -> x4, starting transfers between devices: none -> 34.3 us  [the longest x1 16 us: shards(): got = lax.all_to_all(along, ZZ, 0, 0)]
    ppermute x0 -> x3, starting transfers between devices: none -> 28.3 us  [the longest x1 15.4 us: shards(): weights_far = lax.ppermute(weights, axes, swap_zh)]
    all_to_all x0 -> x1, blocking collectives: none -> 21.2 us  [shards(): got = lax.all_to_all(sends, XY, 0, 0)]
  transfers between devices with their start and end apart: 5 -> 7, of which waited for: 5 -> 6; matrix products, arithmetic and copies ran while one was open for 0% -> 2% of each run, Pallas kernels for 0% -> 6%
where the time goes in v1:
time: 172 us; the launch traced here: 171 us
  starting transfers between devices  62.5 us (36%)
  waiting for transfers between devices  42.9 us (25%)
  blocking collectives  27.8 us (16%)
  Pallas kernels  20.7 us (12%)
  local copies, waits for them, and re-layouts  13.4 us (8%)
  between operations  2.71 us (2%)
    all_to_all x1, blocking collectives, shards(): got = lax.all_to_all(sends, XY, 0, 0)  21.2 us
    all_to_all x1, starting transfers between devices, shards(): got = lax.all_to_all(along, ZZ, 0, 0)  16 us
    all_to_all x2, waiting for transfers between devices, shards(): lax.all_to_all(jnp.broadcast_to(w[None], (X * Y,) + w.shape), XY, 0, 0)  15.6 us
    ppermute x1, starting transfers between devices, shards(): weights_far = lax.ppermute(weights, axes, swap_zh)  15.4 us
    all_to_all x2, starting transfers between devices, shards(): lax.all_to_all(jnp.broadcast_to(w[None], (X * Y,) + w.shape), XY, 0, 0)  14.9 us
    all_to_all x1, waiting for transfers between devices, shards(): got = lax.all_to_all(along, ZZ, 0, 0)  13 us
    pallas_call x2, Pallas kernels, forward(): pl.pallas_call(lambda *refs: forward_kernel(before is None, *refs), grid=...  10.9 us
    all_to_all x1, waiting for transfers between devices, shards(): lax.all_to_all(jnp.broadcast_to(summed[None, :rows], (ZL, rows, wide)), '...  9.1 us
  transfers between devices with their start and end apart: 7, of which 6 were waited for; matrix products, arithmetic and copies ran while one was open for 2% of the time, Pallas kernels for 6%

profile of v1, /device:TPU:1, one launch (start us, length us, event | category | flops | bytes accessed | tf_op | source)
XLA Modules:
  0.0 171.2 jit_solution(15572628477109758424)
XLA Ops:
  0.7 0.9 copy-done
  1.6 0.7 constant_dynamic-slice_fusion.1
  2.3 1.7 broadcast_in_dim.7
  4.0 7.6 %all-to-all-start.1 = ((bf16[16,144,512]{2,1,0:T(8,128)(2,1)}), bf16[16,144,512]{2,1,0:T(8,128)(2,1)S(1)}, u32[]{:S(2)}, u32[]{:S(2)}) async-start(bf16[16,144,512]{2,1,0:T(8,128)(2,1)} %broadcast_in_dim.7), calls=%async_computation.1 | async-start | bytes 4718592 | tf_op jit(solution)/shard_map/all_to_all | solution.py:222
  11.6 15.4 %collective-permute-start.1 = (bf16[144,512]{1,0:T(8,128)(2,1)S(1)}, bf16[144,512]{1,0:T(8,128)(2,1)S(1)}, u32[]{:S(2)}, u32[]{:S(2)}) collective-permute-start(bf16[144,512]{1,0:T(8,128)(2,1)S(1)} %pad_maximum_fusion), channel_id=1, source_target_pairs={{0,4},{1,5},{2,6},{3,7},{4,0},{5,1},{6,2},{7,3},{8,12},{9,13},{10,... | collective-permute-start | bytes 442376 | tf_op jit(solution)/shard_map/ppermute | solution.py:221
  27.2 5.3 %order.1 = bf16[2,256,4096]{2,1,0:T(8,128)(2,1)} custom-call(s32[2]{0:T(128)S(1)} %pad_add_fusion.where_ref, bf16[256,8192]{1,0:T(8,128)(2,1)} %bitcast.23), custom_call_target="tpu_custom_call" | custom-call | tf_op jit(solution)/shard_map/order/pallas_call | solution.py:225
  32.4 6.9 %all-to-all-done.1.refs_2_ = bf16[16,144,512]{2,1,0:T(8,128)(2,1)S(1)} async-done(((bf16[16,144,512]{2,1,0:T(8,128)(2,1)}), bf16[16,144,512]{2,1,0:T(8,128)(2,1)S(1)}, u32[]{:S(2)}, u32[]{:S(2)}) %all-to-all-start.1) | async-done | bytes 2359328 | tf_op jit(solution)/shard_map/all_to_all | solution.py:222
  39.3 1.8 %broadcast_in_dim.6 = bf16[16,144,512]{2,1,0:T(8,128)(2,1)} broadcast(bf16[144,512]{1,0:T(8,128)(2,1)S(1)} %collective-permute-done.1), dimensions={1,2} | broadcast | bytes 2506752 | tf_op jit(solution)/shard_map/broadcast_in_dim | solution.py:222
  41.5 7.3 %all-to-all-start = ((bf16[16,144,512]{2,1,0:T(8,128)(2,1)}), bf16[16,144,512]{2,1,0:T(8,128)(2,1)}, u32[]{:S(2)}, u32[]{:S(2)}) async-start(bf16[16,144,512]{2,1,0:T(8,128)(2,1)} %broadcast_in_dim.6), calls=%async_computation | async-start | bytes 4718592 | tf_op jit(solution)/shard_map/all_to_all | solution.py:222
  48.9 2.6 %slice_bitcast_fusion = (bf16[256,4096]{1,0:T(8,128)(2,1)S(1)}, bf16[256,4096]{1,0:T(8,128)(2,1)S(1)}) fusion(bf16[2,256,4096]{2,1,0:T(8,128)(2,1)} %order.1), kind=kLoop, calls=%fused_computation | loop fusion | bytes 8388608 | tf_op jit(solution)/shard_map/squeeze | solution.py:234
  51.5 5.0 %collective-permute-start = (bf16[256,4096]{1,0:T(8,128)(2,1)S(1)}, bf16[256,4096]{1,0:T(8,128)(2,1)S(1)}, u32[]{:S(2)}, u32[]{:S(2)}) collective-permute-start(bf16[256,4096]{1,0:T(8,128)(2,1)S(1)} %get-tuple-element.8), channel_id=1, source_target_pairs={{0,32},{32,0},{1,33},{33,1},{2,34},{34,2},{3,35},{35,3},{4,36},{36... | collective-permute-start | bytes 6291464 | tf_op jit(solution)/shard_map/ppermute | solution.py:234
  56.5 3.8 %collective-permute-done.refs_1_ = bf16[256,4096]{1,0:T(8,128)(2,1)S(1)} collective-permute-done((bf16[256,4096]{1,0:T(8,128)(2,1)S(1)}, bf16[256,4096]{1,0:T(8,128)(2,1)S(1)}, u32[]{:S(2)}, u32[]{:S(2)}) %collective-permute-start) | collective-permute-done | bytes 2097184 | tf_op jit(solution)/shard_map/ppermute | solution.py:234
  60.2 1.3 copy-done.6
  61.5 5.3 %forward.2.refs_3_ = f32[512,640]{1,0:T(8,128)S(1)} custom-call(bf16[256,4096]{1,0:T(8,128)(2,1)S(1)} %get-tuple-element.9.refs_0_, bf16[256,4096]{1,0:T(8,128)(2,1)} %copy-done.6, bf16[16,144,512]{2,1,0:T(8,128)(2,1)} %copy-done.5), custom_call_target="tpu_custom_call" | custom-call | tf_op jit(solution)/shard_map/forward/pallas_call | solution.py:111
  66.9 1.0 copy-done.2
  67.9 8.7 %all-to-all-done.refs_2_ = bf16[16,144,512]{2,1,0:T(8,128)(2,1)} async-done(((bf16[16,144,512]{2,1,0:T(8,128)(2,1)}), bf16[16,144,512]{2,1,0:T(8,128)(2,1)}, u32[]{:S(2)}, u32[]{:S(2)}) %all-to-all-start) | async-done | bytes 2359328 | tf_op jit(solution)/shard_map/all_to_all | solution.py:222
  76.6 1.3 copy-done.3
  77.9 5.6 %forward.3.mine_ref = f32[512,640]{1,0:T(8,128)S(1)} custom-call(bf16[256,4096]{1,0:T(8,128)(2,1)} %copy-done.1, bf16[256,4096]{1,0:T(8,128)(2,1)} %copy-done.6, bf16[16,144,512]{2,1,0:T(8,128)(2,1)} %all-to-all-done.refs_2_, f32[512,640]{1,0:T(8,128)S(1)} %copy-done.3), custom_call_target="tpu_custom_call" | custom-call | tf_op jit(solution)/shard_map/forward/pallas_call | solution.py:111
  83.6 7.9 %collective-permute-start.2 = (f32[256,640]{1,0:T(8,128)S(1)}, f32[256,640]{1,0:T(8,128)S(1)}, u32[]{:S(2)}, u32[]{:S(2)}) collective-permute-start(f32[256,640]{1,0:T(8,128)S(1)} %slice.26), channel_id=1, source_target_pairs={{0,32},{32,0},{1,33},{33,1},{2,34},{34,2},{3,35},{35,3},{4,36},{36... | collective-permute-start | bytes 1966088 | tf_op jit(solution)/shard_map/ppermute | solution.py:239
  91.6 1.5 collective-permute-done.2.other_ref
  93.2 3.5 %middle.1 = bf16[16,144,256]{2,1,0:T(8,128)(2,1)S(1)} custom-call(f32[512,640]{1,0:T(8,128)S(1)} %forward.3.mine_ref, f32[256,640]{1,0:T(8,128)S(1)} %collective-permute-done.2.other_ref, bf16[256,8192]{1,0:T(8,128)(2,1)} %bitcast.24, bf16[256,512]{1,0:T(8,128)(2,1)S(1)} %bitcast.22, f32[256,1]{1,0:T(8,128)S(1)} %copy.12.mask_ref, ...), custom_call_target="tpu_custom_call" | custom-call | tf_op jit(solution)/shard_map/middle/pallas_call | solution.py:245
  96.7 21.2 %all_to_all.25.got_ref = bf16[16,144,256]{2,1,0:T(8,128)(2,1)S(1)} all-to-all(bf16[16,144,256]{2,1,0:T(8,128)(2,1)S(1)} %middle.1), channel_id=1, replica_groups=mesh['zl'=8,'core'=2,'x'=4,'zh'=2,'y'=4] {'x','y'}, dimensions={0} | all-to-all | bytes 2359296 | tf_op jit(solution)/shard_map/all_to_all | solution.py:253
  117.9 0.9 plane.1
  118.7 16.0 %all-to-all-start.3 = ((bf16[16,16,256]{2,1,0:T(8,128)(2,1)}), bf16[16,16,256]{2,1,0:T(8,128)(2,1)S(1)}, u32[]{:S(2)}, u32[]{:S(2)}) async-start(bf16[16,16,256]{2,1,0:T(8,128)(2,1)} %plane.1), calls=%async_computation.3 | async-start | bytes 262144 | tf_op jit(solution)/shard_map/all_to_all | solution.py:262
  134.7 13.0 %all-to-all-done.3.got_ref = bf16[16,16,256]{2,1,0:T(8,128)(2,1)S(1)} async-done(((bf16[16,16,256]{2,1,0:T(8,128)(2,1)}), bf16[16,16,256]{2,1,0:T(8,128)(2,1)S(1)}, u32[]{:S(2)}, u32[]{:S(2)}) %all-to-all-start.3) | async-done | bytes 131104 | tf_op jit(solution)/shard_map/all_to_all | solution.py:262
  147.8 0.5 fusion.1
  149.1 6.6 %psum.7 = f32[16,256]{1,0:T(8,128)S(1)} all-reduce(f32[16,256]{1,0:T(8,128)S(1)} %get-tuple-element.6), channel_id=1, replica_groups=mesh['zl'=8,'core'=2,'x'=4,'zh'=2,'y'=4] {'core'}, use_global_device_ids=true, to_apply=%region_0.1 | all-reduce | flops 4096 | bytes 32768 | tf_op jit(solution)/shard_map/psum | solution.py:271
  155.7 0.6 broadcast_in_dim.8
  156.3 3.4 %all-to-all-start.4 = ((f32[8,8,256]{2,1,0:T(8,128)}), f32[8,8,256]{2,1,0:T(8,128)S(1)}, u32[]{:S(2)}, u32[]{:S(2)}) async-start(f32[8,8,256]{2,1,0:T(8,128)} %broadcast_in_dim.8), calls=%async_computation.4 | async-start | bytes 131072 | tf_op jit(solution)/shard_map/all_to_all | solution.py:273
  159.8 0.6 pad_maximum_fusion.1
  160.4 9.1 %all-to-all-done.4 = f32[8,8,256]{2,1,0:T(8,128)S(1)} async-done(((f32[8,8,256]{2,1,0:T(8,128)}), f32[8,8,256]{2,1,0:T(8,128)S(1)}, u32[]{:S(2)}, u32[]{:S(2)}) %all-to-all-start.4) | async-done | bytes 65568 | tf_op jit(solution)/shard_map/all_to_all | solution.py:273
  169.5 0.6 copy.17
  (26 shorter events, 0.8 us)
Async XLA Ops:
  0.6 1.0 copy-start
  4.0 35.3 %all-to-all-start.1 = ((bf16[16,144,512]{2,1,0:T(8,128)(2,1)}), bf16[16,144,512]{2,1,0:T(8,128)(2,1)S(1)}, u32[]{:S(2)}, u32[]{:S(2)}) async-start(bf16[16,144,512]{2,1,0:T(8,128)(2,1)} %broadcast_in_dim.7), calls=%async_computation.1 | async-start | bytes 4718592 | tf_op jit(solution)/shard_map/all_to_all | solution.py:222
  11.6 20.8 %collective-permute-start.1 = (bf16[144,512]{1,0:T(8,128)(2,1)S(1)}, bf16[144,512]{1,0:T(8,128)(2,1)S(1)}, u32[]{:S(2)}, u32[]{:S(2)}) collective-permute-start(bf16[144,512]{1,0:T(8,128)(2,1)S(1)} %pad_maximum_fusion), channel_id=1, source_target_pairs={{0,4},{1,5},{2,6},{3,7},{4,0},{5,1},{6,2},{7,3},{8,12},{9,13},{10,... | collective-permute-start | bytes 442376 | tf_op jit(solution)/shard_map/ppermute | solution.py:221
  39.3 2.2 %copy-start.5 = (bf16[16,144,512]{2,1,0:T(8,128)(2,1)}, bf16[16,144,512]{2,1,0:T(8,128)(2,1)S(1)}, u32[]{:S(2)}) copy-start(bf16[16,144,512]{2,1,0:T(8,128)(2,1)S(1)} %all-to-all-done.1.refs_2_) | copy-start | bytes 7077892
  41.5 35.1 %all-to-all-start = ((bf16[16,144,512]{2,1,0:T(8,128)(2,1)}), bf16[16,144,512]{2,1,0:T(8,128)(2,1)}, u32[]{:S(2)}, u32[]{:S(2)}) async-start(bf16[16,144,512]{2,1,0:T(8,128)(2,1)} %broadcast_in_dim.6), calls=%async_computation | async-start | bytes 4718592 | tf_op jit(solution)/shard_map/all_to_all | solution.py:222
  51.5 15.4 %copy-start.1 = (bf16[256,4096]{1,0:T(8,128)(2,1)}, bf16[256,4096]{1,0:T(8,128)(2,1)S(1)}, u32[]{:S(2)}) copy-start(bf16[256,4096]{1,0:T(8,128)(2,1)S(1)} %get-tuple-element.9.refs_0_) | copy-start | bytes 6291460
  51.5 8.8 %collective-permute-start = (bf16[256,4096]{1,0:T(8,128)(2,1)S(1)}, bf16[256,4096]{1,0:T(8,128)(2,1)S(1)}, u32[]{:S(2)}, u32[]{:S(2)}) collective-permute-start(bf16[256,4096]{1,0:T(8,128)(2,1)S(1)} %get-tuple-element.8), channel_id=1, source_target_pairs={{0,32},{32,0},{1,33},{33,1},{2,34},{34,2},{3,35},{35,3},{4,36},{36... | collective-permute-start | bytes 6291464 | tf_op jit(solution)/shard_map/ppermute | solution.py:234
  60.2 1.3 copy-start.6
  66.9 1.0 copy-start.2
  76.6 1.3 copy-start.3
  77.9 13.5 %copy-start.8 = (s32[1,2,128]{2,1,0:T(2,128)S(1)}, s32[1,2,128]{2,1,0:T(2,128)}, u32[]{:S(2)}) copy-start(s32[1,2,128]{2,1,0:T(2,128)} %param.8) | copy-start | bytes 3076
  77.9 13.7 %copy-start.7 = (bf16[64,512]{1,0:T(8,128)(2,1)S(1)}, bf16[64,512]{1,0:T(8,128)(2,1)}, u32[]{:S(2)}) copy-start(bf16[64,512]{1,0:T(8,128)(2,1)} %param.11) | copy-start | bytes 196612
  77.9 15.2 %copy-start.4 = (bf16[1,2,128,512]{3,2,1,0:T(8,128)(2,1)S(1)}, bf16[1,2,128,512]{3,2,1,0:T(8,128)(2,1)}, u32[]{:S(2)}) copy-start(bf16[1,2,128,512]{3,2,1,0:T(8,128)(2,1)} %param.7) | copy-start | bytes 786436
  83.6 9.6 %collective-permute-start.2 = (f32[256,640]{1,0:T(8,128)S(1)}, f32[256,640]{1,0:T(8,128)S(1)}, u32[]{:S(2)}, u32[]{:S(2)}) collective-permute-start(f32[256,640]{1,0:T(8,128)S(1)} %slice.26), channel_id=1, source_target_pairs={{0,32},{32,0},{1,33},{33,1},{2,34},{34,2},{3,35},{35,3},{4,36},{36... | collective-permute-start | bytes 1966088 | tf_op jit(solution)/shard_map/ppermute | solution.py:239
  118.7 29.0 %all-to-all-start.3 = ((bf16[16,16,256]{2,1,0:T(8,128)(2,1)}), bf16[16,16,256]{2,1,0:T(8,128)(2,1)S(1)}, u32[]{:S(2)}, u32[]{:S(2)}) async-start(bf16[16,16,256]{2,1,0:T(8,128)(2,1)} %plane.1), calls=%async_computation.3 | async-start | bytes 262144 | tf_op jit(solution)/shard_map/all_to_all | solution.py:262
  156.3 13.1 %all-to-all-start.4 = ((f32[8,8,256]{2,1,0:T(8,128)}), f32[8,8,256]{2,1,0:T(8,128)S(1)}, u32[]{:S(2)}, u32[]{:S(2)}) async-start(f32[8,8,256]{2,1,0:T(8,128)} %broadcast_in_dim.8), calls=%async_computation.4 | async-start | bytes 131072 | tf_op jit(solution)/shard_map/all_to_all | solution.py:273

commit v2 on v1

--- a/solution.py
+++ b/solution.py
@@ -22,7 +22,7 @@
 
 
 def params():
-    return pltpu.CompilerParams(vmem_limit_bytes=50 * 1024 * 1024)
+    return pltpu.CompilerParams(vmem_limit_bytes=28 * 1024 * 1024)
 
 
 def pieces(total, shape):
@@ -36,94 +36,121 @@
     return jnp.where(lane == 0, high, jnp.where(lane == 1, middle, jnp.where(lane == 2, low, zero)))
 
 
-def order_kernel(where_ref, hidden_ref, out_ref):
+def order_kernel(where_ref, hidden_ref, mine_ref, other_ref):
     core, zh = where_ref[0], where_ref[1]
-    at = 0
-    for core_rel in range(2):
-        for zh_rel in range(ZH):
-            for x in range(X):
-                for y in range(Y):
-                    own_core = jnp.where(core_rel == 0, core, 1 - core)
-                    own_zh = jnp.where(zh_rel == 0, zh, 1 - zh)
-                    start = (((x * ZH + own_zh) * Y + y) * 2 + own_core) * LANES
-                    out_ref[core_rel, :, at * LANES : (at + 1) * LANES] = hidden_ref[
-                        :, pl.ds(pl.multiple_of(start, LANES), LANES)
-                    ]
-                    at = (at + 1) % (ZH * X * Y)
-
-
-def forward_kernel(first, *refs):
-    if first:
-        mine_ref, other_ref, weight_ref, out_ref = refs
-    else:
-        mine_ref, other_ref, weight_ref, before_ref, out_ref = refs
-    step = pl.program_id(0)
-    tokens = mine_ref.shape[0]
+    for own_core, out_ref in ((core, mine_ref), (1 - core, other_ref)):
+        at = 0
+        for own_zh in (zh, 1 - zh):
+            for x, y in BLOCKS:
+                start = (((x * ZH + own_zh) * Y + y) * 2 + own_core) * LANES
+                out_ref[:, at * LANES : (at + 1) * LANES] = hidden_ref[
+                    :, pl.ds(pl.multiple_of(start, LANES), LANES)
+                ]
+                at += 1
+
+
+def unpacked(weight_ref):
+    sources, _, features = weight_ref.shape
+    value = weight_ref[:, :LANES, :].reshape(sources * LANES, features)
+    down_t = [
+        jnp.concatenate(
+            [weight_ref[s, LANES:, g * LANES : (g + 1) * LANES] for g in range(features // LANES)], axis=0
+        )
+        for s in range(sources)
+    ]
+    return value, down_t
+
+
+def low_part(hidden, down_t):
+    down_t = jnp.concatenate(down_t, axis=1)
+    down_t = jnp.concatenate([down_t, jnp.zeros((LANES - down_t.shape[0], down_t.shape[1]), BF16)], axis=0)
+    return lax.dot_general(hidden, down_t, (((1,), (1,)), ((), ())), preferred_element_type=F32)
+
+
+def near_kernel(mine_ref, other_ref, weight_ref, out_mine_ref, out_other_ref):
     features = weight_ref.shape[2]
-    sources = weight_ref.shape[0]
-    value = weight_ref[:, :LANES, :].reshape(sources * LANES, features)
-    down_t = jnp.concatenate(
-        [
-            jnp.concatenate(
-                [weight_ref[s, LANES:, g * LANES : (g + 1) * LANES] for g in range(features // LANES)], axis=0
-            )
-            for s in range(sources)
-        ],
-        axis=1,
-    )
-    down_t = jnp.concatenate([down_t, jnp.zeros_like(down_t)], axis=0)
-    for at, ref in enumerate((mine_ref, other_ref)):
-        rows = slice(at * tokens, (at + 1) * tokens)
-        base = jnp.dot(ref[...], value, preferred_element_type=F32)
-        low = lax.dot_general(ref[...], down_t, (((1,), (1,)), ((), ())), preferred_element_type=F32)
-
-        @pl.when(step == 0)
-        def _():
-            if first:
-                out_ref[rows, :features] = base
-                out_ref[rows, features:] = low
-            else:
-                out_ref[rows, :features] = before_ref[rows, :features] + base
-                out_ref[rows, features:] = before_ref[rows, features:] + low
-
-        @pl.when(step != 0)
-        def _():
-            out_ref[rows, :features] += base
-            out_ref[rows, features:] += low
-
-
-def forward(mine, other, weights, part, before=None):
-    tokens = mine.shape[0]
-    features = weights.shape[2]
-    steps = 4
-    sources = X * Y // steps
-    wide = sources * LANES
-    specs = [
-        pl.BlockSpec((tokens, wide), lambda i: (0, part * steps + i)),
-        pl.BlockSpec((tokens, wide), lambda i: (0, part * steps + i)),
-        pl.BlockSpec((sources,) + weights.shape[1:], lambda i: (i, 0, 0)),
-    ]
-    given = [mine, other, weights]
-    whole = pl.BlockSpec((2 * tokens, features + LANES), lambda i: (0, 0))
-    if before is not None:
-        specs.append(whole)
-        given.append(before)
+    value, down_t = unpacked(weight_ref)
+    for ref, out_ref in ((mine_ref, out_mine_ref), (other_ref, out_other_ref)):
+        hidden = ref[...]
+        out_ref[:, :features] = jnp.dot(hidden, value, preferred_element_type=F32)
+        out_ref[:, features:] = low_part(hidden, down_t)
+
+
+def far_kernel(hidden_ref, first_ref, second_ref, before_ref, out_ref):
+    half = first_ref.shape[2]
+    first, first_t = unpacked(first_ref)
+    second, second_t = unpacked(second_ref)
+    hidden = hidden_ref[...]
+    turned = jnp.concatenate(
+        [hidden[:, BLOCKS.index(p) * LANES : (BLOCKS.index(p) + 1) * LANES] for p in TURNED], axis=1
+    )
+    down_t = [jnp.concatenate([first_t[k], second_t[TURNED.index(p)]], axis=0) for k, p in enumerate(BLOCKS)]
+    out_ref[:, :half] = before_ref[:, :half] + jnp.dot(hidden, first, preferred_element_type=F32)
+    out_ref[:, half : 2 * half] = before_ref[:, half : 2 * half] + jnp.dot(
+        turned, second, preferred_element_type=F32
+    )
+    out_ref[:, 2 * half :] = before_ref[:, 2 * half :] + low_part(hidden, down_t)
+
+
+def half_of(tokens, half, part):
+    return pl.BlockSpec((tokens, half), lambda i: (0, part))
+
+
+def whole(shape):
+    return pl.BlockSpec(shape, lambda i: (0,) * len(shape))
+
+
+def near_forward(mine, other, weights):
+    tokens, half = mine.shape[0], mine.shape[1] // 2
+    out = (tokens, weights.shape[2] + LANES)
     return pl.pallas_call(
-        lambda *refs: forward_kernel(before is None, *refs),
-        grid=(steps,),
-        in_specs=specs,
-        out_specs=whole,
-        out_shape=jax.ShapeDtypeStruct((2 * tokens, features + LANES), F32),
-        compiler_params=params(),
-        name="forward",
-    )(*given)
+        near_kernel,
+        grid=(1,),
+        in_specs=[half_of(tokens, half, 0), half_of(tokens, half, 0), whole(weights.shape)],
+        out_specs=[whole(out)] * 2,
+        out_shape=[jax.ShapeDtypeStruct(out, F32)] * 2,
+        compiler_params=params(),
+        name="near",
+    )(mine, other, weights)
+
+
+def far_forward(hidden, first, second, before):
+    tokens, half = hidden.shape[0], hidden.shape[1] // 2
+    return pl.pallas_call(
+        far_kernel,
+        grid=(1,),
+        in_specs=[half_of(tokens, half, 1), whole(first.shape), whole(second.shape), whole(before.shape)],
+        out_specs=whole(before.shape),
+        out_shape=jax.ShapeDtypeStruct(before.shape, F32),
+        compiler_params=params(),
+        name="far",
+    )(hidden, first, second, before)
+
+
+EVEN_FIRST = ((0, 1), (2, 3)), ((1, 2), (0, 3))
+ODD_FIRST = ((1, 2), (3, 0)), ((1, 0), (2, 3))
+
+
+def block_order(first):
+    return [(a[i], b[j]) for a in first for b in first for i in range(2) for j in range(2)]
+
+
+BLOCKS = block_order(EVEN_FIRST[0])
+TURNED = block_order(ODD_FIRST[0])
+
+
+def two_step_gather(w, tilings):
+    for pairs in tilings:
+        groups = [[a * Y + b for a in first for b in second] for first in pairs for second in pairs]
+        w = lax.all_to_all(jnp.broadcast_to(w[None], (4,) + w.shape), XY, 0, 0, axis_index_groups=groups)
+    return w.reshape((X * Y,) + w.shape[2:])
 
 
 def middle_kernel(mine_ref, other_ref, hidden_ref, read_ref, mask_ref, up_ref, out_ref):
     tokens, features = read_ref.shape
     rank = up_ref.shape[0] // 2
-    base = mine_ref[:tokens, :features] + other_ref[:, :features]
-    low = mine_ref[:tokens, features:] + other_ref[:, features:]
+    base = mine_ref[:, :features] + other_ref[:, :features]
+    low = mine_ref[:, features:] + other_ref[:, features:]
     low_b = low.astype(BF16)
     policy = base + ADAPTER_SCALE * jnp.dot(low_b, up_ref[...], preferred_element_type=F32)
     read = read_ref[...].astype(F32)
@@ -219,24 +246,23 @@
     swap_core = [(0, 1), (1, 0)]
 
     weights_far = lax.ppermute(weights, axes, swap_zh)
-    spread = lambda w: lax.all_to_all(jnp.broadcast_to(w[None], (X * Y,) + w.shape), XY, 0, 0)
-    near = spread(weights)
-
-    halves = pl.pallas_call(
+    near = two_step_gather(weights, EVEN_FIRST)
+    mine, for_other = pl.pallas_call(
         order_kernel,
         in_specs=[pl.BlockSpec(memory_space=pltpu.SMEM), vmem()],
-        out_specs=vmem(),
-        out_shape=jax.ShapeDtypeStruct((2, tokens, width // 2), BF16),
+        out_specs=[vmem(), vmem()],
+        out_shape=[jax.ShapeDtypeStruct((tokens, width // 2), BF16)] * 2,
         compiler_params=params(),
         name="order",
     )(jnp.stack([core, zh]).astype(jnp.int32), hidden)
-    mine = halves[0]
-    other = lax.ppermute(halves[1], "core", swap_core)
-
-    far = spread(weights_far)
-    part = forward(mine, other, near, 0)
-    part = forward(mine, other, far, 1, part)
-    from_other = lax.ppermute(part[tokens:], "core", swap_core)
+    other = lax.ppermute(for_other, "core", swap_core)
+    near_mine, near_other = near_forward(mine, other, near)
+
+    first = two_step_gather(weights_far[:, : features // 2], EVEN_FIRST)
+    second = two_step_gather(weights_far[:, features // 2 :], ODD_FIRST)
+    part_other = far_forward(other, first, second, near_other)
+    from_other = lax.ppermute(part_other, "core", swap_core)
+    part_mine = far_forward(mine, first, second, near_mine)
 
     read = readout.reshape(tokens, features)
     mask = response.reshape(tokens, 1).astype(F32)
@@ -249,7 +275,7 @@
         out_shape=jax.ShapeDtypeStruct((X * Y, ZH * rank + EXTRA, wide), BF16),
         compiler_params=params(),
         name="middle",
-    )(part, from_other, hidden, read, mask, up)
+    )(part_mine, from_other, hidden, read, mask, up)
     got = lax.all_to_all(sends, XY, 0, 0)
     along = pl.pallas_call(
         plane_kernel,

time: 172 us -> 211 us (1.23)
  blocking collectives: 27.8 us -> 71.4 us
  Pallas kernels: 20.7 us -> 13.3 us
  local copies, waits for them, and re-layouts: 13.4 us -> 16 us
    all_to_all x0 -> x4, blocking collectives: none -> 42.2 us  [two_step_gather(): lax.all_to_all(jnp.broadcast_to(w[None], (4,) + w.shape), XY, 0, 0, axis_...]
    all_to_all x2, starting transfers between devices: 14.9 us -> 8.14 us  [two_step_gather(): lax.all_to_all(jnp.broadcast_to(w[None], (4,) + w.shape), XY, 0, 0, axis_...]
    unnamed x19 -> x23, local copies, waits for them, and re-layouts: 5.57 us -> 11.4 us
    ppermute x2, waiting for transfers between devices: 5.28 us -> 0.01 us  [the longest x1 0.01 us: shards(): other = lax.ppermute(for_other, 'core', swap_core)]
    all_to_all x1, starting transfers between devices: 16 us -> 20.7 us  [shards(): got = lax.all_to_all(along, ZZ, 0, 0)]
    ppermute x1, waiting for transfers between devices: 0.01 us -> 3.99 us  [shards(): weights_far = lax.ppermute(weights, axes, swap_zh)]
    all_to_all x2, waiting for transfers between devices: 15.6 us -> 18.6 us  [two_step_gather(): lax.all_to_all(jnp.broadcast_to(w[None], (4,) + w.shape), XY, 0, 0, axis_...]
    pallas_call x2 -> x3, Pallas kernels: 10.9 us -> 7.91 us  [the longest x2 4.08 us: far_forward(): pl.pallas_call(far_kernel, grid=(1,), in_specs=[half_of(tokens, half, 1),...]
  transfers between devices with their start and end apart: 7 -> 7, of which waited for: 6 -> 5; matrix products, arithmetic and copies ran while one was open for 2% -> 1% of each run, Pallas kernels for 6% -> 4%
where the time goes in v2:
time: 211 us; the launch traced here: 210 us
  blocking collectives  71.4 us (34%)
  starting transfers between devices  60.8 us (29%)
  waiting for transfers between devices  45 us (21%)
  local copies, waits for them, and re-layouts  16 us (8%)
  Pallas kernels  13.3 us (6%)
  between operations  2.72 us (1%)
    all_to_all x4, blocking collectives, two_step_gather(): lax.all_to_all(jnp.broadcast_to(w[None], (4,) + w.shape), XY, 0, 0, axis_...  42.2 us
    all_to_all x1, blocking collectives, shards(): got = lax.all_to_all(sends, XY, 0, 0)  23 us
    all_to_all x1, starting transfers between devices, shards(): got = lax.all_to_all(along, ZZ, 0, 0)  20.7 us
    all_to_all x2, waiting for transfers between devices, two_step_gather(): lax.all_to_all(jnp.broadcast_to(w[None], (4,) + w.shape), XY, 0, 0, axis_...  18.6 us
    ppermute x1, starting transfers between devices, shards(): weights_far = lax.ppermute(weights, axes, swap_zh)  16.3 us
    all_to_all x1, waiting for transfers between devices, shards(): got = lax.all_to_all(along, ZZ, 0, 0)  13.3 us
    unnamed x23, local copies, waits for them, and re-layouts  11.4 us
    ppermute x1, starting transfers between devices, shards(): other = lax.ppermute(for_other, 'core', swap_core)  9.41 us
  transfers between devices with their start and end apart: 7, of which 5 were waited for; matrix products, arithmetic and copies ran while one was open for 1% of the time, Pallas kernels for 4%

profile of v2, /device:TPU:1, one launch (start us, length us, event | category | flops | bytes accessed | tf_op | source)
XLA Modules:
  0.0 210.3 jit_solution(2008446546148647696)
XLA Ops:
  0.7 0.9 copy-done
  2.3 16.3 %collective-permute-start = (bf16[144,512]{1,0:T(8,128)(2,1)S(1)}, bf16[144,512]{1,0:T(8,128)(2,1)S(1)}, u32[]{:S(2)}, u32[]{:S(2)}) collective-permute-start(bf16[144,512]{1,0:T(8,128)(2,1)S(1)} %pad_maximum_fusion), channel_id=1, source_target_pairs={{0,4},{1,5},{2,6},{3,7},{4,0},{5,1},{6,2},{7,3},{8,12},{9,13},{10,... | collective-permute-start | bytes 442376 | tf_op jit(solution)/shard_map/ppermute | solution.py:248
  18.6 4.0 %collective-permute-done = bf16[144,512]{1,0:T(8,128)(2,1)S(1)} collective-permute-done((bf16[144,512]{1,0:T(8,128)(2,1)S(1)}, bf16[144,512]{1,0:T(8,128)(2,1)S(1)}, u32[]{:S(2)}, u32[]{:S(2)}) %collective-permute-start) | collective-permute-done | bytes 147488 | tf_op jit(solution)/shard_map/ppermute | solution.py:248
  22.7 7.9 %all_to_all.45 = bf16[4,144,256]{2,1,0:T(8,128)(2,1)S(1)} all-to-all(bf16[4,144,256]{2,1,0:T(8,128)(2,1)S(1)} %broadcast_in_dim.14), channel_id=1, replica_groups={{0,1,8,9},{2,3,10,11},{16,17,24,25},{18,19,26,27},{4,5,12,13},{6,7,14,1..., dimensions={0} | all-to-all | bytes 589824 | tf_op jit(solution)/shard_map/all_to_all | solution.py:145
  30.6 8.9 %all_to_all.46 = bf16[4,144,256]{2,1,0:T(8,128)(2,1)S(1)} all-to-all(bf16[4,144,256]{2,1,0:T(8,128)(2,1)S(1)} %broadcast_in_dim.16), channel_id=1, replica_groups={{9,10,17,18},{11,8,19,16},{25,26,1,2},{27,24,3,0},{13,14,21,22},{15,12,..., dimensions={0} | all-to-all | bytes 589824 | tf_op jit(solution)/shard_map/all_to_all | solution.py:145
  39.5 8.9 %all_to_all.47 = bf16[4,144,512]{2,1,0:T(8,128)(2,1)S(1)} all-to-all(bf16[4,144,512]{2,1,0:T(8,128)(2,1)S(1)} %broadcast_in_dim.18), channel_id=1, replica_groups={{0,1,8,9},{2,3,10,11},{16,17,24,25},{18,19,26,27},{4,5,12,13},{6,7,14,1..., dimensions={0} | all-to-all | bytes 1179648 | tf_op jit(solution)/shard_map/all_to_all | solution.py:145
  48.5 16.6 %all_to_all.48 = bf16[4,4,144,256]{3,2,1,0:T(8,128)(2,1)S(1)} all-to-all(bf16[4,4,144,256]{3,2,1,0:T(8,128)(2,1)S(1)} %broadcast_in_dim.15), channel_id=1, replica_groups={{9,10,17,18},{8,11,16,19},{1,2,25,26},{0,3,24,27},{13,14,21,22},{12,15,..., dimensions={0} | all-to-all | bytes 2359296 | tf_op jit(solution)/shard_map/all_to_all | solution.py:145
  65.0 1.7 broadcast_in_dim.19
  66.7 4.5 %all-to-all-start.5 = ((bf16[4,4,144,512]{3,2,1,0:T(8,128)(2,1)}), bf16[4,4,144,512]{3,2,1,0:T(8,128)(2,1)}, u32[]{:S(2)}, u32[]{:S(2)}) async-start(bf16[4,4,144,512]{3,2,1,0:T(8,128)(2,1)} %broadcast_in_dim.19), calls=%async_computation.5 | async-start | bytes 4718592 | tf_op jit(solution)/shard_map/all_to_all | solution.py:145
  71.3 2.2 %copy-done.1 = bf16[1,2,128,8192]{3,2,1,0:T(8,128)(2,1)S(1)} copy-done((bf16[1,2,128,8192]{3,2,1,0:T(8,128)(2,1)S(1)}, bf16[1,2,128,8192]{3,2,1,0:T(8,128)(2,1)}, u32[]{:S(2)}) %copy-start.1) | copy-done | bytes 4194328
  73.5 3.0 %order.1 = (bf16[256,4096]{1,0:T(8,128)(2,1)S(1)}, bf16[256,4096]{1,0:T(8,128)(2,1)}) custom-call(s32[2]{0:T(128)S(1)} %pad_add_fusion.where_ref, bf16[256,8192]{1,0:T(8,128)(2,1)S(1)} %bitcast.21), custom_call_target="tpu_custom_call" | custom-call | tf_op jit(solution)/shard_map/order/pallas_call | solution.py:250
  76.5 1.4 copy-done.3
  77.9 9.4 %collective-permute-start.1 = (bf16[256,4096]{1,0:T(8,128)(2,1)}, bf16[256,4096]{1,0:T(8,128)(2,1)}, u32[]{:S(2)}, u32[]{:S(2)}) collective-permute-start(bf16[256,4096]{1,0:T(8,128)(2,1)} %get-tuple-element.11), channel_id=1, source_target_pairs={{0,32},{32,0},{1,33},{33,1},{2,34},{34,2},{3,35},{35,3},{4,36},{36... | collective-permute-start | bytes 6291464 | tf_op jit(solution)/shard_map/ppermute | solution.py:258
  87.3 11.1 %all-to-all-done.5 = bf16[4,4,144,512]{3,2,1,0:T(8,128)(2,1)} async-done(((bf16[4,4,144,512]{3,2,1,0:T(8,128)(2,1)}), bf16[4,4,144,512]{3,2,1,0:T(8,128)(2,1)}, u32[]{:S(2)}, u32[]{:S(2)}) %all-to-all-start.5) | async-done | bytes 2359328 | tf_op jit(solution)/shard_map/all_to_all | solution.py:145
  98.4 1.1 broadcast_in_dim.17
  99.5 3.6 %all-to-all-start.3 = ((bf16[4,4,144,256]{3,2,1,0:T(8,128)(2,1)}), bf16[4,4,144,256]{3,2,1,0:T(8,128)(2,1)S(1)}, u32[]{:S(2)}, u32[]{:S(2)}) async-start(bf16[4,4,144,256]{3,2,1,0:T(8,128)(2,1)} %broadcast_in_dim.17), calls=%async_computation.3 | async-start | bytes 2359296 | tf_op jit(solution)/shard_map/all_to_all | solution.py:145
  103.1 1.6 copy-done.4
  104.7 3.8 %near.1 = (f32[256,640]{1,0:T(8,128)S(1)}, f32[256,640]{1,0:T(8,128)S(1)}) custom-call(bf16[256,4096]{1,0:T(8,128)(2,1)S(1)} %copy-done.4, bf16[256,4096]{1,0:T(8,128)(2,1)} %collective-permute-done.1.other_ref.hidden_ref, bf16[16,144,512]{2,1,0:T(8,128)(2,1)} %bitcast.8.weight_ref), custom_call_target="tpu_custom_call" | custom-call | tf_op jit(solution)/shard_map/near/pallas_call | solution.py:106
  109.4 7.5 %all-to-all-done.3 = bf16[4,4,144,256]{3,2,1,0:T(8,128)(2,1)S(1)} async-done(((bf16[4,4,144,256]{3,2,1,0:T(8,128)(2,1)}), bf16[4,4,144,256]{3,2,1,0:T(8,128)(2,1)S(1)}, u32[]{:S(2)}, u32[]{:S(2)}) %all-to-all-start.3) | async-done | bytes 1179680 | tf_op jit(solution)/shard_map/all_to_all | solution.py:145
  116.9 3.1 %far.3 = f32[256,640]{1,0:T(8,128)} custom-call(bf16[256,4096]{1,0:T(8,128)(2,1)} %collective-permute-done.1.other_ref.hidden_ref, bf16[16,144,256]{2,1,0:T(8,128)(2,1)S(1)} %bitcast.23, bf16[16,144,256]{2,1,0:T(8,128)(2,1)S(1)} %bitcast.25, f32[256,640]{1,0:T(8,128)S(1)} %get-tuple-element.13.before_ref), custom_call_target="tpu_custom_call" | custom-call | tf_op jit(solution)/shard_map/far/pallas_call | solution.py:119
  120.0 2.9 %collective-permute-start.2 = (f32[256,640]{1,0:T(8,128)}, f32[256,640]{1,0:T(8,128)S(1)}, u32[]{:S(2)}, u32[]{:S(2)}) collective-permute-start(f32[256,640]{1,0:T(8,128)} %far.3), channel_id=1, source_target_pairs={{0,32},{32,0},{1,33},{33,1},{2,34},{34,2},{3,35},{35,3},{4,36},{36... | collective-permute-start | bytes 1966088 | tf_op jit(solution)/shard_map/ppermute | solution.py:264
  123.2 1.6 copy-done.5
  124.7 1.1 copy-done.7
  125.8 1.0 far.2.mine_ref
  126.8 1.2 copy-done.2
  128.0 1.3 middle.1
  129.4 23.0 %all_to_all.49.got_ref = bf16[16,144,256]{2,1,0:T(8,128)(2,1)S(1)} all-to-all(bf16[16,144,256]{2,1,0:T(8,128)(2,1)S(1)} %middle.1), channel_id=1, replica_groups=mesh['zl'=8,'core'=2,'x'=4,'zh'=2,'y'=4] {'x','y'}, dimensions={0} | all-to-all | bytes 2359296 | tf_op jit(solution)/shard_map/all_to_all | solution.py:279
  153.2 20.7 %all-to-all-start.7 = ((bf16[16,16,256]{2,1,0:T(8,128)(2,1)}), bf16[16,16,256]{2,1,0:T(8,128)(2,1)S(1)}, u32[]{:S(2)}, u32[]{:S(2)}) async-start(bf16[16,16,256]{2,1,0:T(8,128)(2,1)} %plane.1), calls=%async_computation.7 | async-start | bytes 262144 | tf_op jit(solution)/shard_map/all_to_all | solution.py:288
  173.9 13.3 %all-to-all-done.7.got_ref = bf16[16,16,256]{2,1,0:T(8,128)(2,1)S(1)} async-done(((bf16[16,16,256]{2,1,0:T(8,128)(2,1)}), bf16[16,16,256]{2,1,0:T(8,128)(2,1)S(1)}, u32[]{:S(2)}, u32[]{:S(2)}) %all-to-all-start.7) | async-done | bytes 131104 | tf_op jit(solution)/shard_map/all_to_all | solution.py:288
  188.6 6.1 %psum.7 = f32[16,256]{1,0:T(8,128)S(1)} all-reduce(f32[16,256]{1,0:T(8,128)S(1)} %get-tuple-element.14), channel_id=1, replica_groups=mesh['zl'=8,'core'=2,'x'=4,'zh'=2,'y'=4] {'core'}, use_global_device_ids=true, to_apply=%region_0.1 | all-reduce | flops 4096 | bytes 32768 | tf_op jit(solution)/shard_map/psum | solution.py:297
  195.4 3.4 %all-to-all-start.8 = ((f32[8,8,256]{2,1,0:T(8,128)}), f32[8,8,256]{2,1,0:T(8,128)S(1)}, u32[]{:S(2)}, u32[]{:S(2)}) async-start(f32[8,8,256]{2,1,0:T(8,128)} %broadcast_in_dim.20), calls=%async_computation.8 | async-start | bytes 131072 | tf_op jit(solution)/shard_map/all_to_all | solution.py:299
  199.4 9.1 %all-to-all-done.8 = f32[8,8,256]{2,1,0:T(8,128)S(1)} async-done(((f32[8,8,256]{2,1,0:T(8,128)}), f32[8,8,256]{2,1,0:T(8,128)S(1)}, u32[]{:S(2)}, u32[]{:S(2)}) %all-to-all-start.8) | async-done | bytes 65568 | tf_op jit(solution)/shard_map/all_to_all | solution.py:299
  (38 shorter events, 5.5 us)
Async XLA Ops:
  0.6 1.0 copy-start
  2.3 20.3 %collective-permute-start = (bf16[144,512]{1,0:T(8,128)(2,1)S(1)}, bf16[144,512]{1,0:T(8,128)(2,1)S(1)}, u32[]{:S(2)}, u32[]{:S(2)}) collective-permute-start(bf16[144,512]{1,0:T(8,128)(2,1)S(1)} %pad_maximum_fusion), channel_id=1, source_target_pairs={{0,4},{1,5},{2,6},{3,7},{4,0},{5,1},{6,2},{7,3},{8,12},{9,13},{10,... | collective-permute-start | bytes 442376 | tf_op jit(solution)/shard_map/ppermute | solution.py:248
  66.7 31.7 %all-to-all-start.5 = ((bf16[4,4,144,512]{3,2,1,0:T(8,128)(2,1)}), bf16[4,4,144,512]{3,2,1,0:T(8,128)(2,1)}, u32[]{:S(2)}, u32[]{:S(2)}) async-start(bf16[4,4,144,512]{3,2,1,0:T(8,128)(2,1)} %broadcast_in_dim.19), calls=%async_computation.5 | async-start | bytes 4718592 | tf_op jit(solution)/shard_map/all_to_all | solution.py:145
  71.3 2.2 %copy-start.1 = (bf16[1,2,128,8192]{3,2,1,0:T(8,128)(2,1)S(1)}, bf16[1,2,128,8192]{3,2,1,0:T(8,128)(2,1)}, u32[]{:S(2)}) copy-start(bf16[1,2,128,8192]{3,2,1,0:T(8,128)(2,1)} %param.6) | copy-start | bytes 12582916
  76.5 1.4 copy-start.3
  77.9 25.3 %collective-permute-start.1 = (bf16[256,4096]{1,0:T(8,128)(2,1)}, bf16[256,4096]{1,0:T(8,128)(2,1)}, u32[]{:S(2)}, u32[]{:S(2)}) collective-permute-start(bf16[256,4096]{1,0:T(8,128)(2,1)} %get-tuple-element.11), channel_id=1, source_target_pairs={{0,32},{32,0},{1,33},{33,1},{2,34},{34,2},{3,35},{35,3},{4,36},{36... | collective-permute-start | bytes 6291464 | tf_op jit(solution)/shard_map/ppermute | solution.py:258
  99.5 17.4 %all-to-all-start.3 = ((bf16[4,4,144,256]{3,2,1,0:T(8,128)(2,1)}), bf16[4,4,144,256]{3,2,1,0:T(8,128)(2,1)S(1)}, u32[]{:S(2)}, u32[]{:S(2)}) async-start(bf16[4,4,144,256]{3,2,1,0:T(8,128)(2,1)} %broadcast_in_dim.17), calls=%async_computation.3 | async-start | bytes 2359296 | tf_op jit(solution)/shard_map/all_to_all | solution.py:145
  103.1 1.6 copy-start.4
  108.6 0.8 copy-start.6
  116.9 6.1 %copy-start.10 = (s32[1,2,128]{2,1,0:T(2,128)S(1)}, s32[1,2,128]{2,1,0:T(2,128)}, u32[]{:S(2)}) copy-start(s32[1,2,128]{2,1,0:T(2,128)} %param.8) | copy-start | bytes 3076
  116.9 6.2 %copy-start.9 = (bf16[64,512]{1,0:T(8,128)(2,1)S(1)}, bf16[64,512]{1,0:T(8,128)(2,1)}, u32[]{:S(2)}) copy-start(bf16[64,512]{1,0:T(8,128)(2,1)} %param.11) | copy-start | bytes 196612
  120.0 6.8 %collective-permute-start.2 = (f32[256,640]{1,0:T(8,128)}, f32[256,640]{1,0:T(8,128)S(1)}, u32[]{:S(2)}, u32[]{:S(2)}) collective-permute-start(f32[256,640]{1,0:T(8,128)} %far.3), channel_id=1, source_target_pairs={{0,32},{32,0},{1,33},{33,1},{2,34},{34,2},{3,35},{35,3},{4,36},{36... | collective-permute-start | bytes 1966088 | tf_op jit(solution)/shard_map/ppermute | solution.py:264
  123.1 1.6 copy-start.5
  124.7 1.1 copy-start.7
  125.8 2.2 %copy-start.2 = (bf16[1,2,128,8192]{3,2,1,0:T(8,128)(2,1)S(1)}, bf16[1,2,128,8192]{3,2,1,0:T(8,128)(2,1)}, u32[]{:S(2)}) copy-start(bf16[1,2,128,8192]{3,2,1,0:T(8,128)(2,1)} %param.6) | copy-start | bytes 12582916
  125.8 2.2 %copy-start.8 = (bf16[1,2,128,512]{3,2,1,0:T(8,128)(2,1)S(1)}, bf16[1,2,128,512]{3,2,1,0:T(8,128)(2,1)}, u32[]{:S(2)}) copy-start(bf16[1,2,128,512]{3,2,1,0:T(8,128)(2,1)} %param.7) | copy-start | bytes 786436
  153.2 34.0 %all-to-all-start.7 = ((bf16[16,16,256]{2,1,0:T(8,128)(2,1)}), bf16[16,16,256]{2,1,0:T(8,128)(2,1)S(1)}, u32[]{:S(2)}, u32[]{:S(2)}) async-start(bf16[16,16,256]{2,1,0:T(8,128)(2,1)} %plane.1), calls=%async_computation.7 | async-start | bytes 262144 | tf_op jit(solution)/shard_map/all_to_all | solution.py:288
  195.4 13.1 %all-to-all-start.8 = ((f32[8,8,256]{2,1,0:T(8,128)}), f32[8,8,256]{2,1,0:T(8,128)S(1)}, u32[]{:S(2)}, u32[]{:S(2)}) async-start(f32[8,8,256]{2,1,0:T(8,128)} %broadcast_in_dim.20), calls=%async_computation.8 | async-start | bytes 131072 | tf_op jit(solution)/shard_map/all_to_all | solution.py:299

commit v3 on v2

--- a/solution.py
+++ b/solution.py
@@ -41,109 +41,75 @@
     for own_core, out_ref in ((core, mine_ref), (1 - core, other_ref)):
         at = 0
         for own_zh in (zh, 1 - zh):
-            for x, y in BLOCKS:
-                start = (((x * ZH + own_zh) * Y + y) * 2 + own_core) * LANES
-                out_ref[:, at * LANES : (at + 1) * LANES] = hidden_ref[
-                    :, pl.ds(pl.multiple_of(start, LANES), LANES)
-                ]
-                at += 1
+            for x in range(X):
+                for y in range(Y):
+                    start = (((x * ZH + own_zh) * Y + y) * 2 + own_core) * LANES
+                    out_ref[:, at * LANES : (at + 1) * LANES] = hidden_ref[
+                        :, pl.ds(pl.multiple_of(start, LANES), LANES)
+                    ]
+                    at += 1
 
 
 def unpacked(weight_ref):
     sources, _, features = weight_ref.shape
     value = weight_ref[:, :LANES, :].reshape(sources * LANES, features)
     down_t = [
-        jnp.concatenate(
-            [weight_ref[s, LANES:, g * LANES : (g + 1) * LANES] for g in range(features // LANES)], axis=0
-        )
-        for s in range(sources)
+        jnp.concatenate([weight_ref[s, LANES:, g * LANES : (g + 1) * LANES] for s in range(sources)], axis=1)
+        for g in range(features // LANES)
     ]
-    return value, down_t
+    return value, jnp.concatenate(down_t, axis=0)
 
 
 def low_part(hidden, down_t):
-    down_t = jnp.concatenate(down_t, axis=1)
     down_t = jnp.concatenate([down_t, jnp.zeros((LANES - down_t.shape[0], down_t.shape[1]), BF16)], axis=0)
     return lax.dot_general(hidden, down_t, (((1,), (1,)), ((), ())), preferred_element_type=F32)
 
 
-def near_kernel(mine_ref, other_ref, weight_ref, out_mine_ref, out_other_ref):
-    features = weight_ref.shape[2]
-    value, down_t = unpacked(weight_ref)
-    for ref, out_ref in ((mine_ref, out_mine_ref), (other_ref, out_other_ref)):
-        hidden = ref[...]
-        out_ref[:, :features] = jnp.dot(hidden, value, preferred_element_type=F32)
-        out_ref[:, features:] = low_part(hidden, down_t)
-
-
-def far_kernel(hidden_ref, first_ref, second_ref, before_ref, out_ref):
+def near_kernel(mine_ref, other_ref, first_ref, second_ref, out_mine_ref, out_other_ref):
     half = first_ref.shape[2]
     first, first_t = unpacked(first_ref)
     second, second_t = unpacked(second_ref)
-    hidden = hidden_ref[...]
-    turned = jnp.concatenate(
-        [hidden[:, BLOCKS.index(p) * LANES : (BLOCKS.index(p) + 1) * LANES] for p in TURNED], axis=1
-    )
-    down_t = [jnp.concatenate([first_t[k], second_t[TURNED.index(p)]], axis=0) for k, p in enumerate(BLOCKS)]
-    out_ref[:, :half] = before_ref[:, :half] + jnp.dot(hidden, first, preferred_element_type=F32)
-    out_ref[:, half : 2 * half] = before_ref[:, half : 2 * half] + jnp.dot(
-        turned, second, preferred_element_type=F32
-    )
-    out_ref[:, 2 * half :] = before_ref[:, 2 * half :] + low_part(hidden, down_t)
-
-
-def half_of(tokens, half, part):
-    return pl.BlockSpec((tokens, half), lambda i: (0, part))
-
-
-def whole(shape):
-    return pl.BlockSpec(shape, lambda i: (0,) * len(shape))
-
-
-def near_forward(mine, other, weights):
-    tokens, half = mine.shape[0], mine.shape[1] // 2
-    out = (tokens, weights.shape[2] + LANES)
+    down_t = jnp.concatenate([first_t, second_t], axis=0)
+    for ref, out_ref in ((mine_ref, out_mine_ref), (other_ref, out_other_ref)):
+        hidden = ref[:, : first.shape[0]]
+        out_ref[:, :half] = jnp.dot(hidden, first, preferred_element_type=F32)
+        out_ref[:, half : 2 * half] = jnp.dot(hidden, second, preferred_element_type=F32)
+        out_ref[:, 2 * half :] = low_part(hidden, down_t)
+
+
+def far_kernel(hidden_ref, weight_ref, before_ref, out_ref):
+    features = weight_ref.shape[2]
+    value, down_t = unpacked(weight_ref)
+    hidden = hidden_ref[:, value.shape[0] :]
+    out_ref[:, :features] = before_ref[:, :features] + jnp.dot(hidden, value, preferred_element_type=F32)
+    out_ref[:, features:] = before_ref[:, features:] + low_part(hidden, down_t)
+
+
+def near_forward(mine, other, first, second):
+    out = (mine.shape[0], 2 * first.shape[2] + LANES)
     return pl.pallas_call(
         near_kernel,
-        grid=(1,),
-        in_specs=[half_of(tokens, half, 0), half_of(tokens, half, 0), whole(weights.shape)],
-        out_specs=[whole(out)] * 2,
+        in_specs=[vmem()] * 4,
+        out_specs=[vmem()] * 2,
         out_shape=[jax.ShapeDtypeStruct(out, F32)] * 2,
         compiler_params=params(),
         name="near",
-    )(mine, other, weights)
-
-
-def far_forward(hidden, first, second, before):
-    tokens, half = hidden.shape[0], hidden.shape[1] // 2
+    )(mine, other, first, second)
+
+
+def far_forward(hidden, weights, before):
     return pl.pallas_call(
         far_kernel,
-        grid=(1,),
-        in_specs=[half_of(tokens, half, 1), whole(first.shape), whole(second.shape), whole(before.shape)],
-        out_specs=whole(before.shape),
+        in_specs=[vmem()] * 3,
+        out_specs=vmem(),
         out_shape=jax.ShapeDtypeStruct(before.shape, F32),
         compiler_params=params(),
         name="far",
-    )(hidden, first, second, before)
-
-
-EVEN_FIRST = ((0, 1), (2, 3)), ((1, 2), (0, 3))
-ODD_FIRST = ((1, 2), (3, 0)), ((1, 0), (2, 3))
-
-
-def block_order(first):
-    return [(a[i], b[j]) for a in first for b in first for i in range(2) for j in range(2)]
-
-
-BLOCKS = block_order(EVEN_FIRST[0])
-TURNED = block_order(ODD_FIRST[0])
-
-
-def two_step_gather(w, tilings):
-    for pairs in tilings:
-        groups = [[a * Y + b for a in first for b in second] for first in pairs for second in pairs]
-        w = lax.all_to_all(jnp.broadcast_to(w[None], (4,) + w.shape), XY, 0, 0, axis_index_groups=groups)
-    return w.reshape((X * Y,) + w.shape[2:])
+    )(hidden, weights, before)
+
+
+def plane_gather(w):
+    return lax.all_to_all(jnp.broadcast_to(w[None], (X * Y,) + w.shape), XY, 0, 0)
 
 
 def middle_kernel(mine_ref, other_ref, hidden_ref, read_ref, mask_ref, up_ref, out_ref):
@@ -238,15 +204,24 @@
     down_half = lax.dynamic_slice_in_dim(adapter_down, core * LANES, LANES, 0)
     packed = down_half.T.reshape(features // LANES, EXTRA, LANES).transpose(1, 0, 2).reshape(EXTRA, features)
     weights = jnp.concatenate([value_half, packed], axis=0)
-    spots = [(a, c, b, e, d) for a in range(ZL) for c in range(2) for b in range(X) for e in range(ZH) for d in range(Y)]
     sizes = (ZL, 2, X, ZH, Y)
     axes = ("zl", "core", "x", "zh", "y")
+    spots = list(np.ndindex(*sizes))
     flat = lambda p: int(np.ravel_multi_index(p, sizes))
-    swap_zh = [(flat(p), flat((p[0], p[1], p[2], 1 - p[3], p[4]))) for p in spots]
+
+    def along_z(step):
+        moved = []
+        for a, c, b, e, d in spots:
+            z = (e * ZL + a + step) % (ZH * ZL)
+            moved.append((flat((a, c, b, e, d)), flat((z % ZL, c, b, z // ZL, d))))
+        return moved
+
     swap_core = [(0, 1), (1, 0)]
-
-    weights_far = lax.ppermute(weights, axes, swap_zh)
-    near = two_step_gather(weights, EVEN_FIRST)
+    odd = zl % 2
+    half = features // 2
+
+    weights_far = lax.ppermute(weights, axes, along_z(ZL))
+    near = plane_gather(lax.dynamic_slice_in_dim(weights, odd * half, half, 1))
     mine, for_other = pl.pallas_call(
         order_kernel,
         in_specs=[pl.BlockSpec(memory_space=pltpu.SMEM), vmem()],
@@ -256,13 +231,16 @@
         name="order",
     )(jnp.stack([core, zh]).astype(jnp.int32), hidden)
     other = lax.ppermute(for_other, "core", swap_core)
-    near_mine, near_other = near_forward(mine, other, near)
-
-    first = two_step_gather(weights_far[:, : features // 2], EVEN_FIRST)
-    second = two_step_gather(weights_far[:, features // 2 :], ODD_FIRST)
-    part_other = far_forward(other, first, second, near_other)
+
+    weights_far, near = lax.optimization_barrier((weights_far, near))
+    far = plane_gather(weights_far)
+    near_too = lax.ppermute(near, "zl", [(a, a ^ 1) for a in range(ZL)])
+    near_mine, near_other = near_forward(
+        mine, other, jnp.where(odd == 0, near, near_too), jnp.where(odd == 0, near_too, near)
+    )
+    part_other = far_forward(other, far, near_other)
     from_other = lax.ppermute(part_other, "core", swap_core)
-    part_mine = far_forward(mine, first, second, near_mine)
+    part_mine = far_forward(mine, far, near_mine)
 
     read = readout.reshape(tokens, features)
     mask = response.reshape(tokens, 1).astype(F32)

time: 211 us -> 180 us (0.85)
  blocking collectives: 71.4 us -> 30.9 us
  waiting for transfers between devices: 45 us -> 52.3 us
    all_to_all x4 -> x0, blocking collectives: 42.2 us -> none  [two_step_gather(): lax.all_to_all(jnp.broadcast_to(w[None], (4,) + w.shape), XY, 0, 0, axis_...]
    ppermute x1 -> x2, waiting for transfers between devices: 3.99 us -> 29.9 us  [the longest x1 26.6 us: shards(): near_too = lax.ppermute(near, 'zl', [(a, a ^ 1) for a in range(ZL)])]
    all_to_all x2, waiting for transfers between devices: 18.6 us -> 0.01 us  [plane_gather(): lax.all_to_all(jnp.broadcast_to(w[None], (X * Y,) + w.shape), XY, 0, 0)]
    ppermute x1 -> x2, starting transfers between devices: 16.3 us -> 26.9 us  [the longest x1 15.4 us: shards(): weights_far = lax.ppermute(weights, axes, along_z(ZL))]
    all_to_all x1, starting transfers between devices: 20.7 us -> 11.7 us  [shards(): got = lax.all_to_all(along, ZZ, 0, 0)]
    all_to_all x2, starting transfers between devices: 8.14 us -> 13.9 us  [plane_gather(): lax.all_to_all(jnp.broadcast_to(w[None], (X * Y,) + w.shape), XY, 0, 0)]
    ppermute x1, starting transfers between devices: 9.41 us -> 4.34 us  [shards(): other = lax.ppermute(for_other, 'core', swap_core)]
  transfers between devices with their start and end apart: 7 -> 8, of which waited for: 5 -> 4; matrix products, arithmetic and copies ran while one was open for 1% -> 2% of each run, Pallas kernels for 4% -> 4%
where the time goes in v3:
time: 180 us; the launch traced here: 179 us
  starting transfers between devices  62.7 us (35%)
  waiting for transfers between devices  52.3 us (29%)
  blocking collectives  30.9 us (17%)
  local copies, waits for them, and re-layouts  14.5 us (8%)
  Pallas kernels  13.2 us (7%)
  other arithmetic  3.15 us (2%)
  between operations  2.73 us (2%)
    ppermute x1, waiting for transfers between devices, shards(): near_too = lax.ppermute(near, 'zl', [(a, a ^ 1) for a in range(ZL)])  26.6 us
    all_to_all x1, blocking collectives, shards(): got = lax.all_to_all(sends, XY, 0, 0)  24.7 us
    ppermute x1, starting transfers between devices, shards(): weights_far = lax.ppermute(weights, axes, along_z(ZL))  15.4 us
    all_to_all x2, starting transfers between devices, plane_gather(): lax.all_to_all(jnp.broadcast_to(w[None], (X * Y,) + w.shape), XY, 0, 0)  13.9 us
    all_to_all x1, waiting for transfers between devices, shards(): got = lax.all_to_all(along, ZZ, 0, 0)  13.3 us
    all_to_all x1, starting transfers between devices, shards(): got = lax.all_to_all(along, ZZ, 0, 0)  11.7 us
    ppermute x1, starting transfers between devices, shards(): near_too = lax.ppermute(near, 'zl', [(a, a ^ 1) for a in range(ZL)])  11.5 us
    unnamed x23, local copies, waits for them, and re-layouts  10.2 us
  transfers between devices with their start and end apart: 8, of which 4 were waited for; matrix products, arithmetic and copies ran while one was open for 2% of the time, Pallas kernels for 4%

profile of v3, /device:TPU:1, one launch (start us, length us, event | category | flops | bytes accessed | tf_op | source)
XLA Modules:
  0.0 179.5 jit_solution(11966232337950470454)
XLA Ops:
  0.7 0.9 copy-done
  1.6 0.7 constant_dynamic-slice_fusion.1
  2.3 1.1 broadcast_in_dim.6
  3.5 7.6 %all-to-all-start = ((bf16[16,144,256]{2,1,0:T(8,128)(2,1)}), bf16[16,144,256]{2,1,0:T(8,128)(2,1)}, u32[]{:S(2)}, u32[]{:S(2)}) async-start(bf16[16,144,256]{2,1,0:T(8,128)(2,1)} %broadcast_in_dim.6), calls=%async_computation | async-start | bytes 2359296 | tf_op jit(solution)/shard_map/all_to_all | solution.py:112
  11.1 15.4 %collective-permute-start = (bf16[144,512]{1,0:T(8,128)(2,1)S(1)}, bf16[144,512]{1,0:T(8,128)(2,1)S(1)}, u32[]{:S(2)}, u32[]{:S(2)}) collective-permute-start(bf16[144,512]{1,0:T(8,128)(2,1)S(1)} %pad_maximum_fusion), channel_id=1, source_target_pairs={{0,4},{1,5},{2,6},{3,7},{4,0},{5,1},{6,2},{7,3},{8,12},{9,13},{10,... | collective-permute-start | bytes 442376 | tf_op jit(solution)/shard_map/ppermute | solution.py:223
  26.6 3.2 %collective-permute-done = bf16[144,512]{1,0:T(8,128)(2,1)S(1)} collective-permute-done((bf16[144,512]{1,0:T(8,128)(2,1)S(1)}, bf16[144,512]{1,0:T(8,128)(2,1)S(1)}, u32[]{:S(2)}, u32[]{:S(2)}) %collective-permute-start) | collective-permute-done | bytes 147488 | tf_op jit(solution)/shard_map/ppermute | solution.py:223
  29.8 1.7 broadcast_in_dim.7
  31.5 6.3 %all-to-all-start.1 = ((bf16[16,144,512]{2,1,0:T(8,128)(2,1)}), bf16[16,144,512]{2,1,0:T(8,128)(2,1)S(1)}, u32[]{:S(2)}, u32[]{:S(2)}) async-start(bf16[16,144,512]{2,1,0:T(8,128)(2,1)} %broadcast_in_dim.7), calls=%async_computation.1 | async-start | bytes 4718592 | tf_op jit(solution)/shard_map/all_to_all | solution.py:112
  37.9 2.2 %copy-done.1 = bf16[1,2,128,8192]{3,2,1,0:T(8,128)(2,1)S(1)} copy-done((bf16[1,2,128,8192]{3,2,1,0:T(8,128)(2,1)S(1)}, bf16[1,2,128,8192]{3,2,1,0:T(8,128)(2,1)}, u32[]{:S(2)}) %copy-start.1) | copy-done | bytes 4194328
  40.0 3.1 %order.1 = (bf16[256,4096]{1,0:T(8,128)(2,1)S(1)}, bf16[256,4096]{1,0:T(8,128)(2,1)}) custom-call(s32[2]{0:T(128)S(1)} %pad_add_fusion.where_ref, bf16[256,8192]{1,0:T(8,128)(2,1)S(1)} %bitcast.18), custom_call_target="tpu_custom_call" | custom-call | tf_op jit(solution)/shard_map/order/pallas_call | solution.py:225
  43.1 1.3 copy-done.3
  44.5 4.3 %collective-permute-start.1 = (bf16[256,4096]{1,0:T(8,128)(2,1)}, bf16[256,4096]{1,0:T(8,128)(2,1)}, u32[]{:S(2)}, u32[]{:S(2)}) collective-permute-start(bf16[256,4096]{1,0:T(8,128)(2,1)} %get-tuple-element.14), channel_id=1, source_target_pairs={{0,32},{32,0},{1,33},{33,1},{2,34},{34,2},{3,35},{35,3},{4,36},{36... | collective-permute-start | bytes 6291464 | tf_op jit(solution)/shard_map/ppermute | solution.py:233
  48.8 11.5 %collective-permute-start.2 = (bf16[16,144,256]{2,1,0:T(8,128)(2,1)}, bf16[16,144,256]{2,1,0:T(8,128)(2,1)}, u32[]{:S(2)}, u32[]{:S(2)}) collective-permute-start(bf16[16,144,256]{2,1,0:T(8,128)(2,1)} %all-to-all-done), channel_id=1, source_target_pairs={{0,64},{64,0},{128,192},{192,128},{256,320},{320,256},{384,448},{4... | collective-permute-start | bytes 3538952 | tf_op jit(solution)/shard_map/ppermute | solution.py:237
  60.3 26.6 %collective-permute-done.2 = bf16[16,144,256]{2,1,0:T(8,128)(2,1)} collective-permute-done((bf16[16,144,256]{2,1,0:T(8,128)(2,1)}, bf16[16,144,256]{2,1,0:T(8,128)(2,1)}, u32[]{:S(2)}, u32[]{:S(2)}) %collective-permute-start.2) | collective-permute-done | bytes 1179680 | tf_op jit(solution)/shard_map/ppermute | solution.py:237
  86.9 1.9 %broadcast_select_fusion = (bf16[16,144,256]{2,1,0:T(8,128)(2,1)S(1)}, bf16[16,144,256]{2,1,0:T(8,128)(2,1)S(1)}) fusion(bf16[16,144,256]{2,1,0:T(8,128)(2,1)} %collective-permute-done.2, bf16[16,144,256]{2,1,0:T(8,128)(2,1)} %all-to-all-done, pred[]{:T(512)S(6)} %eq.6), kind=kLoop, calls=%fused_computation | loop fusion | flops 1179648 | bytes 4718593 | tf_op jit(solution)/shard_map/jit(_where)/select_n | solution.py:239
  89.2 3.4 %near.1 = (f32[256,640]{1,0:T(8,128)S(1)}, f32[256,640]{1,0:T(8,128)S(1)}) custom-call(bf16[256,4096]{1,0:T(8,128)(2,1)S(1)} %copy-done.4, bf16[256,4096]{1,0:T(8,128)(2,1)} %collective-permute-done.1.other_ref.hidden_ref, bf16[16,144,256]{2,1,0:T(8,128)(2,1)S(1)} %get-tuple-element.21.first_ref, bf16[16,144,256]{2,1,0:T(8,128)(2,1)S(1)} %get-tuple-element.20.second_ref), custom_call_target="tpu_custom_call" | custom-call | tf_op jit(solution)/shard_map/near/pallas_call | solution.py:90
  92.6 0.8 copy-done.6
  93.4 3.5 %far.3 = f32[256,640]{1,0:T(8,128)} custom-call(bf16[256,4096]{1,0:T(8,128)(2,1)} %collective-permute-done.1.other_ref.hidden_ref, bf16[16,144,512]{2,1,0:T(8,128)(2,1)S(1)} %all-to-all-done.1.weight_ref, f32[256,640]{1,0:T(8,128)S(1)} %get-tuple-element.17.before_ref), custom_call_target="tpu_custom_call" | custom-call | tf_op jit(solution)/shard_map/far/pallas_call | solution.py:101
  96.9 2.5 %collective-permute-start.3 = (f32[256,640]{1,0:T(8,128)}, f32[256,640]{1,0:T(8,128)S(1)}, u32[]{:S(2)}, u32[]{:S(2)}) collective-permute-start(f32[256,640]{1,0:T(8,128)} %far.3), channel_id=1, source_target_pairs={{0,32},{32,0},{1,33},{33,1},{2,34},{34,2},{3,35},{35,3},{4,36},{36... | collective-permute-start | bytes 1966088 | tf_op jit(solution)/shard_map/ppermute | solution.py:242
  99.6 1.6 copy-done.5
  101.2 1.1 copy-done.7
  102.3 1.0 far.2.mine_ref
  103.2 1.2 copy-done.2
  104.5 1.3 middle.1
  105.8 24.7 %all_to_all.25.got_ref = bf16[16,144,256]{2,1,0:T(8,128)(2,1)S(1)} all-to-all(bf16[16,144,256]{2,1,0:T(8,128)(2,1)S(1)} %middle.1), channel_id=1, replica_groups=mesh['zl'=8,'core'=2,'x'=4,'zh'=2,'y'=4] {'x','y'}, dimensions={0} | all-to-all | bytes 2359296 | tf_op jit(solution)/shard_map/all_to_all | solution.py:257
  130.5 0.9 plane.1
  131.4 11.7 %all-to-all-start.3 = ((bf16[16,16,256]{2,1,0:T(8,128)(2,1)}), bf16[16,16,256]{2,1,0:T(8,128)(2,1)S(1)}, u32[]{:S(2)}, u32[]{:S(2)}) async-start(bf16[16,16,256]{2,1,0:T(8,128)(2,1)} %plane.1), calls=%async_computation.3 | async-start | bytes 262144 | tf_op jit(solution)/shard_map/all_to_all | solution.py:266
  143.1 13.3 %all-to-all-done.3.got_ref = bf16[16,16,256]{2,1,0:T(8,128)(2,1)S(1)} async-done(((bf16[16,16,256]{2,1,0:T(8,128)(2,1)}), bf16[16,16,256]{2,1,0:T(8,128)(2,1)S(1)}, u32[]{:S(2)}, u32[]{:S(2)}) %all-to-all-start.3) | async-done | bytes 131104 | tf_op jit(solution)/shard_map/all_to_all | solution.py:266
  157.8 6.1 %psum.7 = f32[16,256]{1,0:T(8,128)S(1)} all-reduce(f32[16,256]{1,0:T(8,128)S(1)} %get-tuple-element.18), channel_id=1, replica_groups=mesh['zl'=8,'core'=2,'x'=4,'zh'=2,'y'=4] {'core'}, use_global_device_ids=true, to_apply=%region_0.1 | all-reduce | flops 4096 | bytes 32768 | tf_op jit(solution)/shard_map/psum | solution.py:275
  163.9 0.6 broadcast_in_dim.8
  164.6 3.4 %all-to-all-start.4 = ((f32[8,8,256]{2,1,0:T(8,128)}), f32[8,8,256]{2,1,0:T(8,128)S(1)}, u32[]{:S(2)}, u32[]{:S(2)}) async-start(f32[8,8,256]{2,1,0:T(8,128)} %broadcast_in_dim.8), calls=%async_computation.4 | async-start | bytes 131072 | tf_op jit(solution)/shard_map/all_to_all | solution.py:277
  168.6 9.1 %all-to-all-done.4 = f32[8,8,256]{2,1,0:T(8,128)S(1)} async-done(((f32[8,8,256]{2,1,0:T(8,128)}), f32[8,8,256]{2,1,0:T(8,128)S(1)}, u32[]{:S(2)}, u32[]{:S(2)}) %all-to-all-start.4) | async-done | bytes 65568 | tf_op jit(solution)/shard_map/all_to_all | solution.py:277
  (33 shorter events, 2.6 us)
Async XLA Ops:
  0.6 1.0 copy-start
  3.5 26.4 %all-to-all-start = ((bf16[16,144,256]{2,1,0:T(8,128)(2,1)}), bf16[16,144,256]{2,1,0:T(8,128)(2,1)}, u32[]{:S(2)}, u32[]{:S(2)}) async-start(bf16[16,144,256]{2,1,0:T(8,128)(2,1)} %broadcast_in_dim.6), calls=%async_computation | async-start | bytes 2359296 | tf_op jit(solution)/shard_map/all_to_all | solution.py:112
  11.1 18.7 %collective-permute-start = (bf16[144,512]{1,0:T(8,128)(2,1)S(1)}, bf16[144,512]{1,0:T(8,128)(2,1)S(1)}, u32[]{:S(2)}, u32[]{:S(2)}) collective-permute-start(bf16[144,512]{1,0:T(8,128)(2,1)S(1)} %pad_maximum_fusion), channel_id=1, source_target_pairs={{0,4},{1,5},{2,6},{3,7},{4,0},{5,1},{6,2},{7,3},{8,12},{9,13},{10,... | collective-permute-start | bytes 442376 | tf_op jit(solution)/shard_map/ppermute | solution.py:223
  31.5 61.9 %all-to-all-start.1 = ((bf16[16,144,512]{2,1,0:T(8,128)(2,1)}), bf16[16,144,512]{2,1,0:T(8,128)(2,1)S(1)}, u32[]{:S(2)}, u32[]{:S(2)}) async-start(bf16[16,144,512]{2,1,0:T(8,128)(2,1)} %broadcast_in_dim.7), calls=%async_computation.1 | async-start | bytes 4718592 | tf_op jit(solution)/shard_map/all_to_all | solution.py:112
  37.9 2.2 %copy-start.1 = (bf16[1,2,128,8192]{3,2,1,0:T(8,128)(2,1)S(1)}, bf16[1,2,128,8192]{3,2,1,0:T(8,128)(2,1)}, u32[]{:S(2)}) copy-start(bf16[1,2,128,8192]{3,2,1,0:T(8,128)(2,1)} %param.6) | copy-start | bytes 12582916
  43.1 1.3 copy-start.3
  44.5 44.4 %collective-permute-start.1 = (bf16[256,4096]{1,0:T(8,128)(2,1)}, bf16[256,4096]{1,0:T(8,128)(2,1)}, u32[]{:S(2)}, u32[]{:S(2)}) collective-permute-start(bf16[256,4096]{1,0:T(8,128)(2,1)} %get-tuple-element.14), channel_id=1, source_target_pairs={{0,32},{32,0},{1,33},{33,1},{2,34},{34,2},{3,35},{35,3},{4,36},{36... | collective-permute-start | bytes 6291464 | tf_op jit(solution)/shard_map/ppermute | solution.py:233
  48.8 38.1 %collective-permute-start.2 = (bf16[16,144,256]{2,1,0:T(8,128)(2,1)}, bf16[16,144,256]{2,1,0:T(8,128)(2,1)}, u32[]{:S(2)}, u32[]{:S(2)}) collective-permute-start(bf16[16,144,256]{2,1,0:T(8,128)(2,1)} %all-to-all-done), channel_id=1, source_target_pairs={{0,64},{64,0},{128,192},{192,128},{256,320},{320,256},{384,448},{4... | collective-permute-start | bytes 3538952 | tf_op jit(solution)/shard_map/ppermute | solution.py:237
  86.9 2.3 %copy-start.4 = (bf16[256,4096]{1,0:T(8,128)(2,1)S(1)}, bf16[256,4096]{1,0:T(8,128)(2,1)}, u32[]{:S(2)}) copy-start(bf16[256,4096]{1,0:T(8,128)(2,1)} %copy-done.3) | copy-start | bytes 6291460
  92.6 0.8 copy-start.6
  93.4 6.0 %copy-start.10 = (s32[1,2,128]{2,1,0:T(2,128)S(1)}, s32[1,2,128]{2,1,0:T(2,128)}, u32[]{:S(2)}) copy-start(s32[1,2,128]{2,1,0:T(2,128)} %param.8) | copy-start | bytes 3076
  93.4 6.1 %copy-start.9 = (bf16[64,512]{1,0:T(8,128)(2,1)S(1)}, bf16[64,512]{1,0:T(8,128)(2,1)}, u32[]{:S(2)}) copy-start(bf16[64,512]{1,0:T(8,128)(2,1)} %param.11) | copy-start | bytes 196612
  96.9 6.4 %collective-permute-start.3 = (f32[256,640]{1,0:T(8,128)}, f32[256,640]{1,0:T(8,128)S(1)}, u32[]{:S(2)}, u32[]{:S(2)}) collective-permute-start(f32[256,640]{1,0:T(8,128)} %far.3), channel_id=1, source_target_pairs={{0,32},{32,0},{1,33},{33,1},{2,34},{34,2},{3,35},{35,3},{4,36},{36... | collective-permute-start | bytes 1966088 | tf_op jit(solution)/shard_map/ppermute | solution.py:242
  99.6 1.6 copy-start.5
  101.2 1.1 copy-start.7
  102.3 2.2 %copy-start.2 = (bf16[1,2,128,8192]{3,2,1,0:T(8,128)(2,1)S(1)}, bf16[1,2,128,8192]{3,2,1,0:T(8,128)(2,1)}, u32[]{:S(2)}) copy-start(bf16[1,2,128,8192]{3,2,1,0:T(8,128)(2,1)} %param.6) | copy-start | bytes 12582916
  102.3 2.2 %copy-start.8 = (bf16[1,2,128,512]{3,2,1,0:T(8,128)(2,1)S(1)}, bf16[1,2,128,512]{3,2,1,0:T(8,128)(2,1)}, u32[]{:S(2)}) copy-start(bf16[1,2,128,512]{3,2,1,0:T(8,128)(2,1)} %param.7) | copy-start | bytes 786436
  131.4 25.0 %all-to-all-start.3 = ((bf16[16,16,256]{2,1,0:T(8,128)(2,1)}), bf16[16,16,256]{2,1,0:T(8,128)(2,1)S(1)}, u32[]{:S(2)}, u32[]{:S(2)}) async-start(bf16[16,16,256]{2,1,0:T(8,128)(2,1)} %plane.1), calls=%async_computation.3 | async-start | bytes 262144 | tf_op jit(solution)/shard_map/all_to_all | solution.py:266
  164.6 13.1 %all-to-all-start.4 = ((f32[8,8,256]{2,1,0:T(8,128)}), f32[8,8,256]{2,1,0:T(8,128)S(1)}, u32[]{:S(2)}, u32[]{:S(2)}) async-start(f32[8,8,256]{2,1,0:T(8,128)} %broadcast_in_dim.8), calls=%async_computation.4 | async-start | bytes 131072 | tf_op jit(solution)/shard_map/all_to_all | solution.py:277

commit v4 on v3

--- a/solution.py
+++ b/solution.py
@@ -22,7 +22,7 @@
 
 
 def params():
-    return pltpu.CompilerParams(vmem_limit_bytes=28 * 1024 * 1024)
+    return pltpu.CompilerParams(vmem_limit_bytes=50 * 1024 * 1024)
 
 
 def pieces(total, shape):
@@ -36,18 +36,26 @@
     return jnp.where(lane == 0, high, jnp.where(lane == 1, middle, jnp.where(lane == 2, low, zero)))
 
 
-def order_kernel(where_ref, hidden_ref, mine_ref, other_ref):
-    core, zh = where_ref[0], where_ref[1]
-    for own_core, out_ref in ((core, mine_ref), (1 - core, other_ref)):
-        at = 0
-        for own_zh in (zh, 1 - zh):
-            for x in range(X):
-                for y in range(Y):
-                    start = (((x * ZH + own_zh) * Y + y) * 2 + own_core) * LANES
-                    out_ref[:, at * LANES : (at + 1) * LANES] = hidden_ref[
-                        :, pl.ds(pl.multiple_of(start, LANES), LANES)
-                    ]
-                    at += 1
+def anywhere():
+    return pl.BlockSpec(memory_space=pl.ANY)
+
+
+def fetches(where_ref, hidden_ref, buffer, sems, far):
+    core = where_ref[0]
+    zh = 1 - where_ref[1] if far else where_ref[1]
+    copies = []
+    for x in range(X):
+        for y in range(Y):
+            at = x * Y + y
+            start = (((x * ZH + zh) * Y + y) * 2 + core) * LANES
+            copies.append(
+                pltpu.make_async_copy(
+                    hidden_ref.at[:, pl.ds(pl.multiple_of(start, LANES), LANES)],
+                    buffer.at[:, at * LANES : (at + 1) * LANES],
+                    sems.at[at],
+                )
+            )
+    return copies
 
 
 def unpacked(weight_ref):
@@ -65,54 +73,87 @@
     return lax.dot_general(hidden, down_t, (((1,), (1,)), ((), ())), preferred_element_type=F32)
 
 
-def near_kernel(mine_ref, other_ref, first_ref, second_ref, out_mine_ref, out_other_ref):
-    half = first_ref.shape[2]
-    first, first_t = unpacked(first_ref)
-    second, second_t = unpacked(second_ref)
-    down_t = jnp.concatenate([first_t, second_t], axis=0)
-    for ref, out_ref in ((mine_ref, out_mine_ref), (other_ref, out_other_ref)):
-        hidden = ref[:, : first.shape[0]]
-        out_ref[:, :half] = jnp.dot(hidden, first, preferred_element_type=F32)
-        out_ref[:, half : 2 * half] = jnp.dot(hidden, second, preferred_element_type=F32)
-        out_ref[:, 2 * half :] = low_part(hidden, down_t)
-
-
-def far_kernel(hidden_ref, weight_ref, before_ref, out_ref):
+def near_kernel(
+    where_ref, mine_ref, other_ref, own_ref, passed_ref, out_mine_ref, out_other_ref, mine, other, mine_sems, other_sems
+):
+    copies = fetches(where_ref, mine_ref, mine, mine_sems, False)
+    copies += fetches(where_ref, other_ref, other, other_sems, False)
+    for copy in copies:
+        copy.start()
+    for copy in copies:
+        copy.wait()
+
+    def body(first_ref, second_ref):
+        half = first_ref.shape[2]
+        first, first_t = unpacked(first_ref)
+        second, second_t = unpacked(second_ref)
+        down_t = jnp.concatenate([first_t, second_t], axis=0)
+        for ref, out_ref in ((mine, out_mine_ref), (other, out_other_ref)):
+            hidden = ref[...]
+            out_ref[:, :half] = jnp.dot(hidden, first, preferred_element_type=F32)
+            out_ref[:, half : 2 * half] = jnp.dot(hidden, second, preferred_element_type=F32)
+            out_ref[:, 2 * half :] = low_part(hidden, down_t)
+
+    @pl.when(where_ref[2] == 0)
+    def _():
+        body(own_ref, passed_ref)
+
+    @pl.when(where_ref[2] != 0)
+    def _():
+        body(passed_ref, own_ref)
+
+
+def far_kernel(where_ref, hidden_ref, weight_ref, before_ref, out_ref, buffer, sems):
+    copies = fetches(where_ref, hidden_ref, buffer, sems, True)
+    for copy in copies:
+        copy.start()
     features = weight_ref.shape[2]
     value, down_t = unpacked(weight_ref)
-    hidden = hidden_ref[:, value.shape[0] :]
+    for copy in copies:
+        copy.wait()
+    hidden = buffer[...]
     out_ref[:, :features] = before_ref[:, :features] + jnp.dot(hidden, value, preferred_element_type=F32)
     out_ref[:, features:] = before_ref[:, features:] + low_part(hidden, down_t)
 
 
-def near_forward(mine, other, first, second):
-    out = (mine.shape[0], 2 * first.shape[2] + LANES)
+def smem():
+    return pl.BlockSpec(memory_space=pltpu.SMEM)
+
+
+def near_forward(where, mine, other, own, passed):
+    tokens, width = mine.shape
+    out = (tokens, 2 * own.shape[2] + LANES)
     return pl.pallas_call(
         near_kernel,
-        in_specs=[vmem()] * 4,
+        in_specs=[smem(), anywhere(), anywhere(), vmem(), vmem()],
         out_specs=[vmem()] * 2,
         out_shape=[jax.ShapeDtypeStruct(out, F32)] * 2,
+        scratch_shapes=[pltpu.VMEM((tokens, width // 4), BF16)] * 2 + [pltpu.SemaphoreType.DMA((X * Y,))] * 2,
         compiler_params=params(),
         name="near",
-    )(mine, other, first, second)
-
-
-def far_forward(hidden, weights, before):
+    )(where, mine, other, own, passed)
+
+
+def far_forward(where, hidden, weights, before):
+    tokens, width = hidden.shape
     return pl.pallas_call(
         far_kernel,
-        in_specs=[vmem()] * 3,
+        in_specs=[smem(), anywhere(), vmem(), vmem()],
         out_specs=vmem(),
         out_shape=jax.ShapeDtypeStruct(before.shape, F32),
+        scratch_shapes=[pltpu.VMEM((tokens, width // 4), BF16), pltpu.SemaphoreType.DMA((X * Y,))],
         compiler_params=params(),
         name="far",
-    )(hidden, weights, before)
+    )(where, hidden, weights, before)
 
 
 def plane_gather(w):
     return lax.all_to_all(jnp.broadcast_to(w[None], (X * Y,) + w.shape), XY, 0, 0)
 
 
-def middle_kernel(mine_ref, other_ref, hidden_ref, read_ref, mask_ref, up_ref, out_ref):
+def middle_kernel(mine_ref, other_ref, held_ref, read_ref, mask_ref, up_ref, out_ref, hidden_ref, sem):
+    copy = pltpu.make_async_copy(held_ref, hidden_ref, sem)
+    copy.start()
     tokens, features = read_ref.shape
     rank = up_ref.shape[0] // 2
     base = mine_ref[:, :features] + other_ref[:, :features]
@@ -139,6 +180,7 @@
     part = features // (X * ZH * Y)
     lane = lax.broadcasted_iota(jnp.int32, (EXTRA, LANES), 1)
     sent = pieces(total, (EXTRA, LANES)).astype(BF16)
+    copy.wait()
     for x in range(X):
         for y in range(Y):
             to = x * Y + y
@@ -222,25 +264,16 @@
 
     weights_far = lax.ppermute(weights, axes, along_z(ZL))
     near = plane_gather(lax.dynamic_slice_in_dim(weights, odd * half, half, 1))
-    mine, for_other = pl.pallas_call(
-        order_kernel,
-        in_specs=[pl.BlockSpec(memory_space=pltpu.SMEM), vmem()],
-        out_specs=[vmem(), vmem()],
-        out_shape=[jax.ShapeDtypeStruct((tokens, width // 2), BF16)] * 2,
-        compiler_params=params(),
-        name="order",
-    )(jnp.stack([core, zh]).astype(jnp.int32), hidden)
-    other = lax.ppermute(for_other, "core", swap_core)
+    where = jnp.stack([core, zh, odd]).astype(jnp.int32)
+    other = lax.ppermute(hidden, "core", swap_core)
 
     weights_far, near = lax.optimization_barrier((weights_far, near))
     far = plane_gather(weights_far)
-    near_too = lax.ppermute(near, "zl", [(a, a ^ 1) for a in range(ZL)])
-    near_mine, near_other = near_forward(
-        mine, other, jnp.where(odd == 0, near, near_too), jnp.where(odd == 0, near_too, near)
-    )
-    part_other = far_forward(other, far, near_other)
+    passed = lax.ppermute(near, "zl", [(a, a ^ 1) for a in range(ZL)])
+    near_mine, near_other = near_forward(where, hidden, other, near, passed)
+    part_other = far_forward(where, other, far, near_other)
     from_other = lax.ppermute(part_other, "core", swap_core)
-    part_mine = far_forward(mine, far, near_mine)
+    part_mine = far_forward(where, hidden, far, near_mine)
 
     read = readout.reshape(tokens, features)
     mask = response.reshape(tokens, 1).astype(F32)
@@ -248,9 +281,10 @@
     wide = width // (X * ZH * Y)
     sends = pl.pallas_call(
         middle_kernel,
-        in_specs=[vmem()] * 6,
+        in_specs=[vmem(), vmem(), anywhere(), vmem(), vmem(), vmem()],
         out_specs=vmem(),
         out_shape=jax.ShapeDtypeStruct((X * Y, ZH * rank + EXTRA, wide), BF16),
+        scratch_shapes=[pltpu.VMEM((tokens, width), BF16), pltpu.SemaphoreType.DMA],
         compiler_params=params(),
         name="middle",
     )(part_mine, from_other, hidden, read, mask, up)
@@ -272,7 +306,7 @@
         compiler_params=params(),
         name="gate",
     )(got)
-    summed = lax.psum(gated, "core")
+    summed, diffs = lax.optimization_barrier((lax.psum(gated, "core"), diffs))
     rows = rank // ZL
     all_rows = lax.all_to_all(jnp.broadcast_to(summed[None, :rows], (ZL, rows, wide)), "zl", 0, 0)
     down_gradient = all_rows.reshape(rank, wide).T

time: 180 us -> 174 us (0.967)
  local copies, waits for them, and re-layouts: 14.5 us -> 8.38 us
  Pallas kernels: 13.2 us -> 16.2 us
  starting transfers between devices: 62.7 us -> 60.5 us
  other arithmetic: 3.15 us -> 1.23 us
    all_to_all x2, starting transfers between devices: 13.9 us -> 7.53 us  [plane_gather(): lax.all_to_all(jnp.broadcast_to(w[None], (X * Y,) + w.shape), XY, 0, 0)]
    unnamed x23 -> x17, local copies, waits for them, and re-layouts: 10.2 us -> 3.84 us
    ppermute x2, starting transfers between devices: 15.8 us -> 20.7 us  [the longest x1 11.7 us: shards(): passed = lax.ppermute(near, 'zl', [(a, a ^ 1) for a in range(ZL)])]
    pallas_call x5 -> x4, Pallas kernels: 12.2 us -> 15.3 us  [the longest x2 6.75 us: far_forward(): pl.pallas_call(far_kernel, in_specs=[smem(), anywhere(), vmem(), vmem()],...]
    all_to_all x2, waiting for transfers between devices: 0.01 us -> 2.51 us  [plane_gather(): lax.all_to_all(jnp.broadcast_to(w[None], (X * Y,) + w.shape), XY, 0, 0)]
    ppermute x1, starting transfers between devices: 15.4 us -> 13.1 us  [shards(): weights_far = lax.ppermute(weights, axes, along_z(ZL))]
    select_n x1 -> x0, other arithmetic: 1.93 us -> none  [shards(): jnp.where(odd == 0, near_too, near)]
    ppermute x2, waiting for transfers between devices: 26.6 us -> 24.8 us  [the longest x1 24.8 us: shards(): passed = lax.ppermute(near, 'zl', [(a, a ^ 1) for a in range(ZL)])]
  transfers between devices with their start and end apart: 8 -> 8, of which waited for: 4 -> 5; matrix products, arithmetic and copies ran while one was open for 2% -> 3% of each run, Pallas kernels for 4% -> 5%
where the time goes in v4:
time: 174 us; the launch traced here: 173 us
  starting transfers between devices  60.5 us (35%)
  waiting for transfers between devices  53.7 us (31%)
  blocking collectives  30.6 us (18%)
  Pallas kernels  16.2 us (9%)
  local copies, waits for them, and re-layouts  8.38 us (5%)
  between operations  2.75 us (2%)
    ppermute x1, waiting for transfers between devices, shards(): passed = lax.ppermute(near, 'zl', [(a, a ^ 1) for a in range(ZL)])  24.8 us
    all_to_all x1, blocking collectives, shards(): got = lax.all_to_all(sends, XY, 0, 0)  24.5 us
    all_to_all x1, waiting for transfers between devices, shards(): got = lax.all_to_all(along, ZZ, 0, 0)  13.3 us
    ppermute x1, starting transfers between devices, shards(): weights_far = lax.ppermute(weights, axes, along_z(ZL))  13.1 us
    ppermute x1, starting transfers between devices, shards(): passed = lax.ppermute(near, 'zl', [(a, a ^ 1) for a in range(ZL)])  11.7 us
    all_to_all x1, starting transfers between devices, shards(): got = lax.all_to_all(along, ZZ, 0, 0)  11.6 us
    all_to_all x1, waiting for transfers between devices, shards(): lax.all_to_all(jnp.broadcast_to(summed[None, :rows], (ZL, rows, wide)), '...  9.02 us
    ppermute x1, starting transfers between devices, shards(): other = lax.ppermute(hidden, 'core', swap_core)  8.92 us
  transfers between devices with their start and end apart: 8, of which 5 were waited for; matrix products, arithmetic and copies ran while one was open for 3% of the time, Pallas kernels for 5%

profile of v4, /device:TPU:1, one launch (start us, length us, event | category | flops | bytes accessed | tf_op | source)
XLA Modules:
  0.0 173.4 jit_solution(11966209254642814106)
XLA Ops:
  0.6 8.9 %collective-permute-start.1 = (bf16[256,8192]{1,0:T(8,128)(2,1)}, bf16[256,8192]{1,0:T(8,128)(2,1)}, u32[]{:S(2)}, u32[]{:S(2)}) collective-permute-start(bf16[256,8192]{1,0:T(8,128)(2,1)} %bitcast.20), channel_id=1, source_target_pairs={{0,32},{32,0},{1,33},{33,1},{2,34},{34,2},{3,35},{35,3},{4,36},{36... | collective-permute-start | bytes 12582920 | tf_op jit(solution)/shard_map/ppermute | solution.py:268
  9.6 0.7 constant_dynamic-slice_fusion.1
  10.4 1.1 broadcast_in_dim.6
  11.5 3.7 %all-to-all-start = ((bf16[16,144,256]{2,1,0:T(8,128)(2,1)}), bf16[16,144,256]{2,1,0:T(8,128)(2,1)S(1)}, u32[]{:S(2)}, u32[]{:S(2)}) async-start(bf16[16,144,256]{2,1,0:T(8,128)(2,1)} %broadcast_in_dim.6), calls=%async_computation | async-start | bytes 2359296 | tf_op jit(solution)/shard_map/all_to_all | solution.py:151
  15.2 13.1 %collective-permute-start = (bf16[144,512]{1,0:T(8,128)(2,1)S(1)}, bf16[144,512]{1,0:T(8,128)(2,1)S(1)}, u32[]{:S(2)}, u32[]{:S(2)}) collective-permute-start(bf16[144,512]{1,0:T(8,128)(2,1)S(1)} %pad_maximum_fusion), channel_id=1, source_target_pairs={{0,4},{1,5},{2,6},{3,7},{4,0},{5,1},{6,2},{7,3},{8,12},{9,13},{10,... | collective-permute-start | bytes 442376 | tf_op jit(solution)/shard_map/ppermute | solution.py:265
  28.3 4.0 %collective-permute-done = bf16[144,512]{1,0:T(8,128)(2,1)S(1)} collective-permute-done((bf16[144,512]{1,0:T(8,128)(2,1)S(1)}, bf16[144,512]{1,0:T(8,128)(2,1)S(1)}, u32[]{:S(2)}, u32[]{:S(2)}) %collective-permute-start) | collective-permute-done | bytes 147488 | tf_op jit(solution)/shard_map/ppermute | solution.py:265
  32.3 2.5 %all-to-all-done.own_ref = bf16[16,144,256]{2,1,0:T(8,128)(2,1)S(1)} async-done(((bf16[16,144,256]{2,1,0:T(8,128)(2,1)}), bf16[16,144,256]{2,1,0:T(8,128)(2,1)S(1)}, u32[]{:S(2)}, u32[]{:S(2)}) %all-to-all-start) | async-done | bytes 1179680 | tf_op jit(solution)/shard_map/all_to_all | solution.py:151
  34.9 1.8 %broadcast_in_dim.7 = bf16[16,144,512]{2,1,0:T(8,128)(2,1)} broadcast(bf16[144,512]{1,0:T(8,128)(2,1)S(1)} %collective-permute-done), dimensions={1,2} | broadcast | bytes 2506752 | tf_op jit(solution)/shard_map/broadcast_in_dim | solution.py:151
  36.7 3.8 %all-to-all-start.1 = ((bf16[16,144,512]{2,1,0:T(8,128)(2,1)}), bf16[16,144,512]{2,1,0:T(8,128)(2,1)S(1)}, u32[]{:S(2)}, u32[]{:S(2)}) async-start(bf16[16,144,512]{2,1,0:T(8,128)(2,1)} %broadcast_in_dim.7), calls=%async_computation.1 | async-start | bytes 4718592 | tf_op jit(solution)/shard_map/all_to_all | solution.py:151
  40.5 11.7 %collective-permute-start.2 = (bf16[16,144,256]{2,1,0:T(8,128)(2,1)}, bf16[16,144,256]{2,1,0:T(8,128)(2,1)}, u32[]{:S(2)}, u32[]{:S(2)}) collective-permute-start(bf16[16,144,256]{2,1,0:T(8,128)(2,1)} %copy-done.1), channel_id=1, source_target_pairs={{0,64},{64,0},{128,192},{192,128},{256,320},{320,256},{384,448},{4... | collective-permute-start | bytes 3538952 | tf_op jit(solution)/shard_map/ppermute | solution.py:272
  52.3 24.8 %collective-permute-done.2.passed_ref = bf16[16,144,256]{2,1,0:T(8,128)(2,1)} collective-permute-done((bf16[16,144,256]{2,1,0:T(8,128)(2,1)}, bf16[16,144,256]{2,1,0:T(8,128)(2,1)}, u32[]{:S(2)}, u32[]{:S(2)}) %collective-permute-start.2) | collective-permute-done | bytes 1179680 | tf_op jit(solution)/shard_map/ppermute | solution.py:272
  77.2 1.3 copy-done.2
  78.4 5.0 %near.1 = (f32[256,640]{1,0:T(8,128)S(1)}, f32[256,640]{1,0:T(8,128)S(1)}) custom-call(s32[3]{0:T(128)S(1)} %pad_add_fusion.where_ref, bf16[256,8192]{1,0:T(8,128)(2,1)} %bitcast.21, bf16[256,8192]{1,0:T(8,128)(2,1)} %collective-permute-done.1.other_ref.hidden_ref, bf16[16,144,256]{2,1,0:T(8,128)(2,1)S(1)} %copy-done.2, ...), custom_call_target="tpu_custom_call" | custom-call | tf_op jit(solution)/shard_map/near/pallas_call | solution.py:126
  83.4 0.8 copy-done.3
  84.3 3.8 %far.3 = f32[256,640]{1,0:T(8,128)} custom-call(s32[3]{0:T(128)S(1)} %pad_add_fusion.where_ref, bf16[256,8192]{1,0:T(8,128)(2,1)} %collective-permute-done.1.other_ref.hidden_ref, bf16[16,144,512]{2,1,0:T(8,128)(2,1)S(1)} %all-to-all-done.1.weight_ref, f32[256,640]{1,0:T(8,128)S(1)} %get-tuple-element.15.before_ref), custom_call_target="tpu_custom_call" | custom-call | tf_op jit(solution)/shard_map/far/pallas_call | solution.py:139
  88.1 4.2 %collective-permute-start.3 = (f32[256,640]{1,0:T(8,128)}, f32[256,640]{1,0:T(8,128)S(1)}, u32[]{:S(2)}, u32[]{:S(2)}) collective-permute-start(f32[256,640]{1,0:T(8,128)} %far.3), channel_id=1, source_target_pairs={{0,32},{32,0},{1,33},{33,1},{2,34},{34,2},{3,35},{35,3},{4,36},{36... | collective-permute-start | bytes 1966088 | tf_op jit(solution)/shard_map/ppermute | solution.py:275
  92.3 0.1 copy.12.mask_ref
  92.5 1.1 copy-done.4
  93.6 2.9 %far.2.mine_ref = f32[256,640]{1,0:T(8,128)S(1)} custom-call(s32[3]{0:T(128)S(1)} %pad_add_fusion.where_ref, bf16[256,8192]{1,0:T(8,128)(2,1)} %bitcast.22, bf16[16,144,512]{2,1,0:T(8,128)(2,1)S(1)} %all-to-all-done.1.weight_ref, f32[256,640]{1,0:T(8,128)S(1)} %copy-done.4), custom_call_target="tpu_custom_call" | custom-call | tf_op jit(solution)/shard_map/far/pallas_call | solution.py:139
  96.6 3.5 %middle.1 = bf16[16,144,256]{2,1,0:T(8,128)(2,1)S(1)} custom-call(f32[256,640]{1,0:T(8,128)S(1)} %far.2.mine_ref, f32[256,640]{1,0:T(8,128)S(1)} %collective-permute-done.3.other_ref, bf16[256,8192]{1,0:T(8,128)(2,1)} %bitcast.23, bf16[256,512]{1,0:T(8,128)(2,1)S(1)} %bitcast.19, f32[256,1]{1,0:T(8,128)S(1)} %copy.12.mask_ref, bf16[128,512]{1,0:T(8,128)(2,1)S(1)} %pad.4.up_ref), custom_call_target="tpu_custom_call" | custom-call | tf_op jit(solution)/shard_map/middle/pallas_call | solution.py:282
  100.1 24.5 %all_to_all.25.got_ref = bf16[16,144,256]{2,1,0:T(8,128)(2,1)S(1)} all-to-all(bf16[16,144,256]{2,1,0:T(8,128)(2,1)S(1)} %middle.1), channel_id=1, replica_groups=mesh['zl'=8,'core'=2,'x'=4,'zh'=2,'y'=4] {'x','y'}, dimensions={0} | all-to-all | bytes 2359296 | tf_op jit(solution)/shard_map/all_to_all | solution.py:291
  124.6 0.9 plane.1
  125.4 11.6 %all-to-all-start.3 = ((bf16[16,16,256]{2,1,0:T(8,128)(2,1)}), bf16[16,16,256]{2,1,0:T(8,128)(2,1)S(1)}, u32[]{:S(2)}, u32[]{:S(2)}) async-start(bf16[16,16,256]{2,1,0:T(8,128)(2,1)} %plane.1), calls=%async_computation.3 | async-start | bytes 262144 | tf_op jit(solution)/shard_map/all_to_all | solution.py:300
  137.0 13.3 %all-to-all-done.3.got_ref = bf16[16,16,256]{2,1,0:T(8,128)(2,1)S(1)} async-done(((bf16[16,16,256]{2,1,0:T(8,128)(2,1)}), bf16[16,16,256]{2,1,0:T(8,128)(2,1)S(1)}, u32[]{:S(2)}, u32[]{:S(2)}) %all-to-all-start.3) | async-done | bytes 131104 | tf_op jit(solution)/shard_map/all_to_all | solution.py:300
  150.4 0.1 gate.1
  150.5 6.1 %psum.7 = f32[16,256]{1,0:T(8,128)S(1)} all-reduce(f32[16,256]{1,0:T(8,128)S(1)} %get-tuple-element.16), channel_id=1, replica_groups=mesh['zl'=8,'core'=2,'x'=4,'zh'=2,'y'=4] {'core'}, use_global_device_ids=true, to_apply=%region_0.1 | all-reduce | flops 4096 | bytes 32768 | tf_op jit(solution)/shard_map/psum | solution.py:309
  156.6 0.5 fusion.2
  157.8 0.6 broadcast_in_dim.8
  158.5 3.4 %all-to-all-start.4 = ((f32[8,8,256]{2,1,0:T(8,128)}), f32[8,8,256]{2,1,0:T(8,128)S(1)}, u32[]{:S(2)}, u32[]{:S(2)}) async-start(f32[8,8,256]{2,1,0:T(8,128)} %broadcast_in_dim.8), calls=%async_computation.4 | async-start | bytes 131072 | tf_op jit(solution)/shard_map/all_to_all | solution.py:311
  162.0 0.6 pad_maximum_fusion.1
  162.6 9.0 %all-to-all-done.4 = f32[8,8,256]{2,1,0:T(8,128)S(1)} async-done(((f32[8,8,256]{2,1,0:T(8,128)}), f32[8,8,256]{2,1,0:T(8,128)S(1)}, u32[]{:S(2)}, u32[]{:S(2)}) %all-to-all-start.4) | async-done | bytes 65568 | tf_op jit(solution)/shard_map/all_to_all | solution.py:311
  171.6 0.6 copy.17
  (25 shorter events, 0.2 us)
Async XLA Ops:
  0.6 9.7 %copy-start = (bf16[256,512]{1,0:T(8,128)(2,1)S(1)}, bf16[256,512]{1,0:T(8,128)(2,1)}, u32[]{:S(2)}) copy-start(bf16[256,512]{1,0:T(8,128)(2,1)} %param.9) | copy-start | bytes 786436
  0.6 76.5 %collective-permute-start.1 = (bf16[256,8192]{1,0:T(8,128)(2,1)}, bf16[256,8192]{1,0:T(8,128)(2,1)}, u32[]{:S(2)}, u32[]{:S(2)}) collective-permute-start(bf16[256,8192]{1,0:T(8,128)(2,1)} %bitcast.20), channel_id=1, source_target_pairs={{0,32},{32,0},{1,33},{33,1},{2,34},{34,2},{3,35},{35,3},{4,36},{36... | collective-permute-start | bytes 12582920 | tf_op jit(solution)/shard_map/ppermute | solution.py:268
  11.5 23.4 %all-to-all-start = ((bf16[16,144,256]{2,1,0:T(8,128)(2,1)}), bf16[16,144,256]{2,1,0:T(8,128)(2,1)S(1)}, u32[]{:S(2)}, u32[]{:S(2)}) async-start(bf16[16,144,256]{2,1,0:T(8,128)(2,1)} %broadcast_in_dim.6), calls=%async_computation | async-start | bytes 2359296 | tf_op jit(solution)/shard_map/all_to_all | solution.py:151
  15.2 17.1 %collective-permute-start = (bf16[144,512]{1,0:T(8,128)(2,1)S(1)}, bf16[144,512]{1,0:T(8,128)(2,1)S(1)}, u32[]{:S(2)}, u32[]{:S(2)}) collective-permute-start(bf16[144,512]{1,0:T(8,128)(2,1)S(1)} %pad_maximum_fusion), channel_id=1, source_target_pairs={{0,4},{1,5},{2,6},{3,7},{4,0},{5,1},{6,2},{7,3},{8,12},{9,13},{10,... | collective-permute-start | bytes 442376 | tf_op jit(solution)/shard_map/ppermute | solution.py:265
  34.8 1.8 %copy-start.1 = (bf16[16,144,256]{2,1,0:T(8,128)(2,1)}, bf16[16,144,256]{2,1,0:T(8,128)(2,1)S(1)}, u32[]{:S(2)}) copy-start(bf16[16,144,256]{2,1,0:T(8,128)(2,1)S(1)} %all-to-all-done.own_ref) | copy-start | bytes 3538948
  36.7 47.6 %all-to-all-start.1 = ((bf16[16,144,512]{2,1,0:T(8,128)(2,1)}), bf16[16,144,512]{2,1,0:T(8,128)(2,1)S(1)}, u32[]{:S(2)}, u32[]{:S(2)}) async-start(bf16[16,144,512]{2,1,0:T(8,128)(2,1)} %broadcast_in_dim.7), calls=%async_computation.1 | async-start | bytes 4718592 | tf_op jit(solution)/shard_map/all_to_all | solution.py:151
  40.5 36.6 %collective-permute-start.2 = (bf16[16,144,256]{2,1,0:T(8,128)(2,1)}, bf16[16,144,256]{2,1,0:T(8,128)(2,1)}, u32[]{:S(2)}, u32[]{:S(2)}) collective-permute-start(bf16[16,144,256]{2,1,0:T(8,128)(2,1)} %copy-done.1), channel_id=1, source_target_pairs={{0,64},{64,0},{128,192},{192,128},{256,320},{320,256},{384,448},{4... | collective-permute-start | bytes 3538952 | tf_op jit(solution)/shard_map/ppermute | solution.py:272
  77.2 1.3 copy-start.2
  83.4 0.8 copy-start.3
  84.3 8.1 %copy-start.7 = (s32[1,2,128]{2,1,0:T(2,128)S(1)}, s32[1,2,128]{2,1,0:T(2,128)}, u32[]{:S(2)}) copy-start(s32[1,2,128]{2,1,0:T(2,128)} %param.8) | copy-start | bytes 3076
  84.3 8.2 %copy-start.6 = (bf16[64,512]{1,0:T(8,128)(2,1)S(1)}, bf16[64,512]{1,0:T(8,128)(2,1)}, u32[]{:S(2)}) copy-start(bf16[64,512]{1,0:T(8,128)(2,1)} %param.11) | copy-start | bytes 196612
  88.1 8.5 %collective-permute-start.3 = (f32[256,640]{1,0:T(8,128)}, f32[256,640]{1,0:T(8,128)S(1)}, u32[]{:S(2)}, u32[]{:S(2)}) collective-permute-start(f32[256,640]{1,0:T(8,128)} %far.3), channel_id=1, source_target_pairs={{0,32},{32,0},{1,33},{33,1},{2,34},{34,2},{3,35},{35,3},{4,36},{36... | collective-permute-start | bytes 1966088 | tf_op jit(solution)/shard_map/ppermute | solution.py:275
  92.5 1.1 copy-start.4
  93.6 3.0 %copy-start.5 = (bf16[1,2,128,512]{3,2,1,0:T(8,128)(2,1)S(1)}, bf16[1,2,128,512]{3,2,1,0:T(8,128)(2,1)}, u32[]{:S(2)}) copy-start(bf16[1,2,128,512]{3,2,1,0:T(8,128)(2,1)} %param.7) | copy-start | bytes 786436
  125.4 24.9 %all-to-all-start.3 = ((bf16[16,16,256]{2,1,0:T(8,128)(2,1)}), bf16[16,16,256]{2,1,0:T(8,128)(2,1)S(1)}, u32[]{:S(2)}, u32[]{:S(2)}) async-start(bf16[16,16,256]{2,1,0:T(8,128)(2,1)} %plane.1), calls=%async_computation.3 | async-start | bytes 262144 | tf_op jit(solution)/shard_map/all_to_all | solution.py:300
  158.5 13.1 %all-to-all-start.4 = ((f32[8,8,256]{2,1,0:T(8,128)}), f32[8,8,256]{2,1,0:T(8,128)S(1)}, u32[]{:S(2)}, u32[]{:S(2)}) async-start(f32[8,8,256]{2,1,0:T(8,128)} %broadcast_in_dim.8), calls=%async_computation.4 | async-start | bytes 131072 | tf_op jit(solution)/shard_map/all_to_all | solution.py:311

commit v5 on v4

--- a/solution.py
+++ b/solution.py
@@ -21,8 +21,8 @@
     return pl.BlockSpec(memory_space=pltpu.VMEM)
 
 
-def params():
-    return pltpu.CompilerParams(vmem_limit_bytes=50 * 1024 * 1024)
+def params(mib=50):
+    return pltpu.CompilerParams(vmem_limit_bytes=mib * 1024 * 1024)
 
 
 def pieces(total, shape):
@@ -73,87 +73,118 @@
     return lax.dot_general(hidden, down_t, (((1,), (1,)), ((), ())), preferred_element_type=F32)
 
 
-def near_kernel(
-    where_ref, mine_ref, other_ref, own_ref, passed_ref, out_mine_ref, out_other_ref, mine, other, mine_sems, other_sems
-):
+def own_kernel(where_ref, mine_ref, other_ref, own_ref, out_mine_ref, out_other_ref, mine, other, mine_sems, other_sems):
     copies = fetches(where_ref, mine_ref, mine, mine_sems, False)
     copies += fetches(where_ref, other_ref, other, other_sems, False)
     for copy in copies:
         copy.start()
     for copy in copies:
         copy.wait()
-
-    def body(first_ref, second_ref):
-        half = first_ref.shape[2]
-        first, first_t = unpacked(first_ref)
-        second, second_t = unpacked(second_ref)
-        down_t = jnp.concatenate([first_t, second_t], axis=0)
+    half = own_ref.shape[2]
+    value, down_t = unpacked(own_ref)
+    nothing = jnp.zeros_like(down_t)
+
+    def body(columns, rest, down_t):
         for ref, out_ref in ((mine, out_mine_ref), (other, out_other_ref)):
             hidden = ref[...]
-            out_ref[:, :half] = jnp.dot(hidden, first, preferred_element_type=F32)
-            out_ref[:, half : 2 * half] = jnp.dot(hidden, second, preferred_element_type=F32)
+            out_ref[:, columns] = jnp.dot(hidden, value, preferred_element_type=F32)
+            out_ref[:, rest] = jnp.zeros((hidden.shape[0], half), F32)
             out_ref[:, 2 * half :] = low_part(hidden, down_t)
 
     @pl.when(where_ref[2] == 0)
     def _():
-        body(own_ref, passed_ref)
+        body(slice(0, half), slice(half, 2 * half), jnp.concatenate([down_t, nothing], axis=0))
 
     @pl.when(where_ref[2] != 0)
     def _():
-        body(passed_ref, own_ref)
-
-
-def far_kernel(where_ref, hidden_ref, weight_ref, before_ref, out_ref, buffer, sems):
-    copies = fetches(where_ref, hidden_ref, buffer, sems, True)
-    for copy in copies:
+        body(slice(half, 2 * half), slice(0, half), jnp.concatenate([nothing, down_t], axis=0))
+
+
+def last_kernel(keep, where_ref, hidden_ref, weight_ref, sent_ref, before_ref, out_ref, *refs):
+    if keep:
+        kept_ref, far, near, far_sems, near_sems, passed_ref, passed_sem, keep_sem = refs
+    else:
+        far, near, far_sems, near_sems, passed_ref, passed_sem = refs
+    far_copies = fetches(where_ref, hidden_ref, far, far_sems, True)
+    near_copies = fetches(where_ref, hidden_ref, near, near_sems, False)
+    near_copies.append(pltpu.make_async_copy(sent_ref, passed_ref, passed_sem))
+    for copy in far_copies + near_copies:
         copy.start()
+    if keep:
+        whole = pltpu.make_async_copy(hidden_ref, kept_ref, keep_sem)
+        whole.start()
     features = weight_ref.shape[2]
+    half = passed_ref.shape[2]
     value, down_t = unpacked(weight_ref)
-    for copy in copies:
+    for copy in far_copies:
         copy.wait()
-    hidden = buffer[...]
+    hidden = far[...]
     out_ref[:, :features] = before_ref[:, :features] + jnp.dot(hidden, value, preferred_element_type=F32)
     out_ref[:, features:] = before_ref[:, features:] + low_part(hidden, down_t)
+    for copy in near_copies:
+        copy.wait()
+    value, down_t = unpacked(passed_ref)
+    nothing = jnp.zeros_like(down_t)
+
+    def body(columns, down_t):
+        hidden = near[...]
+        out_ref[:, columns] += jnp.dot(hidden, value, preferred_element_type=F32)
+        out_ref[:, features:] += low_part(hidden, down_t)
+
+    @pl.when(where_ref[2] == 0)
+    def _():
+        body(slice(half, features), jnp.concatenate([nothing, down_t], axis=0))
+
+    @pl.when(where_ref[2] != 0)
+    def _():
+        body(slice(0, half), jnp.concatenate([down_t, nothing], axis=0))
+
+    if keep:
+        whole.wait()
 
 
 def smem():
     return pl.BlockSpec(memory_space=pltpu.SMEM)
 
 
-def near_forward(where, mine, other, own, passed):
+def blocks(tokens, width, count):
+    return [pltpu.VMEM((tokens, width // 4), BF16)] * count + [pltpu.SemaphoreType.DMA((X * Y,))] * count
+
+
+def own_forward(where, mine, other, own):
     tokens, width = mine.shape
     out = (tokens, 2 * own.shape[2] + LANES)
     return pl.pallas_call(
-        near_kernel,
-        in_specs=[smem(), anywhere(), anywhere(), vmem(), vmem()],
+        own_kernel,
+        in_specs=[smem(), anywhere(), anywhere(), vmem()],
         out_specs=[vmem()] * 2,
         out_shape=[jax.ShapeDtypeStruct(out, F32)] * 2,
-        scratch_shapes=[pltpu.VMEM((tokens, width // 4), BF16)] * 2 + [pltpu.SemaphoreType.DMA((X * Y,))] * 2,
+        scratch_shapes=blocks(tokens, width, 2),
         compiler_params=params(),
-        name="near",
-    )(where, mine, other, own, passed)
-
-
-def far_forward(where, hidden, weights, before):
+        name="own",
+    )(where, mine, other, own)
+
+
+def last_forward(where, hidden, weights, passed, before, keep):
     tokens, width = hidden.shape
+    out = jax.ShapeDtypeStruct(before.shape, F32)
+    scratch = blocks(tokens, width, 2) + [pltpu.VMEM(passed.shape, BF16), pltpu.SemaphoreType.DMA]
     return pl.pallas_call(
-        far_kernel,
-        in_specs=[smem(), anywhere(), vmem(), vmem()],
-        out_specs=vmem(),
-        out_shape=jax.ShapeDtypeStruct(before.shape, F32),
-        scratch_shapes=[pltpu.VMEM((tokens, width // 4), BF16), pltpu.SemaphoreType.DMA((X * Y,))],
-        compiler_params=params(),
-        name="far",
-    )(where, hidden, weights, before)
+        lambda *refs: last_kernel(keep, *refs),
+        in_specs=[smem(), anywhere(), vmem(), anywhere(), vmem()],
+        out_specs=[vmem(), vmem()] if keep else vmem(),
+        out_shape=[out, jax.ShapeDtypeStruct(hidden.shape, BF16)] if keep else out,
+        scratch_shapes=scratch + [pltpu.SemaphoreType.DMA] if keep else scratch,
+        compiler_params=params(48),
+        name="last",
+    )(where, hidden, weights, passed, before)
 
 
 def plane_gather(w):
     return lax.all_to_all(jnp.broadcast_to(w[None], (X * Y,) + w.shape), XY, 0, 0)
 
 
-def middle_kernel(mine_ref, other_ref, held_ref, read_ref, mask_ref, up_ref, out_ref, hidden_ref, sem):
-    copy = pltpu.make_async_copy(held_ref, hidden_ref, sem)
-    copy.start()
+def middle_kernel(mine_ref, other_ref, hidden_ref, read_ref, mask_ref, up_ref, out_ref):
     tokens, features = read_ref.shape
     rank = up_ref.shape[0] // 2
     base = mine_ref[:, :features] + other_ref[:, :features]
@@ -180,7 +211,6 @@
     part = features // (X * ZH * Y)
     lane = lax.broadcasted_iota(jnp.int32, (EXTRA, LANES), 1)
     sent = pieces(total, (EXTRA, LANES)).astype(BF16)
-    copy.wait()
     for x in range(X):
         for y in range(Y):
             to = x * Y + y
@@ -251,18 +281,12 @@
     spots = list(np.ndindex(*sizes))
     flat = lambda p: int(np.ravel_multi_index(p, sizes))
 
-    def along_z(step):
-        moved = []
-        for a, c, b, e, d in spots:
-            z = (e * ZL + a + step) % (ZH * ZL)
-            moved.append((flat((a, c, b, e, d)), flat((z % ZL, c, b, z // ZL, d))))
-        return moved
-
+    mirror = [(flat((a, c, b, e, d)), flat((ZL - 1 - a, c, b, 1 - e, d))) for a, c, b, e, d in spots]
     swap_core = [(0, 1), (1, 0)]
     odd = zl % 2
     half = features // 2
 
-    weights_far = lax.ppermute(weights, axes, along_z(ZL))
+    weights_far = lax.ppermute(weights, axes, mirror)
     near = plane_gather(lax.dynamic_slice_in_dim(weights, odd * half, half, 1))
     where = jnp.stack([core, zh, odd]).astype(jnp.int32)
     other = lax.ppermute(hidden, "core", swap_core)
@@ -270,10 +294,10 @@
     weights_far, near = lax.optimization_barrier((weights_far, near))
     far = plane_gather(weights_far)
     passed = lax.ppermute(near, "zl", [(a, a ^ 1) for a in range(ZL)])
-    near_mine, near_other = near_forward(where, hidden, other, near, passed)
-    part_other = far_forward(where, other, far, near_other)
+    before_mine, before_other = own_forward(where, hidden, other, near)
+    part_other = last_forward(where, other, far, passed, before_other, False)
     from_other = lax.ppermute(part_other, "core", swap_core)
-    part_mine = far_forward(where, hidden, far, near_mine)
+    part_mine, kept = last_forward(where, hidden, far, passed, before_mine, True)
 
     read = readout.reshape(tokens, features)
     mask = response.reshape(tokens, 1).astype(F32)
@@ -281,13 +305,12 @@
     wide = width // (X * ZH * Y)
     sends = pl.pallas_call(
         middle_kernel,
-        in_specs=[vmem(), vmem(), anywhere(), vmem(), vmem(), vmem()],
+        in_specs=[vmem()] * 6,
         out_specs=vmem(),
         out_shape=jax.ShapeDtypeStruct((X * Y, ZH * rank + EXTRA, wide), BF16),
-        scratch_shapes=[pltpu.VMEM((tokens, width), BF16), pltpu.SemaphoreType.DMA],
         compiler_params=params(),
         name="middle",
-    )(part_mine, from_other, hidden, read, mask, up)
+    )(part_mine, from_other, kept, read, mask, up)
     got = lax.all_to_all(sends, XY, 0, 0)
     along = pl.pallas_call(
         plane_kernel,

time: 174 us -> 165 us (0.948)
  starting transfers between devices: 60.5 us -> 46.9 us
  waiting for transfers between devices: 53.7 us -> 58.3 us
  Pallas kernels: 16.2 us -> 19.7 us
  blocking collectives: 30.6 us -> 27.3 us
    ppermute x1, starting transfers between devices: 11.7 us -> 1.92 us  [shards(): passed = lax.ppermute(near, 'zl', [(a, a ^ 1) for a in range(ZL)])]
    ppermute x1, waiting for transfers between devices: 4 us -> 13.5 us  [shards(): weights_far = lax.ppermute(weights, axes, mirror)]
    ppermute x1, starting transfers between devices: 13.1 us -> 8.81 us  [shards(): weights_far = lax.ppermute(weights, axes, mirror)]
    ppermute x1, waiting for transfers between devices: 24.8 us -> 20.6 us  [shards(): passed = lax.ppermute(near, 'zl', [(a, a ^ 1) for a in range(ZL)])]
    all_to_all x1, starting transfers between devices: 11.6 us -> 7.63 us  [shards(): got = lax.all_to_all(along, ZZ, 0, 0)]
    pallas_call x4, Pallas kernels: 15.3 us -> 18.7 us  [the longest x2 11.2 us: last_forward(): pl.pallas_call(lambda *refs: last_kernel(keep, *refs), in_specs=[smem(),...]
    all_to_all x1, blocking collectives: 24.5 us -> 21.2 us  [shards(): got = lax.all_to_all(sends, XY, 0, 0)]
    all_to_all x2, starting transfers between devices: 7.53 us -> 10.2 us  [plane_gather(): lax.all_to_all(jnp.broadcast_to(w[None], (X * Y,) + w.shape), XY, 0, 0)]
  transfers between devices with their start and end apart: 8 -> 8, of which waited for: 5 -> 5; matrix products, arithmetic and copies ran while one was open for 3% -> 3% of each run, Pallas kernels for 5% -> 6%
where the time goes in v5:
time: 165 us
  waiting for transfers between devices  58.3 us (35%)
  starting transfers between devices  46.9 us (28%)
  blocking collectives  27.3 us (17%)
  Pallas kernels  19.7 us (12%)
  local copies, waits for them, and re-layouts  8.39 us (5%)
  between operations  2.75 us (2%)
    all_to_all x1, blocking collectives, shards(): got = lax.all_to_all(sends, XY, 0, 0)  21.2 us
    ppermute x1, waiting for transfers between devices, shards(): passed = lax.ppermute(near, 'zl', [(a, a ^ 1) for a in range(ZL)])  20.6 us
    ppermute x1, waiting for transfers between devices, shards(): weights_far = lax.ppermute(weights, axes, mirror)  13.5 us
    all_to_all x1, waiting for transfers between devices, shards(): got = lax.all_to_all(along, ZZ, 0, 0)  13.3 us
    pallas_call x2, Pallas kernels, last_forward(): pl.pallas_call(lambda *refs: last_kernel(keep, *refs), in_specs=[smem(),...  11.2 us
    all_to_all x2, starting transfers between devices, plane_gather(): lax.all_to_all(jnp.broadcast_to(w[None], (X * Y,) + w.shape), XY, 0, 0)  10.2 us
    all_to_all x1, waiting for transfers between devices, shards(): lax.all_to_all(jnp.broadcast_to(summed[None, :rows], (ZL, rows, wide)), '...  9.1 us
    ppermute x1, starting transfers between devices, shards(): other = lax.ppermute(hidden, 'core', swap_core)  8.92 us
  transfers between devices with their start and end apart: 8, of which 5 were waited for; matrix products, arithmetic and copies ran while one was open for 3% of the time, Pallas kernels for 6%

profile of v5, /device:TPU:1, one launch (start us, length us, event | category | flops | bytes accessed | tf_op | source)
XLA Modules:
  0.0 164.6 jit_solution(16755794718547672628)
XLA Ops:
  0.6 8.9 %collective-permute-start.2 = (bf16[256,8192]{1,0:T(8,128)(2,1)}, bf16[256,8192]{1,0:T(8,128)(2,1)}, u32[]{:S(2)}, u32[]{:S(2)}) collective-permute-start(bf16[256,8192]{1,0:T(8,128)(2,1)} %bitcast.20), channel_id=1, source_target_pairs={{0,32},{32,0},{1,33},{33,1},{2,34},{34,2},{3,35},{35,3},{4,36},{36... | collective-permute-start | bytes 12582920 | tf_op jit(solution)/shard_map/ppermute | solution.py:292
  9.6 0.7 constant_dynamic-slice_fusion.1
  10.4 1.1 broadcast_in_dim.6
  11.5 3.7 %all-to-all-start = ((bf16[16,144,256]{2,1,0:T(8,128)(2,1)}), bf16[16,144,256]{2,1,0:T(8,128)(2,1)S(1)}, u32[]{:S(2)}, u32[]{:S(2)}) async-start(bf16[16,144,256]{2,1,0:T(8,128)(2,1)} %broadcast_in_dim.6), calls=%async_computation | async-start | bytes 2359296 | tf_op jit(solution)/shard_map/all_to_all | solution.py:184
  15.2 8.8 %collective-permute-start = (bf16[144,512]{1,0:T(8,128)(2,1)S(1)}, bf16[144,512]{1,0:T(8,128)(2,1)S(1)}, u32[]{:S(2)}, u32[]{:S(2)}) collective-permute-start(bf16[144,512]{1,0:T(8,128)(2,1)S(1)} %pad_maximum_fusion), channel_id=1, source_target_pairs={{0,452},{1,453},{2,454},{3,455},{4,448},{5,449},{6,450},{7,451},{8... | collective-permute-start | bytes 442376 | tf_op jit(solution)/shard_map/ppermute | solution.py:289
  24.0 13.5 %collective-permute-done = bf16[144,512]{1,0:T(8,128)(2,1)S(1)} collective-permute-done((bf16[144,512]{1,0:T(8,128)(2,1)S(1)}, bf16[144,512]{1,0:T(8,128)(2,1)S(1)}, u32[]{:S(2)}, u32[]{:S(2)}) %collective-permute-start) | collective-permute-done | bytes 147488 | tf_op jit(solution)/shard_map/ppermute | solution.py:289
  37.5 1.8 %broadcast_in_dim.7 = bf16[16,144,512]{2,1,0:T(8,128)(2,1)} broadcast(bf16[144,512]{1,0:T(8,128)(2,1)S(1)} %collective-permute-done), dimensions={1,2} | broadcast | bytes 2506752 | tf_op jit(solution)/shard_map/broadcast_in_dim | solution.py:184
  39.3 6.5 %all-to-all-start.1 = ((bf16[16,144,512]{2,1,0:T(8,128)(2,1)}), bf16[16,144,512]{2,1,0:T(8,128)(2,1)S(1)}, u32[]{:S(2)}, u32[]{:S(2)}) async-start(bf16[16,144,512]{2,1,0:T(8,128)(2,1)} %broadcast_in_dim.7), calls=%async_computation.1 | async-start | bytes 4718592 | tf_op jit(solution)/shard_map/all_to_all | solution.py:184
  45.9 1.9 %collective-permute-start.1 = (bf16[16,144,256]{2,1,0:T(8,128)(2,1)}, bf16[16,144,256]{2,1,0:T(8,128)(2,1)}, u32[]{:S(2)}, u32[]{:S(2)}) collective-permute-start(bf16[16,144,256]{2,1,0:T(8,128)(2,1)} %copy-done.1), channel_id=1, source_target_pairs={{0,64},{64,0},{128,192},{192,128},{256,320},{320,256},{384,448},{4... | collective-permute-start | bytes 3538952 | tf_op jit(solution)/shard_map/ppermute | solution.py:296
  47.9 1.3 copy-done.2
  49.2 3.8 %own.1 = (f32[256,640]{1,0:T(8,128)S(1)}, f32[256,640]{1,0:T(8,128)S(1)}) custom-call(s32[3]{0:T(128)S(1)} %pad_add_fusion.where_ref.refs_0_, bf16[256,8192]{1,0:T(8,128)(2,1)} %bitcast.21, bf16[256,8192]{1,0:T(8,128)(2,1)} %collective-permute-done.2.other_ref.refs_1_, bf16[16,144,256]{2,1,0:T(8,128)(2,1)S(1)} %copy-done.2), custom_call_target="tpu_custom_call" | custom-call | tf_op jit(solution)/shard_map/own/pallas_call | solution.py:157
  53.0 0.8 copy-done.3
  53.8 20.6 %collective-permute-done.1.refs_3_ = bf16[16,144,256]{2,1,0:T(8,128)(2,1)} collective-permute-done((bf16[16,144,256]{2,1,0:T(8,128)(2,1)}, bf16[16,144,256]{2,1,0:T(8,128)(2,1)}, u32[]{:S(2)}, u32[]{:S(2)}) %collective-permute-start.1) | collective-permute-done | bytes 1179680 | tf_op jit(solution)/shard_map/ppermute | solution.py:296
  74.4 1.8 %all-to-all-done.1.refs_2_ = bf16[16,144,512]{2,1,0:T(8,128)(2,1)S(1)} async-done(((bf16[16,144,512]{2,1,0:T(8,128)(2,1)}), bf16[16,144,512]{2,1,0:T(8,128)(2,1)S(1)}, u32[]{:S(2)}, u32[]{:S(2)}) %all-to-all-start.1) | async-done | bytes 2359328 | tf_op jit(solution)/shard_map/all_to_all | solution.py:184
  76.2 1.1 copy-done.4
  77.3 5.0 %last.3 = f32[256,640]{1,0:T(8,128)} custom-call(s32[3]{0:T(128)S(1)} %pad_add_fusion.where_ref.refs_0_, bf16[256,8192]{1,0:T(8,128)(2,1)} %collective-permute-done.2.other_ref.refs_1_, bf16[16,144,512]{2,1,0:T(8,128)(2,1)S(1)} %all-to-all-done.1.refs_2_, bf16[16,144,256]{2,1,0:T(8,128)(2,1)} %collective-permute-done.1.refs_3_, f32[256,640]{1,0:T(8,128)S(1)} %copy-done.4), custom_call_target="tpu_custom_call" | custom-call | tf_op jit(solution)/shard_map/last/pallas_call | solution.py:172
  82.3 6.1 %collective-permute-start.3 = (f32[256,640]{1,0:T(8,128)}, f32[256,640]{1,0:T(8,128)}, u32[]{:S(2)}, u32[]{:S(2)}) collective-permute-start(f32[256,640]{1,0:T(8,128)} %last.3), channel_id=1, source_target_pairs={{0,32},{32,0},{1,33},{33,1},{2,34},{34,2},{3,35},{35,3},{4,36},{36... | collective-permute-start | bytes 1966088 | tf_op jit(solution)/shard_map/ppermute | solution.py:299
  88.4 0.1 copy.12.mask_ref
  88.6 6.2 %last.2 = (f32[256,640]{1,0:T(8,128)S(1)}, bf16[256,8192]{1,0:T(8,128)(2,1)}) custom-call(s32[3]{0:T(128)S(1)} %pad_add_fusion.where_ref.refs_0_, bf16[256,8192]{1,0:T(8,128)(2,1)} %bitcast.22, bf16[16,144,512]{2,1,0:T(8,128)(2,1)S(1)} %all-to-all-done.1.refs_2_, bf16[16,144,256]{2,1,0:T(8,128)(2,1)} %collective-permute-done.1.refs_3_, ...), custom_call_target="tpu_custom_call" | custom-call | tf_op jit(solution)/shard_map/last/pallas_call | solution.py:172
  94.8 3.7 %middle.1 = bf16[16,144,256]{2,1,0:T(8,128)(2,1)S(1)} custom-call(f32[256,640]{1,0:T(8,128)S(1)} %get-tuple-element.17.mine_ref, f32[256,640]{1,0:T(8,128)} %collective-permute-done.3.other_ref, bf16[256,8192]{1,0:T(8,128)(2,1)} %get-tuple-element.19.hidden_ref, bf16[256,512]{1,0:T(8,128)(2,1)S(1)} %bitcast.19, f32[256,1]{1,0:T(8,128)S(1)} %copy.12.mask_ref, ...), custom_call_target="tpu_custom_call" | custom-call | tf_op jit(solution)/shard_map/middle/pallas_call | solution.py:306
  98.5 21.2 %all_to_all.25.got_ref = bf16[16,144,256]{2,1,0:T(8,128)(2,1)S(1)} all-to-all(bf16[16,144,256]{2,1,0:T(8,128)(2,1)S(1)} %middle.1), channel_id=1, replica_groups=mesh['zl'=8,'core'=2,'x'=4,'zh'=2,'y'=4] {'x','y'}, dimensions={0} | all-to-all | bytes 2359296 | tf_op jit(solution)/shard_map/all_to_all | solution.py:314
  119.7 0.9 plane.1
  120.6 7.6 %all-to-all-start.3 = ((bf16[16,16,256]{2,1,0:T(8,128)(2,1)}), bf16[16,16,256]{2,1,0:T(8,128)(2,1)S(1)}, u32[]{:S(2)}, u32[]{:S(2)}) async-start(bf16[16,16,256]{2,1,0:T(8,128)(2,1)} %plane.1), calls=%async_computation.3 | async-start | bytes 262144 | tf_op jit(solution)/shard_map/all_to_all | solution.py:323
  128.2 13.3 %all-to-all-done.3.got_ref = bf16[16,16,256]{2,1,0:T(8,128)(2,1)S(1)} async-done(((bf16[16,16,256]{2,1,0:T(8,128)(2,1)}), bf16[16,16,256]{2,1,0:T(8,128)(2,1)S(1)}, u32[]{:S(2)}, u32[]{:S(2)}) %all-to-all-start.3) | async-done | bytes 131104 | tf_op jit(solution)/shard_map/all_to_all | solution.py:323
  141.5 0.1 gate.1
  141.7 6.1 %psum.7 = f32[16,256]{1,0:T(8,128)S(1)} all-reduce(f32[16,256]{1,0:T(8,128)S(1)} %get-tuple-element.20), channel_id=1, replica_groups=mesh['zl'=8,'core'=2,'x'=4,'zh'=2,'y'=4] {'core'}, use_global_device_ids=true, to_apply=%region_0.1 | all-reduce | flops 4096 | bytes 32768 | tf_op jit(solution)/shard_map/psum | solution.py:332
  147.8 0.5 fusion.2
  149.1 0.6 broadcast_in_dim.8
  149.7 3.4 %all-to-all-start.4 = ((f32[8,8,256]{2,1,0:T(8,128)}), f32[8,8,256]{2,1,0:T(8,128)S(1)}, u32[]{:S(2)}, u32[]{:S(2)}) async-start(f32[8,8,256]{2,1,0:T(8,128)} %broadcast_in_dim.8), calls=%async_computation.4 | async-start | bytes 131072 | tf_op jit(solution)/shard_map/all_to_all | solution.py:334
  153.1 0.6 pad_maximum_fusion.1
  153.7 9.1 %all-to-all-done.4 = f32[8,8,256]{2,1,0:T(8,128)S(1)} async-done(((f32[8,8,256]{2,1,0:T(8,128)}), f32[8,8,256]{2,1,0:T(8,128)S(1)}, u32[]{:S(2)}, u32[]{:S(2)}) %all-to-all-start.4) | async-done | bytes 65568 | tf_op jit(solution)/shard_map/all_to_all | solution.py:334
  162.8 0.6 copy.17
  (25 shorter events, 0.2 us)
Async XLA Ops:
  0.6 9.7 %copy-start = (bf16[256,512]{1,0:T(8,128)(2,1)S(1)}, bf16[256,512]{1,0:T(8,128)(2,1)}, u32[]{:S(2)}) copy-start(bf16[256,512]{1,0:T(8,128)(2,1)} %param.9) | copy-start | bytes 786436
  0.6 47.3 %collective-permute-start.2 = (bf16[256,8192]{1,0:T(8,128)(2,1)}, bf16[256,8192]{1,0:T(8,128)(2,1)}, u32[]{:S(2)}, u32[]{:S(2)}) collective-permute-start(bf16[256,8192]{1,0:T(8,128)(2,1)} %bitcast.20), channel_id=1, source_target_pairs={{0,32},{32,0},{1,33},{33,1},{2,34},{34,2},{3,35},{35,3},{4,36},{36... | collective-permute-start | bytes 12582920 | tf_op jit(solution)/shard_map/ppermute | solution.py:292
  11.5 26.0 %all-to-all-start = ((bf16[16,144,256]{2,1,0:T(8,128)(2,1)}), bf16[16,144,256]{2,1,0:T(8,128)(2,1)S(1)}, u32[]{:S(2)}, u32[]{:S(2)}) async-start(bf16[16,144,256]{2,1,0:T(8,128)(2,1)} %broadcast_in_dim.6), calls=%async_computation | async-start | bytes 2359296 | tf_op jit(solution)/shard_map/all_to_all | solution.py:184
  15.2 22.3 %collective-permute-start = (bf16[144,512]{1,0:T(8,128)(2,1)S(1)}, bf16[144,512]{1,0:T(8,128)(2,1)S(1)}, u32[]{:S(2)}, u32[]{:S(2)}) collective-permute-start(bf16[144,512]{1,0:T(8,128)(2,1)S(1)} %pad_maximum_fusion), channel_id=1, source_target_pairs={{0,452},{1,453},{2,454},{3,455},{4,448},{5,449},{6,450},{7,451},{8... | collective-permute-start | bytes 442376 | tf_op jit(solution)/shard_map/ppermute | solution.py:289
  37.5 1.8 %copy-start.1 = (bf16[16,144,256]{2,1,0:T(8,128)(2,1)}, bf16[16,144,256]{2,1,0:T(8,128)(2,1)S(1)}, u32[]{:S(2)}) copy-start(bf16[16,144,256]{2,1,0:T(8,128)(2,1)S(1)} %all-to-all-done.own_ref) | copy-start | bytes 3538948
  39.3 36.8 %all-to-all-start.1 = ((bf16[16,144,512]{2,1,0:T(8,128)(2,1)}), bf16[16,144,512]{2,1,0:T(8,128)(2,1)S(1)}, u32[]{:S(2)}, u32[]{:S(2)}) async-start(bf16[16,144,512]{2,1,0:T(8,128)(2,1)} %broadcast_in_dim.7), calls=%async_computation.1 | async-start | bytes 4718592 | tf_op jit(solution)/shard_map/all_to_all | solution.py:184
  45.9 28.5 %collective-permute-start.1 = (bf16[16,144,256]{2,1,0:T(8,128)(2,1)}, bf16[16,144,256]{2,1,0:T(8,128)(2,1)}, u32[]{:S(2)}, u32[]{:S(2)}) collective-permute-start(bf16[16,144,256]{2,1,0:T(8,128)(2,1)} %copy-done.1), channel_id=1, source_target_pairs={{0,64},{64,0},{128,192},{192,128},{256,320},{320,256},{384,448},{4... | collective-permute-start | bytes 3538952 | tf_op jit(solution)/shard_map/ppermute | solution.py:296
  47.9 1.3 copy-start.2
  53.0 0.8 copy-start.3
  76.2 1.1 copy-start.4
  77.2 11.1 %copy-start.7 = (s32[1,2,128]{2,1,0:T(2,128)S(1)}, s32[1,2,128]{2,1,0:T(2,128)}, u32[]{:S(2)}) copy-start(s32[1,2,128]{2,1,0:T(2,128)} %param.8) | copy-start | bytes 3076
  77.2 11.3 %copy-start.6 = (bf16[64,512]{1,0:T(8,128)(2,1)S(1)}, bf16[64,512]{1,0:T(8,128)(2,1)}, u32[]{:S(2)}) copy-start(bf16[64,512]{1,0:T(8,128)(2,1)} %param.11) | copy-start | bytes 196612
  82.3 12.5 %collective-permute-start.3 = (f32[256,640]{1,0:T(8,128)}, f32[256,640]{1,0:T(8,128)}, u32[]{:S(2)}, u32[]{:S(2)}) collective-permute-start(f32[256,640]{1,0:T(8,128)} %last.3), channel_id=1, source_target_pairs={{0,32},{32,0},{1,33},{33,1},{2,34},{34,2},{3,35},{35,3},{4,36},{36... | collective-permute-start | bytes 1966088 | tf_op jit(solution)/shard_map/ppermute | solution.py:299
  88.5 6.2 %copy-start.5 = (bf16[1,2,128,512]{3,2,1,0:T(8,128)(2,1)S(1)}, bf16[1,2,128,512]{3,2,1,0:T(8,128)(2,1)}, u32[]{:S(2)}) copy-start(bf16[1,2,128,512]{3,2,1,0:T(8,128)(2,1)} %param.7) | copy-start | bytes 786436
  120.6 21.0 %all-to-all-start.3 = ((bf16[16,16,256]{2,1,0:T(8,128)(2,1)}), bf16[16,16,256]{2,1,0:T(8,128)(2,1)S(1)}, u32[]{:S(2)}, u32[]{:S(2)}) async-start(bf16[16,16,256]{2,1,0:T(8,128)(2,1)} %plane.1), calls=%async_computation.3 | async-start | bytes 262144 | tf_op jit(solution)/shard_map/all_to_all | solution.py:323
  149.7 13.1 %all-to-all-start.4 = ((f32[8,8,256]{2,1,0:T(8,128)}), f32[8,8,256]{2,1,0:T(8,128)S(1)}, u32[]{:S(2)}, u32[]{:S(2)}) async-start(f32[8,8,256]{2,1,0:T(8,128)} %broadcast_in_dim.8), calls=%async_computation.4 | async-start | bytes 131072 | tf_op jit(solution)/shard_map/all_to_all | solution.py:334

commit v6 on v5

--- a/solution.py
+++ b/solution.py
@@ -15,6 +15,7 @@
 XY = ("x", "y")
 ZZ = ("zl", "zh")
 EXTRA = 16
+OWN, LAST, MIDDLE = 50, 20, 20
 
 
 def vmem():
@@ -73,9 +74,14 @@
     return lax.dot_general(hidden, down_t, (((1,), (1,)), ((), ())), preferred_element_type=F32)
 
 
-def own_kernel(where_ref, mine_ref, other_ref, own_ref, out_mine_ref, out_other_ref, mine, other, mine_sems, other_sems):
-    copies = fetches(where_ref, mine_ref, mine, mine_sems, False)
-    copies += fetches(where_ref, other_ref, other, other_sems, False)
+def own_kernel(where_ref, mine_ref, other_ref, own_ref, *refs):
+    out_mine_ref, out_other_ref, near_mine, near_other, far_mine, far_other, sems = refs
+    held = ((mine_ref, near_mine, False), (other_ref, near_other, False), (mine_ref, far_mine, True), (other_ref, far_other, True))
+    copies = [
+        copy
+        for at, (ref, block_ref, far) in enumerate(held)
+        for copy in fetches(where_ref, ref, block_ref, sems.at[at], far)
+    ]
     for copy in copies:
         copy.start()
     for copy in copies:
@@ -85,7 +91,7 @@
     nothing = jnp.zeros_like(down_t)
 
     def body(columns, rest, down_t):
-        for ref, out_ref in ((mine, out_mine_ref), (other, out_other_ref)):
+        for ref, out_ref in ((near_mine, out_mine_ref), (near_other, out_other_ref)):
             hidden = ref[...]
             out_ref[:, columns] = jnp.dot(hidden, value, preferred_element_type=F32)
             out_ref[:, rest] = jnp.zeros((hidden.shape[0], half), F32)
@@ -100,36 +106,20 @@
         body(slice(half, 2 * half), slice(0, half), jnp.concatenate([nothing, down_t], axis=0))
 
 
-def last_kernel(keep, where_ref, hidden_ref, weight_ref, sent_ref, before_ref, out_ref, *refs):
-    if keep:
-        kept_ref, far, near, far_sems, near_sems, passed_ref, passed_sem, keep_sem = refs
-    else:
-        far, near, far_sems, near_sems, passed_ref, passed_sem = refs
-    far_copies = fetches(where_ref, hidden_ref, far, far_sems, True)
-    near_copies = fetches(where_ref, hidden_ref, near, near_sems, False)
-    near_copies.append(pltpu.make_async_copy(sent_ref, passed_ref, passed_sem))
-    for copy in far_copies + near_copies:
-        copy.start()
-    if keep:
-        whole = pltpu.make_async_copy(hidden_ref, kept_ref, keep_sem)
-        whole.start()
+def last_kernel(where_ref, near_ref, far_ref, weight_ref, passed_ref, before_ref, out_ref):
     features = weight_ref.shape[2]
     half = passed_ref.shape[2]
     value, down_t = unpacked(weight_ref)
-    for copy in far_copies:
-        copy.wait()
-    hidden = far[...]
-    out_ref[:, :features] = before_ref[:, :features] + jnp.dot(hidden, value, preferred_element_type=F32)
-    out_ref[:, features:] = before_ref[:, features:] + low_part(hidden, down_t)
-    for copy in near_copies:
-        copy.wait()
+    far = far_ref[...]
+    out_ref[:, :features] = before_ref[:, :features] + jnp.dot(far, value, preferred_element_type=F32)
+    out_ref[:, features:] = before_ref[:, features:] + low_part(far, down_t)
     value, down_t = unpacked(passed_ref)
     nothing = jnp.zeros_like(down_t)
 
     def body(columns, down_t):
-        hidden = near[...]
-        out_ref[:, columns] += jnp.dot(hidden, value, preferred_element_type=F32)
-        out_ref[:, features:] += low_part(hidden, down_t)
+        near = near_ref[...]
+        out_ref[:, columns] += jnp.dot(near, value, preferred_element_type=F32)
+        out_ref[:, features:] += low_part(near, down_t)
 
     @pl.when(where_ref[2] == 0)
     def _():
@@ -139,45 +129,35 @@
     def _():
         body(slice(0, half), jnp.concatenate([down_t, nothing], axis=0))
 
-    if keep:
-        whole.wait()
-
 
 def smem():
     return pl.BlockSpec(memory_space=pltpu.SMEM)
 
 
-def blocks(tokens, width, count):
-    return [pltpu.VMEM((tokens, width // 4), BF16)] * count + [pltpu.SemaphoreType.DMA((X * Y,))] * count
-
-
 def own_forward(where, mine, other, own):
     tokens, width = mine.shape
-    out = (tokens, 2 * own.shape[2] + LANES)
+    out = jax.ShapeDtypeStruct((tokens, 2 * own.shape[2] + LANES), F32)
+    block = jax.ShapeDtypeStruct((tokens, width // 4), BF16)
     return pl.pallas_call(
         own_kernel,
         in_specs=[smem(), anywhere(), anywhere(), vmem()],
-        out_specs=[vmem()] * 2,
-        out_shape=[jax.ShapeDtypeStruct(out, F32)] * 2,
-        scratch_shapes=blocks(tokens, width, 2),
-        compiler_params=params(),
+        out_specs=[vmem()] * 6,
+        out_shape=[out] * 2 + [block] * 4,
+        scratch_shapes=[pltpu.SemaphoreType.DMA((4, X * Y))],
+        compiler_params=params(OWN),
         name="own",
     )(where, mine, other, own)
 
 
-def last_forward(where, hidden, weights, passed, before, keep):
-    tokens, width = hidden.shape
-    out = jax.ShapeDtypeStruct(before.shape, F32)
-    scratch = blocks(tokens, width, 2) + [pltpu.VMEM(passed.shape, BF16), pltpu.SemaphoreType.DMA]
+def last_forward(where, near, far, weights, passed, before):
     return pl.pallas_call(
-        lambda *refs: last_kernel(keep, *refs),
-        in_specs=[smem(), anywhere(), vmem(), anywhere(), vmem()],
-        out_specs=[vmem(), vmem()] if keep else vmem(),
-        out_shape=[out, jax.ShapeDtypeStruct(hidden.shape, BF16)] if keep else out,
-        scratch_shapes=scratch + [pltpu.SemaphoreType.DMA] if keep else scratch,
-        compiler_params=params(48),
+        last_kernel,
+        in_specs=[smem()] + [vmem()] * 5,
+        out_specs=vmem(),
+        out_shape=jax.ShapeDtypeStruct(before.shape, F32),
+        compiler_params=params(LAST),
         name="last",
-    )(where, hidden, weights, passed, before)
+    )(where, near, far, weights, passed, before)
 
 
 def plane_gather(w):
@@ -294,10 +274,10 @@
     weights_far, near = lax.optimization_barrier((weights_far, near))
     far = plane_gather(weights_far)
     passed = lax.ppermute(near, "zl", [(a, a ^ 1) for a in range(ZL)])
-    before_mine, before_other = own_forward(where, hidden, other, near)
-    part_other = last_forward(where, other, far, passed, before_other, False)
+    before_mine, before_other, near_mine, near_other, far_mine, far_other = own_forward(where, hidden, other, near)
+    part_other = last_forward(where, near_other, far_other, far, passed, before_other)
     from_other = lax.ppermute(part_other, "core", swap_core)
-    part_mine, kept = last_forward(where, hidden, far, passed, before_mine, True)
+    part_mine = last_forward(where, near_mine, far_mine, far, passed, before_mine)
 
     read = readout.reshape(tokens, features)
     mask = response.reshape(tokens, 1).astype(F32)
@@ -308,9 +288,9 @@
         in_specs=[vmem()] * 6,
         out_specs=vmem(),
         out_shape=jax.ShapeDtypeStruct((X * Y, ZH * rank + EXTRA, wide), BF16),
-        compiler_params=params(),
+        compiler_params=params(MIDDLE),
         name="middle",
-    )(part_mine, from_other, kept, read, mask, up)
+    )(part_mine, from_other, hidden, read, mask, up)
     got = lax.all_to_all(sends, XY, 0, 0)
     along = pl.pallas_call(
         plane_kernel,

time: 165 us -> 164 us (level)
  local copies, waits for them, and re-layouts: 8.39 us -> 14.1 us
  waiting for transfers between devices: 58.3 us -> 54.5 us
  Pallas kernels: 19.7 us -> 16.2 us
    unnamed x17 -> x29, local copies, waits for them, and re-layouts: 3.85 us -> 9.45 us
    pallas_call x2, Pallas kernels: 11.2 us -> 7.02 us  [last_forward(): pl.pallas_call(last_kernel, in_specs=[smem()] + [vmem()] * 5, out_specs=v...]
    ppermute x1, waiting for transfers between devices: 20.6 us -> 16.8 us  [shards(): passed = lax.ppermute(near, 'zl', [(a, a ^ 1) for a in range(ZL)])]
    pallas_call x1, Pallas kernels: 3.78 us -> 6.85 us  [own_forward(): pl.pallas_call(own_kernel, in_specs=[smem(), anywhere(), anywhere(), vmem...]
    pallas_call x1, Pallas kernels: 3.74 us -> 1.36 us  [shards(): pl.pallas_call(middle_kernel, in_specs=[vmem()] * 6, out_specs=vmem(), ou...]
where the time goes in v6:
time: 164 us; the launch traced here: 163 us
  waiting for transfers between devices  54.5 us (33%)
  starting transfers between devices  46.9 us (29%)
  blocking collectives  27.3 us (17%)
  Pallas kernels  16.2 us (10%)
  local copies, waits for them, and re-layouts  14.1 us (9%)
  between operations  2.75 us (2%)
    all_to_all x1, blocking collectives, shards(): got = lax.all_to_all(sends, XY, 0, 0)  21.2 us
    ppermute x1, waiting for transfers between devices, shards(): passed = lax.ppermute(near, 'zl', [(a, a ^ 1) for a in range(ZL)])  16.8 us
    ppermute x1, waiting for transfers between devices, shards(): weights_far = lax.ppermute(weights, axes, mirror)  13.5 us
    all_to_all x1, waiting for transfers between devices, shards(): got = lax.all_to_all(along, ZZ, 0, 0)  13.3 us
    all_to_all x2, starting transfers between devices, plane_gather(): lax.all_to_all(jnp.broadcast_to(w[None], (X * Y,) + w.shape), XY, 0, 0)  10.2 us
    unnamed x29, local copies, waits for them, and re-layouts  9.45 us
    all_to_all x1, waiting for transfers between devices, shards(): lax.all_to_all(jnp.broadcast_to(summed[None, :rows], (ZL, rows, wide)), '...  9.1 us
    ppermute x1, starting transfers between devices, shards(): other = lax.ppermute(hidden, 'core', swap_core)  8.92 us
  transfers between devices with their start and end apart: 8, of which 5 were waited for; matrix products, arithmetic and copies ran while one was open for 3% of the time, Pallas kernels for 6%

profile of v6, /device:TPU:1, one launch (start us, length us, event | category | flops | bytes accessed | tf_op | source)
XLA Modules:
  0.0 163.0 jit_solution(12292724768159236368)
XLA Ops:
  0.6 8.9 %collective-permute-start = (bf16[256,8192]{1,0:T(8,128)(2,1)}, bf16[256,8192]{1,0:T(8,128)(2,1)}, u32[]{:S(2)}, u32[]{:S(2)}) collective-permute-start(bf16[256,8192]{1,0:T(8,128)(2,1)} %bitcast.19), channel_id=1, source_target_pairs={{0,32},{32,0},{1,33},{33,1},{2,34},{34,2},{3,35},{35,3},{4,36},{36... | collective-permute-start | bytes 12582920 | tf_op jit(solution)/shard_map/ppermute | solution.py:272
  9.6 0.7 constant_dynamic-slice_fusion.1
  10.4 1.2 broadcast_in_dim.6
  11.5 3.7 %all-to-all-start = ((bf16[16,144,256]{2,1,0:T(8,128)(2,1)}), bf16[16,144,256]{2,1,0:T(8,128)(2,1)S(1)}, u32[]{:S(2)}, u32[]{:S(2)}) async-start(bf16[16,144,256]{2,1,0:T(8,128)(2,1)} %broadcast_in_dim.6), calls=%async_computation | async-start | bytes 2359296 | tf_op jit(solution)/shard_map/all_to_all | solution.py:164
  15.2 8.8 %collective-permute-start.1 = (bf16[144,512]{1,0:T(8,128)(2,1)S(1)}, bf16[144,512]{1,0:T(8,128)(2,1)S(1)}, u32[]{:S(2)}, u32[]{:S(2)}) collective-permute-start(bf16[144,512]{1,0:T(8,128)(2,1)S(1)} %pad_maximum_fusion), channel_id=1, source_target_pairs={{0,452},{1,453},{2,454},{3,455},{4,448},{5,449},{6,450},{7,451},{8... | collective-permute-start | bytes 442376 | tf_op jit(solution)/shard_map/ppermute | solution.py:269
  24.1 13.5 %collective-permute-done.1 = bf16[144,512]{1,0:T(8,128)(2,1)S(1)} collective-permute-done((bf16[144,512]{1,0:T(8,128)(2,1)S(1)}, bf16[144,512]{1,0:T(8,128)(2,1)S(1)}, u32[]{:S(2)}, u32[]{:S(2)}) %collective-permute-start.1) | collective-permute-done | bytes 147488 | tf_op jit(solution)/shard_map/ppermute | solution.py:269
  37.5 1.9 %broadcast_in_dim.7 = bf16[16,144,512]{2,1,0:T(8,128)(2,1)} broadcast(bf16[144,512]{1,0:T(8,128)(2,1)S(1)} %collective-permute-done.1), dimensions={1,2} | broadcast | bytes 2506752 | tf_op jit(solution)/shard_map/broadcast_in_dim | solution.py:164
  39.4 6.5 %all-to-all-start.1 = ((bf16[16,144,512]{2,1,0:T(8,128)(2,1)}), bf16[16,144,512]{2,1,0:T(8,128)(2,1)S(1)}, u32[]{:S(2)}, u32[]{:S(2)}) async-start(bf16[16,144,512]{2,1,0:T(8,128)(2,1)} %broadcast_in_dim.7), calls=%async_computation.1 | async-start | bytes 4718592 | tf_op jit(solution)/shard_map/all_to_all | solution.py:164
  46.0 1.9 %collective-permute-start.2 = (bf16[16,144,256]{2,1,0:T(8,128)(2,1)}, bf16[16,144,256]{2,1,0:T(8,128)(2,1)}, u32[]{:S(2)}, u32[]{:S(2)}) collective-permute-start(bf16[16,144,256]{2,1,0:T(8,128)(2,1)} %copy-done.11), channel_id=1, source_target_pairs={{0,64},{64,0},{128,192},{192,128},{256,320},{320,256},{384,448},{4... | collective-permute-start | bytes 3538952 | tf_op jit(solution)/shard_map/ppermute | solution.py:276
  48.0 6.8 %own.1 = (f32[256,640]{1,0:T(8,128)S(1)}, f32[256,640]{1,0:T(8,128)S(1)}, bf16[256,2048]{1,0:T(8,128)(2,1)S(1)}, bf16[256,2048]{1,0:T(8,128)(2,1)S(1)}, bf16[256...) custom-call(s32[3]{0:T(128)S(1)} %pad_add_fusion.where_ref, bf16[256,8192]{1,0:T(8,128)(2,1)} %bitcast.20, ...), custom_call_target="tpu_custom_call" | custom-call | tf_op jit(solution)/shard_map/own/pallas_call | solution.py:141
  54.9 1.0 copy-done.2
  55.9 1.0 copy-done.5
  56.8 0.8 copy-done.8
  57.7 16.8 %collective-permute-done.2.passed_ref = bf16[16,144,256]{2,1,0:T(8,128)(2,1)} collective-permute-done((bf16[16,144,256]{2,1,0:T(8,128)(2,1)}, bf16[16,144,256]{2,1,0:T(8,128)(2,1)}, u32[]{:S(2)}, u32[]{:S(2)}) %collective-permute-start.2) | collective-permute-done | bytes 1179680 | tf_op jit(solution)/shard_map/ppermute | solution.py:276
  74.5 1.8 %all-to-all-done.1.weight_ref = bf16[16,144,512]{2,1,0:T(8,128)(2,1)S(1)} async-done(((bf16[16,144,512]{2,1,0:T(8,128)(2,1)}), bf16[16,144,512]{2,1,0:T(8,128)(2,1)S(1)}, u32[]{:S(2)}, u32[]{:S(2)}) %all-to-all-start.1) | async-done | bytes 2359328 | tf_op jit(solution)/shard_map/all_to_all | solution.py:164
  76.2 1.2 copy-done.6
  77.5 1.2 copy-done.7
  78.7 3.9 %last.3 = f32[256,640]{1,0:T(8,128)} custom-call(s32[3]{0:T(128)S(1)} %pad_add_fusion.where_ref, bf16[256,2048]{1,0:T(8,128)(2,1)S(1)} %copy-done.6, bf16[256,2048]{1,0:T(8,128)(2,1)S(1)} %copy-done.7, bf16[16,144,512]{2,1,0:T(8,128)(2,1)S(1)} %all-to-all-done.1.weight_ref, bf16[16,144,256]{2,1,0:T(8,128)(2,1)} %collective-permute-done.2.passed_ref, ...), custom_call_target="tpu_custom_call" | custom-call | tf_op jit(solution)/shard_map/last/pallas_call | solution.py:153
  82.6 6.1 %collective-permute-start.3 = (f32[256,640]{1,0:T(8,128)}, f32[256,640]{1,0:T(8,128)S(1)}, u32[]{:S(2)}, u32[]{:S(2)}) collective-permute-start(f32[256,640]{1,0:T(8,128)} %last.3), channel_id=1, source_target_pairs={{0,32},{32,0},{1,33},{33,1},{2,34},{34,2},{3,35},{35,3},{4,36},{36... | collective-permute-start | bytes 1966088 | tf_op jit(solution)/shard_map/ppermute | solution.py:279
  88.8 1.2 copy-done.3
  90.1 1.2 copy-done.4
  91.3 1.1 copy-done.9
  92.4 3.1 %last.2.mine_ref = f32[256,640]{1,0:T(8,128)S(1)} custom-call(s32[3]{0:T(128)S(1)} %pad_add_fusion.where_ref, bf16[256,2048]{1,0:T(8,128)(2,1)S(1)} %copy-done.3, bf16[256,2048]{1,0:T(8,128)(2,1)S(1)} %copy-done.4, bf16[16,144,512]{2,1,0:T(8,128)(2,1)S(1)} %all-to-all-done.1.weight_ref, bf16[16,144,256]{2,1,0:T(8,128)(2,1)} %collective-permute-done.2.passed_ref, ...), custom_call_target="tpu_custom_call" | custom-call | tf_op jit(solution)/shard_map/last/pallas_call | solution.py:153
  95.6 1.4 middle.1
  96.9 21.2 %all_to_all.25.got_ref = bf16[16,144,256]{2,1,0:T(8,128)(2,1)S(1)} all-to-all(bf16[16,144,256]{2,1,0:T(8,128)(2,1)S(1)} %middle.1), channel_id=1, replica_groups=mesh['zl'=8,'core'=2,'x'=4,'zh'=2,'y'=4] {'x','y'}, dimensions={0} | all-to-all | bytes 2359296 | tf_op jit(solution)/shard_map/all_to_all | solution.py:294
  118.1 0.9 plane.1
  119.0 7.6 %all-to-all-start.3 = ((bf16[16,16,256]{2,1,0:T(8,128)(2,1)}), bf16[16,16,256]{2,1,0:T(8,128)(2,1)S(1)}, u32[]{:S(2)}, u32[]{:S(2)}) async-start(bf16[16,16,256]{2,1,0:T(8,128)(2,1)} %plane.1), calls=%async_computation.3 | async-start | bytes 262144 | tf_op jit(solution)/shard_map/all_to_all | solution.py:303
  126.6 13.3 %all-to-all-done.3.got_ref = bf16[16,16,256]{2,1,0:T(8,128)(2,1)S(1)} async-done(((bf16[16,16,256]{2,1,0:T(8,128)(2,1)}), bf16[16,16,256]{2,1,0:T(8,128)(2,1)S(1)}, u32[]{:S(2)}, u32[]{:S(2)}) %all-to-all-start.3) | async-done | bytes 131104 | tf_op jit(solution)/shard_map/all_to_all | solution.py:303
  140.1 6.1 %psum.7 = f32[16,256]{1,0:T(8,128)S(1)} all-reduce(f32[16,256]{1,0:T(8,128)S(1)} %get-tuple-element.24), channel_id=1, replica_groups=mesh['zl'=8,'core'=2,'x'=4,'zh'=2,'y'=4] {'core'}, use_global_device_ids=true, to_apply=%region_0.1 | all-reduce | flops 4096 | bytes 32768 | tf_op jit(solution)/shard_map/psum | solution.py:312
  147.5 0.6 broadcast_in_dim.8
  148.1 3.4 %all-to-all-start.4 = ((f32[8,8,256]{2,1,0:T(8,128)}), f32[8,8,256]{2,1,0:T(8,128)S(1)}, u32[]{:S(2)}, u32[]{:S(2)}) async-start(f32[8,8,256]{2,1,0:T(8,128)} %broadcast_in_dim.8), calls=%async_computation.4 | async-start | bytes 131072 | tf_op jit(solution)/shard_map/all_to_all | solution.py:314
  152.2 9.1 %all-to-all-done.4 = f32[8,8,256]{2,1,0:T(8,128)S(1)} async-done(((f32[8,8,256]{2,1,0:T(8,128)}), f32[8,8,256]{2,1,0:T(8,128)S(1)}, u32[]{:S(2)}, u32[]{:S(2)}) %all-to-all-start.4) | async-done | bytes 65568 | tf_op jit(solution)/shard_map/all_to_all | solution.py:314
  (37 shorter events, 2.2 us)
Async XLA Ops:
  0.6 9.7 %copy-start = (bf16[256,512]{1,0:T(8,128)(2,1)S(1)}, bf16[256,512]{1,0:T(8,128)(2,1)}, u32[]{:S(2)}) copy-start(bf16[256,512]{1,0:T(8,128)(2,1)} %param.9) | copy-start | bytes 786436
  0.6 47.3 %collective-permute-start = (bf16[256,8192]{1,0:T(8,128)(2,1)}, bf16[256,8192]{1,0:T(8,128)(2,1)}, u32[]{:S(2)}, u32[]{:S(2)}) collective-permute-start(bf16[256,8192]{1,0:T(8,128)(2,1)} %bitcast.19), channel_id=1, source_target_pairs={{0,32},{32,0},{1,33},{33,1},{2,34},{34,2},{3,35},{35,3},{4,36},{36... | collective-permute-start | bytes 12582920 | tf_op jit(solution)/shard_map/ppermute | solution.py:272
  11.5 26.0 %all-to-all-start = ((bf16[16,144,256]{2,1,0:T(8,128)(2,1)}), bf16[16,144,256]{2,1,0:T(8,128)(2,1)S(1)}, u32[]{:S(2)}, u32[]{:S(2)}) async-start(bf16[16,144,256]{2,1,0:T(8,128)(2,1)} %broadcast_in_dim.6), calls=%async_computation | async-start | bytes 2359296 | tf_op jit(solution)/shard_map/all_to_all | solution.py:164
  15.2 22.3 %collective-permute-start.1 = (bf16[144,512]{1,0:T(8,128)(2,1)S(1)}, bf16[144,512]{1,0:T(8,128)(2,1)S(1)}, u32[]{:S(2)}, u32[]{:S(2)}) collective-permute-start(bf16[144,512]{1,0:T(8,128)(2,1)S(1)} %pad_maximum_fusion), channel_id=1, source_target_pairs={{0,452},{1,453},{2,454},{3,455},{4,448},{5,449},{6,450},{7,451},{8... | collective-permute-start | bytes 442376 | tf_op jit(solution)/shard_map/ppermute | solution.py:269
  37.5 1.9 %copy-start.11 = (bf16[16,144,256]{2,1,0:T(8,128)(2,1)}, bf16[16,144,256]{2,1,0:T(8,128)(2,1)S(1)}, u32[]{:S(2)}) copy-start(bf16[16,144,256]{2,1,0:T(8,128)(2,1)S(1)} %all-to-all-done.own_ref) | copy-start | bytes 3538948
  39.4 36.8 %all-to-all-start.1 = ((bf16[16,144,512]{2,1,0:T(8,128)(2,1)}), bf16[16,144,512]{2,1,0:T(8,128)(2,1)S(1)}, u32[]{:S(2)}, u32[]{:S(2)}) async-start(bf16[16,144,512]{2,1,0:T(8,128)(2,1)} %broadcast_in_dim.7), calls=%async_computation.1 | async-start | bytes 4718592 | tf_op jit(solution)/shard_map/all_to_all | solution.py:164
  46.0 28.5 %collective-permute-start.2 = (bf16[16,144,256]{2,1,0:T(8,128)(2,1)}, bf16[16,144,256]{2,1,0:T(8,128)(2,1)}, u32[]{:S(2)}, u32[]{:S(2)}) collective-permute-start(bf16[16,144,256]{2,1,0:T(8,128)(2,1)} %copy-done.11), channel_id=1, source_target_pairs={{0,64},{64,0},{128,192},{192,128},{256,320},{320,256},{384,448},{4... | collective-permute-start | bytes 3538952 | tf_op jit(solution)/shard_map/ppermute | solution.py:276
  54.8 1.0 copy-start.2
  55.9 1.0 copy-start.5
  56.8 0.8 copy-start.8
  76.2 1.2 copy-start.6
  77.5 1.2 copy-start.7
  78.7 10.0 %copy-start.13 = (s32[1,2,128]{2,1,0:T(2,128)S(1)}, s32[1,2,128]{2,1,0:T(2,128)}, u32[]{:S(2)}) copy-start(s32[1,2,128]{2,1,0:T(2,128)} %param.8) | copy-start | bytes 3076
  78.7 10.1 %copy-start.12 = (bf16[64,512]{1,0:T(8,128)(2,1)S(1)}, bf16[64,512]{1,0:T(8,128)(2,1)}, u32[]{:S(2)}) copy-start(bf16[64,512]{1,0:T(8,128)(2,1)} %param.11) | copy-start | bytes 196612
  82.6 13.0 %collective-permute-start.3 = (f32[256,640]{1,0:T(8,128)}, f32[256,640]{1,0:T(8,128)S(1)}, u32[]{:S(2)}, u32[]{:S(2)}) collective-permute-start(f32[256,640]{1,0:T(8,128)} %last.3), channel_id=1, source_target_pairs={{0,32},{32,0},{1,33},{33,1},{2,34},{34,2},{3,35},{35,3},{4,36},{36... | collective-permute-start | bytes 1966088 | tf_op jit(solution)/shard_map/ppermute | solution.py:279
  88.8 1.2 copy-start.3
  90.1 1.2 copy-start.4
  91.3 1.1 copy-start.9
  92.4 3.2 %copy-start.1 = (bf16[1,2,128,8192]{3,2,1,0:T(8,128)(2,1)S(1)}, bf16[1,2,128,8192]{3,2,1,0:T(8,128)(2,1)}, u32[]{:S(2)}) copy-start(bf16[1,2,128,8192]{3,2,1,0:T(8,128)(2,1)} %param.6) | copy-start | bytes 12582916
  92.4 3.2 %copy-start.10 = (bf16[1,2,128,512]{3,2,1,0:T(8,128)(2,1)S(1)}, bf16[1,2,128,512]{3,2,1,0:T(8,128)(2,1)}, u32[]{:S(2)}) copy-start(bf16[1,2,128,512]{3,2,1,0:T(8,128)(2,1)} %param.7) | copy-start | bytes 786436
  119.0 21.0 %all-to-all-start.3 = ((bf16[16,16,256]{2,1,0:T(8,128)(2,1)}), bf16[16,16,256]{2,1,0:T(8,128)(2,1)S(1)}, u32[]{:S(2)}, u32[]{:S(2)}) async-start(bf16[16,16,256]{2,1,0:T(8,128)(2,1)} %plane.1), calls=%async_computation.3 | async-start | bytes 262144 | tf_op jit(solution)/shard_map/all_to_all | solution.py:303
  148.1 13.1 %all-to-all-start.4 = ((f32[8,8,256]{2,1,0:T(8,128)}), f32[8,8,256]{2,1,0:T(8,128)S(1)}, u32[]{:S(2)}, u32[]{:S(2)}) async-start(f32[8,8,256]{2,1,0:T(8,128)} %broadcast_in_dim.8), calls=%async_computation.4 | async-start | bytes 131072 | tf_op jit(solution)/shard_map/all_to_all | solution.py:314

commit v7 on v6

--- a/solution.py
+++ b/solution.py
@@ -15,7 +15,7 @@
 XY = ("x", "y")
 ZZ = ("zl", "zh")
 EXTRA = 16
-OWN, LAST, MIDDLE = 50, 20, 20
+OWN, PASSED, LAST, MIDDLE = 50, 20, 20, 20
 
 
 def vmem():
@@ -106,28 +106,36 @@
         body(slice(half, 2 * half), slice(0, half), jnp.concatenate([nothing, down_t], axis=0))
 
 
-def last_kernel(where_ref, near_ref, far_ref, weight_ref, passed_ref, before_ref, out_ref):
+def passed_kernel(where_ref, mine_ref, other_ref, passed_ref, old_mine_ref, old_other_ref, new_mine_ref, new_other_ref):
+    half = passed_ref.shape[2]
+    value, down_t = unpacked(passed_ref)
+    nothing = jnp.zeros_like(down_t)
+
+    def body(columns, rest, down_t):
+        for near_ref, old_ref, new_ref in (
+            (mine_ref, old_mine_ref, new_mine_ref),
+            (other_ref, old_other_ref, new_other_ref),
+        ):
+            near = near_ref[...]
+            new_ref[:, columns] = old_ref[:, columns] + jnp.dot(near, value, preferred_element_type=F32)
+            new_ref[:, rest] = old_ref[:, rest]
+            new_ref[:, 2 * half :] = old_ref[:, 2 * half :] + low_part(near, down_t)
+
+    @pl.when(where_ref[2] == 0)
+    def _():
+        body(slice(half, 2 * half), slice(0, half), jnp.concatenate([nothing, down_t], axis=0))
+
+    @pl.when(where_ref[2] != 0)
+    def _():
+        body(slice(0, half), slice(half, 2 * half), jnp.concatenate([down_t, nothing], axis=0))
+
+
+def last_kernel(far_ref, weight_ref, before_ref, out_ref):
     features = weight_ref.shape[2]
-    half = passed_ref.shape[2]
     value, down_t = unpacked(weight_ref)
     far = far_ref[...]
     out_ref[:, :features] = before_ref[:, :features] + jnp.dot(far, value, preferred_element_type=F32)
     out_ref[:, features:] = before_ref[:, features:] + low_part(far, down_t)
-    value, down_t = unpacked(passed_ref)
-    nothing = jnp.zeros_like(down_t)
-
-    def body(columns, down_t):
-        near = near_ref[...]
-        out_ref[:, columns] += jnp.dot(near, value, preferred_element_type=F32)
-        out_ref[:, features:] += low_part(near, down_t)
-
-    @pl.when(where_ref[2] == 0)
-    def _():
-        body(slice(half, features), jnp.concatenate([nothing, down_t], axis=0))
-
-    @pl.when(where_ref[2] != 0)
-    def _():
-        body(slice(0, half), jnp.concatenate([down_t, nothing], axis=0))
 
 
 def smem():
@@ -149,15 +157,26 @@
     )(where, mine, other, own)
 
 
-def last_forward(where, near, far, weights, passed, before):
+def passed_forward(where, near_mine, near_other, passed, old_mine, old_other):
+    return pl.pallas_call(
+        passed_kernel,
+        in_specs=[smem()] + [vmem()] * 5,
+        out_specs=[vmem()] * 2,
+        out_shape=[jax.ShapeDtypeStruct(old_mine.shape, F32)] * 2,
+        compiler_params=params(PASSED),
+        name="passed",
+    )(where, near_mine, near_other, passed, old_mine, old_other)
+
+
+def last_forward(far, weights, before):
     return pl.pallas_call(
         last_kernel,
-        in_specs=[smem()] + [vmem()] * 5,
+        in_specs=[vmem()] * 3,
         out_specs=vmem(),
         out_shape=jax.ShapeDtypeStruct(before.shape, F32),
         compiler_params=params(LAST),
         name="last",
-    )(where, near, far, weights, passed, before)
+    )(far, weights, before)
 
 
 def plane_gather(w):
@@ -275,9 +294,10 @@
     far = plane_gather(weights_far)
     passed = lax.ppermute(near, "zl", [(a, a ^ 1) for a in range(ZL)])
     before_mine, before_other, near_mine, near_other, far_mine, far_other = own_forward(where, hidden, other, near)
-    part_other = last_forward(where, near_other, far_other, far, passed, before_other)
+    before_mine, before_other = passed_forward(where, near_mine, near_other, passed, before_mine, before_other)
+    part_other = last_forward(far_other, far, before_other)
     from_other = lax.ppermute(part_other, "core", swap_core)
-    part_mine = last_forward(where, near_mine, far_mine, far, passed, before_mine)
+    part_mine = last_forward(far_mine, far, before_mine)
 
     read = readout.reshape(tokens, features)
     mask = response.reshape(tokens, 1).astype(F32)

time: 164 us -> 163 us (level)
  local copies, waits for them, and re-layouts: 14.1 us -> 10.8 us
  blocking collectives: 27.3 us -> 30.2 us
    unnamed x29 -> x21, local copies, waits for them, and re-layouts: 9.45 us -> 6.24 us
    all_to_all x1, blocking collectives: 21.2 us -> 24.1 us  [shards(): got = lax.all_to_all(sends, XY, 0, 0)]
    ppermute x1, waiting for transfers between devices: 16.8 us -> 19.6 us  [shards(): passed = lax.ppermute(near, 'zl', [(a, a ^ 1) for a in range(ZL)])]
    all_to_all x2, waiting for transfers between devices: 1.78 us -> 0.01 us  [plane_gather(): lax.all_to_all(jnp.broadcast_to(w[None], (X * Y,) + w.shape), XY, 0, 0)]
    ppermute x1, starting transfers between devices: 6.06 us -> 4.35 us  [shards(): from_other = lax.ppermute(part_other, 'core', swap_core)]
    pallas_call x2 -> x3, Pallas kernels: 7.02 us -> 5.45 us  [the longest x2 2.82 us: last_forward(): pl.pallas_call(last_kernel, in_specs=[vmem()] * 3, out_specs=vmem(), out_...]
  transfers between devices with their start and end apart: 8 -> 8, of which waited for: 5 -> 4; matrix products, arithmetic and copies ran while one was open for 3% -> 3% of each run, Pallas kernels for 6% -> 6%
where the time goes in v7:
time: 163 us; the launch traced here: 162 us
  waiting for transfers between devices  55.6 us (34%)
  starting transfers between devices  45.4 us (28%)
  blocking collectives  30.2 us (19%)
  Pallas kernels  15.7 us (10%)
  local copies, waits for them, and re-layouts  10.8 us (7%)
  between operations  2.74 us (2%)
    all_to_all x1, blocking collectives, shards(): got = lax.all_to_all(sends, XY, 0, 0)  24.1 us
    ppermute x1, waiting for transfers between devices, shards(): passed = lax.ppermute(near, 'zl', [(a, a ^ 1) for a in range(ZL)])  19.6 us
    ppermute x1, waiting for transfers between devices, shards(): weights_far = lax.ppermute(weights, axes, mirror)  13.5 us
    all_to_all x1, waiting for transfers between devices, shards(): got = lax.all_to_all(along, ZZ, 0, 0)  13.3 us
    all_to_all x2, starting transfers between devices, plane_gather(): lax.all_to_all(jnp.broadcast_to(w[None], (X * Y,) + w.shape), XY, 0, 0)  10.2 us
    all_to_all x1, waiting for transfers between devices, shards(): lax.all_to_all(jnp.broadcast_to(summed[None, :rows], (ZL, rows, wide)), '...  9.1 us
    ppermute x1, starting transfers between devices, shards(): other = lax.ppermute(hidden, 'core', swap_core)  8.92 us
    ppermute x1, starting transfers between devices, shards(): weights_far = lax.ppermute(weights, axes, mirror)  8.81 us
  transfers between devices with their start and end apart: 8, of which 4 were waited for; matrix products, arithmetic and copies ran while one was open for 3% of the time, Pallas kernels for 6%

profile of v7, /device:TPU:1, one launch (start us, length us, event | category | flops | bytes accessed | tf_op | source)
XLA Modules:
  0.0 161.7 jit_solution(3870684080317028156)
XLA Ops:
  0.6 8.9 %collective-permute-start = (bf16[256,8192]{1,0:T(8,128)(2,1)}, bf16[256,8192]{1,0:T(8,128)(2,1)}, u32[]{:S(2)}, u32[]{:S(2)}) collective-permute-start(bf16[256,8192]{1,0:T(8,128)(2,1)} %bitcast.19), channel_id=1, source_target_pairs={{0,32},{32,0},{1,33},{33,1},{2,34},{34,2},{3,35},{35,3},{4,36},{36... | collective-permute-start | bytes 12582920 | tf_op jit(solution)/shard_map/ppermute | solution.py:291
  9.6 0.7 constant_dynamic-slice_fusion.1
  10.4 1.1 broadcast_in_dim.6
  11.5 3.7 %all-to-all-start = ((bf16[16,144,256]{2,1,0:T(8,128)(2,1)}), bf16[16,144,256]{2,1,0:T(8,128)(2,1)S(1)}, u32[]{:S(2)}, u32[]{:S(2)}) async-start(bf16[16,144,256]{2,1,0:T(8,128)(2,1)} %broadcast_in_dim.6), calls=%async_computation | async-start | bytes 2359296 | tf_op jit(solution)/shard_map/all_to_all | solution.py:183
  15.2 8.8 %collective-permute-start.1 = (bf16[144,512]{1,0:T(8,128)(2,1)S(1)}, bf16[144,512]{1,0:T(8,128)(2,1)S(1)}, u32[]{:S(2)}, u32[]{:S(2)}) collective-permute-start(bf16[144,512]{1,0:T(8,128)(2,1)S(1)} %pad_maximum_fusion), channel_id=1, source_target_pairs={{0,452},{1,453},{2,454},{3,455},{4,448},{5,449},{6,450},{7,451},{8... | collective-permute-start | bytes 442376 | tf_op jit(solution)/shard_map/ppermute | solution.py:288
  24.0 13.5 %collective-permute-done.1 = bf16[144,512]{1,0:T(8,128)(2,1)S(1)} collective-permute-done((bf16[144,512]{1,0:T(8,128)(2,1)S(1)}, bf16[144,512]{1,0:T(8,128)(2,1)S(1)}, u32[]{:S(2)}, u32[]{:S(2)}) %collective-permute-start.1) | collective-permute-done | bytes 147488 | tf_op jit(solution)/shard_map/ppermute | solution.py:288
  37.5 1.8 %broadcast_in_dim.7 = bf16[16,144,512]{2,1,0:T(8,128)(2,1)} broadcast(bf16[144,512]{1,0:T(8,128)(2,1)S(1)} %collective-permute-done.1), dimensions={1,2} | broadcast | bytes 2506752 | tf_op jit(solution)/shard_map/broadcast_in_dim | solution.py:183
  39.3 6.5 %all-to-all-start.1 = ((bf16[16,144,512]{2,1,0:T(8,128)(2,1)}), bf16[16,144,512]{2,1,0:T(8,128)(2,1)S(1)}, u32[]{:S(2)}, u32[]{:S(2)}) async-start(bf16[16,144,512]{2,1,0:T(8,128)(2,1)} %broadcast_in_dim.7), calls=%async_computation.1 | async-start | bytes 4718592 | tf_op jit(solution)/shard_map/all_to_all | solution.py:183
  45.9 1.9 %collective-permute-start.2 = (bf16[16,144,256]{2,1,0:T(8,128)(2,1)}, bf16[16,144,256]{2,1,0:T(8,128)(2,1)}, u32[]{:S(2)}, u32[]{:S(2)}) collective-permute-start(bf16[16,144,256]{2,1,0:T(8,128)(2,1)} %copy-done.7), channel_id=1, source_target_pairs={{0,64},{64,0},{128,192},{192,128},{256,320},{320,256},{384,448},{4... | collective-permute-start | bytes 3538952 | tf_op jit(solution)/shard_map/ppermute | solution.py:295
  47.9 6.8 %own.1 = (f32[256,640]{1,0:T(8,128)S(1)}, f32[256,640]{1,0:T(8,128)S(1)}, bf16[256,2048]{1,0:T(8,128)(2,1)S(1)}, bf16[256,2048]{1,0:T(8,128)(2,1)S(1)}, bf16[256...) custom-call(s32[3]{0:T(128)S(1)} %pad_add_fusion.where_ref, bf16[256,8192]{1,0:T(8,128)(2,1)} %bitcast.20, ...), custom_call_target="tpu_custom_call" | custom-call | tf_op jit(solution)/shard_map/own/pallas_call | solution.py:149
  54.8 19.6 %collective-permute-done.2.passed_ref = bf16[16,144,256]{2,1,0:T(8,128)(2,1)} collective-permute-done((bf16[16,144,256]{2,1,0:T(8,128)(2,1)}, bf16[16,144,256]{2,1,0:T(8,128)(2,1)}, u32[]{:S(2)}, u32[]{:S(2)}) %collective-permute-start.2) | collective-permute-done | bytes 1179680 | tf_op jit(solution)/shard_map/ppermute | solution.py:295
  74.4 2.6 %passed.1 = (f32[256,640]{1,0:T(8,128)S(1)}, f32[256,640]{1,0:T(8,128)S(1)}) custom-call(s32[3]{0:T(128)S(1)} %pad_add_fusion.where_ref, bf16[256,2048]{1,0:T(8,128)(2,1)S(1)} %get-tuple-element.21.mine_ref, bf16[256,2048]{1,0:T(8,128)(2,1)S(1)} %get-tuple-element.22.other_ref, bf16[16,144,256]{2,1,0:T(8,128)(2,1)} %collective-permute-done.2.passed_ref, ...), custom_call_target="tpu_custom_call" | custom-call | tf_op jit(solution)/shard_map/passed/pallas_call | solution.py:161
  77.0 0.8 copy-done.4
  77.9 1.2 copy-done.3
  79.1 1.1 copy-done.5
  80.2 1.8 %last.3 = f32[256,640]{1,0:T(8,128)} custom-call(bf16[256,2048]{1,0:T(8,128)(2,1)S(1)} %copy-done.3, bf16[16,144,512]{2,1,0:T(8,128)(2,1)S(1)} %all-to-all-done.1.weight_ref, f32[256,640]{1,0:T(8,128)S(1)} %copy-done.5), custom_call_target="tpu_custom_call" | custom-call | tf_op jit(solution)/shard_map/last/pallas_call | solution.py:172
  82.0 4.3 %collective-permute-start.3 = (f32[256,640]{1,0:T(8,128)}, f32[256,640]{1,0:T(8,128)}, u32[]{:S(2)}, u32[]{:S(2)}) collective-permute-start(f32[256,640]{1,0:T(8,128)} %last.3), channel_id=1, source_target_pairs={{0,32},{32,0},{1,33},{33,1},{2,34},{34,2},{3,35},{35,3},{4,36},{36... | collective-permute-start | bytes 1966088 | tf_op jit(solution)/shard_map/ppermute | solution.py:299
  86.6 1.2 copy-done.2
  87.8 1.0 last.2.mine_ref
  88.8 1.2 copy-done.1
  90.0 2.4 %middle.1 = bf16[16,144,256]{2,1,0:T(8,128)(2,1)S(1)} custom-call(f32[256,640]{1,0:T(8,128)S(1)} %last.2.mine_ref, f32[256,640]{1,0:T(8,128)} %collective-permute-done.3.other_ref, bf16[256,8192]{1,0:T(8,128)(2,1)S(1)} %bitcast.21, bf16[256,512]{1,0:T(8,128)(2,1)S(1)} %bitcast.22, f32[256,1]{1,0:T(8,128)S(1)} %copy.12.mask_ref, bf16[128,512]{1,0:T(8,128)(2,1)S(1)} %pad.4.up_ref), custom_call_target="tpu_custom_call" | custom-call | tf_op jit(solution)/shard_map/middle/pallas_call | solution.py:306
  92.5 24.1 %all_to_all.25.got_ref = bf16[16,144,256]{2,1,0:T(8,128)(2,1)S(1)} all-to-all(bf16[16,144,256]{2,1,0:T(8,128)(2,1)S(1)} %middle.1), channel_id=1, replica_groups=mesh['zl'=8,'core'=2,'x'=4,'zh'=2,'y'=4] {'x','y'}, dimensions={0} | all-to-all | bytes 2359296 | tf_op jit(solution)/shard_map/all_to_all | solution.py:314
  116.6 0.9 plane.1
  117.4 7.8 %all-to-all-start.3 = ((bf16[16,16,256]{2,1,0:T(8,128)(2,1)}), bf16[16,16,256]{2,1,0:T(8,128)(2,1)S(1)}, u32[]{:S(2)}, u32[]{:S(2)}) async-start(bf16[16,16,256]{2,1,0:T(8,128)(2,1)} %plane.1), calls=%async_computation.3 | async-start | bytes 262144 | tf_op jit(solution)/shard_map/all_to_all | solution.py:323
  125.3 13.3 %all-to-all-done.3.got_ref = bf16[16,16,256]{2,1,0:T(8,128)(2,1)S(1)} async-done(((bf16[16,16,256]{2,1,0:T(8,128)(2,1)}), bf16[16,16,256]{2,1,0:T(8,128)(2,1)S(1)}, u32[]{:S(2)}, u32[]{:S(2)}) %all-to-all-start.3) | async-done | bytes 131104 | tf_op jit(solution)/shard_map/all_to_all | solution.py:323
  138.7 6.1 %psum.7 = f32[16,256]{1,0:T(8,128)S(1)} all-reduce(f32[16,256]{1,0:T(8,128)S(1)} %get-tuple-element.28), channel_id=1, replica_groups=mesh['zl'=8,'core'=2,'x'=4,'zh'=2,'y'=4] {'core'}, use_global_device_ids=true, to_apply=%region_0.1 | all-reduce | flops 4096 | bytes 32768 | tf_op jit(solution)/shard_map/psum | solution.py:332
  144.8 0.5 fusion.2
  146.1 0.6 broadcast_in_dim.8
  146.8 3.4 %all-to-all-start.4 = ((f32[8,8,256]{2,1,0:T(8,128)}), f32[8,8,256]{2,1,0:T(8,128)S(1)}, u32[]{:S(2)}, u32[]{:S(2)}) async-start(f32[8,8,256]{2,1,0:T(8,128)} %broadcast_in_dim.8), calls=%async_computation.4 | async-start | bytes 131072 | tf_op jit(solution)/shard_map/all_to_all | solution.py:334
  150.2 0.6 pad_maximum_fusion.1
  150.8 9.1 %all-to-all-done.4 = f32[8,8,256]{2,1,0:T(8,128)S(1)} async-done(((f32[8,8,256]{2,1,0:T(8,128)}), f32[8,8,256]{2,1,0:T(8,128)S(1)}, u32[]{:S(2)}, u32[]{:S(2)}) %all-to-all-start.4) | async-done | bytes 65568 | tf_op jit(solution)/shard_map/all_to_all | solution.py:334
  159.9 0.6 copy.17
  (30 shorter events, 0.5 us)
Async XLA Ops:
  0.6 9.7 %copy-start = (bf16[256,512]{1,0:T(8,128)(2,1)S(1)}, bf16[256,512]{1,0:T(8,128)(2,1)}, u32[]{:S(2)}) copy-start(bf16[256,512]{1,0:T(8,128)(2,1)} %param.9) | copy-start | bytes 786436
  0.6 47.3 %collective-permute-start = (bf16[256,8192]{1,0:T(8,128)(2,1)}, bf16[256,8192]{1,0:T(8,128)(2,1)}, u32[]{:S(2)}, u32[]{:S(2)}) collective-permute-start(bf16[256,8192]{1,0:T(8,128)(2,1)} %bitcast.19), channel_id=1, source_target_pairs={{0,32},{32,0},{1,33},{33,1},{2,34},{34,2},{3,35},{35,3},{4,36},{36... | collective-permute-start | bytes 12582920 | tf_op jit(solution)/shard_map/ppermute | solution.py:291
  11.5 26.0 %all-to-all-start = ((bf16[16,144,256]{2,1,0:T(8,128)(2,1)}), bf16[16,144,256]{2,1,0:T(8,128)(2,1)S(1)}, u32[]{:S(2)}, u32[]{:S(2)}) async-start(bf16[16,144,256]{2,1,0:T(8,128)(2,1)} %broadcast_in_dim.6), calls=%async_computation | async-start | bytes 2359296 | tf_op jit(solution)/shard_map/all_to_all | solution.py:183
  15.2 22.3 %collective-permute-start.1 = (bf16[144,512]{1,0:T(8,128)(2,1)S(1)}, bf16[144,512]{1,0:T(8,128)(2,1)S(1)}, u32[]{:S(2)}, u32[]{:S(2)}) collective-permute-start(bf16[144,512]{1,0:T(8,128)(2,1)S(1)} %pad_maximum_fusion), channel_id=1, source_target_pairs={{0,452},{1,453},{2,454},{3,455},{4,448},{5,449},{6,450},{7,451},{8... | collective-permute-start | bytes 442376 | tf_op jit(solution)/shard_map/ppermute | solution.py:288
  37.5 1.8 %copy-start.7 = (bf16[16,144,256]{2,1,0:T(8,128)(2,1)}, bf16[16,144,256]{2,1,0:T(8,128)(2,1)S(1)}, u32[]{:S(2)}) copy-start(bf16[16,144,256]{2,1,0:T(8,128)(2,1)S(1)} %all-to-all-done.own_ref) | copy-start | bytes 3538948
  39.3 38.5 %all-to-all-start.1 = ((bf16[16,144,512]{2,1,0:T(8,128)(2,1)}), bf16[16,144,512]{2,1,0:T(8,128)(2,1)S(1)}, u32[]{:S(2)}, u32[]{:S(2)}) async-start(bf16[16,144,512]{2,1,0:T(8,128)(2,1)} %broadcast_in_dim.7), calls=%async_computation.1 | async-start | bytes 4718592 | tf_op jit(solution)/shard_map/all_to_all | solution.py:183
  45.9 28.5 %collective-permute-start.2 = (bf16[16,144,256]{2,1,0:T(8,128)(2,1)}, bf16[16,144,256]{2,1,0:T(8,128)(2,1)}, u32[]{:S(2)}, u32[]{:S(2)}) collective-permute-start(bf16[16,144,256]{2,1,0:T(8,128)(2,1)} %copy-done.7), channel_id=1, source_target_pairs={{0,64},{64,0},{128,192},{192,128},{256,320},{320,256},{384,448},{4... | collective-permute-start | bytes 3538952 | tf_op jit(solution)/shard_map/ppermute | solution.py:295
  77.0 0.9 copy-start.4
  77.9 1.2 copy-start.3
  79.1 1.1 copy-start.5
  80.2 6.2 %copy-start.9 = (s32[1,2,128]{2,1,0:T(2,128)S(1)}, s32[1,2,128]{2,1,0:T(2,128)}, u32[]{:S(2)}) copy-start(s32[1,2,128]{2,1,0:T(2,128)} %param.8) | copy-start | bytes 3076
  80.2 6.4 %copy-start.8 = (bf16[64,512]{1,0:T(8,128)(2,1)S(1)}, bf16[64,512]{1,0:T(8,128)(2,1)}, u32[]{:S(2)}) copy-start(bf16[64,512]{1,0:T(8,128)(2,1)} %param.11) | copy-start | bytes 196612
  82.0 6.8 %collective-permute-start.3 = (f32[256,640]{1,0:T(8,128)}, f32[256,640]{1,0:T(8,128)}, u32[]{:S(2)}, u32[]{:S(2)}) collective-permute-start(f32[256,640]{1,0:T(8,128)} %last.3), channel_id=1, source_target_pairs={{0,32},{32,0},{1,33},{33,1},{2,34},{34,2},{3,35},{35,3},{4,36},{36... | collective-permute-start | bytes 1966088 | tf_op jit(solution)/shard_map/ppermute | solution.py:299
  86.6 1.2 copy-start.2
  87.8 2.2 %copy-start.1 = (bf16[1,2,128,8192]{3,2,1,0:T(8,128)(2,1)S(1)}, bf16[1,2,128,8192]{3,2,1,0:T(8,128)(2,1)}, u32[]{:S(2)}) copy-start(bf16[1,2,128,8192]{3,2,1,0:T(8,128)(2,1)} %param.6) | copy-start | bytes 12582916
  87.8 2.2 %copy-start.6 = (bf16[1,2,128,512]{3,2,1,0:T(8,128)(2,1)S(1)}, bf16[1,2,128,512]{3,2,1,0:T(8,128)(2,1)}, u32[]{:S(2)}) copy-start(bf16[1,2,128,512]{3,2,1,0:T(8,128)(2,1)} %param.7) | copy-start | bytes 786436
  117.4 21.2 %all-to-all-start.3 = ((bf16[16,16,256]{2,1,0:T(8,128)(2,1)}), bf16[16,16,256]{2,1,0:T(8,128)(2,1)S(1)}, u32[]{:S(2)}, u32[]{:S(2)}) async-start(bf16[16,16,256]{2,1,0:T(8,128)(2,1)} %plane.1), calls=%async_computation.3 | async-start | bytes 262144 | tf_op jit(solution)/shard_map/all_to_all | solution.py:323
  146.8 13.1 %all-to-all-start.4 = ((f32[8,8,256]{2,1,0:T(8,128)}), f32[8,8,256]{2,1,0:T(8,128)S(1)}, u32[]{:S(2)}, u32[]{:S(2)}) async-start(f32[8,8,256]{2,1,0:T(8,128)} %broadcast_in_dim.8), calls=%async_computation.4 | async-start | bytes 131072 | tf_op jit(solution)/shard_map/all_to_all | solution.py:334

commit v8 on v7

--- a/solution.py
+++ b/solution.py
@@ -329,11 +329,12 @@
         compiler_params=params(),
         name="gate",
     )(got)
-    summed, diffs = lax.optimization_barrier((lax.psum(gated, "core"), diffs))
     rows = rank // ZL
-    all_rows = lax.all_to_all(jnp.broadcast_to(summed[None, :rows], (ZL, rows, wide)), "zl", 0, 0)
-    down_gradient = all_rows.reshape(rank, wide).T
-    up_part = jnp.concatenate([summed[8:16, :rank], summed[8:16, rank : 2 * rank]], axis=0)
+    copies = jnp.broadcast_to(gated[None, :rows], (ZL * 2, rows, wide))
+    all_rows = lax.all_to_all(copies, ("zl", "core"), 0, 0)
+    down_gradient = jnp.sum(all_rows.reshape(ZL, 2, rows, wide), axis=1).reshape(rank, wide).T
+    summed = lax.psum(gated[8:, : 2 * rank], "core")
+    up_part = jnp.concatenate([summed[:, :rank], summed[:, rank:]], axis=0)
     margin = DPO_BETA * lax.dynamic_slice(diffs, (zl, 0), (1, 1)).reshape(1)
     return down_gradient, up_part, jax.nn.softplus(-margin), margin
 

time: 163 us -> 159 us (0.975)
  blocking collectives: 30.2 us -> 47.5 us
  waiting for transfers between devices: 55.6 us -> 40.8 us
  starting transfers between devices: 45.4 us -> 40.5 us
    all_to_all x0 -> x1, blocking collectives: none -> 21 us  [shards(): got = lax.all_to_all(along, ZZ, 0, 0)]
    all_to_all x2 -> x1, waiting for transfers between devices: 22.4 us -> 7.66 us  [shards(): all_rows = lax.all_to_all(copies, ('zl', 'core'), 0, 0)]
    all_to_all x2 -> x1, starting transfers between devices: 11.2 us -> 6.25 us  [shards(): all_rows = lax.all_to_all(copies, ('zl', 'core'), 0, 0)]
    psum x1, blocking collectives: 6.15 us -> 2.48 us  [shards(): summed = lax.psum(gated[8:, :2 * rank], 'core')]
    unnamed x21 -> x20, local copies, waits for them, and re-layouts: 6.24 us -> 5.6 us
  transfers between devices with their start and end apart: 8 -> 7, of which waited for: 4 -> 3; matrix products, arithmetic and copies ran while one was open for 3% -> 3% of each run, Pallas kernels for 6% -> 7%
where the time goes in v8:
time: 159 us
  blocking collectives  47.5 us (30%)
  waiting for transfers between devices  40.8 us (26%)
  starting transfers between devices  40.5 us (25%)
  Pallas kernels  15 us (9%)
  local copies, waits for them, and re-layouts  10.2 us (6%)
  between operations  2.73 us (2%)
  other arithmetic  1.87 us (1%)
    all_to_all x1, blocking collectives, shards(): got = lax.all_to_all(sends, XY, 0, 0)  24.1 us
    all_to_all x1, blocking collectives, shards(): got = lax.all_to_all(along, ZZ, 0, 0)  21 us
    ppermute x1, waiting for transfers between devices, shards(): passed = lax.ppermute(near, 'zl', [(a, a ^ 1) for a in range(ZL)])  19.6 us
    ppermute x1, waiting for transfers between devices, shards(): weights_far = lax.ppermute(weights, axes, mirror)  13.5 us
    all_to_all x2, starting transfers between devices, plane_gather(): lax.all_to_all(jnp.broadcast_to(w[None], (X * Y,) + w.shape), XY, 0, 0)  10.2 us
    ppermute x1, starting transfers between devices, shards(): other = lax.ppermute(hidden, 'core', swap_core)  8.92 us
    ppermute x1, starting transfers between devices, shards(): weights_far = lax.ppermute(weights, axes, mirror)  8.81 us
    all_to_all x1, waiting for transfers between devices, shards(): all_rows = lax.all_to_all(copies, ('zl', 'core'), 0, 0)  7.66 us
  transfers between devices with their start and end apart: 7, of which 3 were waited for; matrix products, arithmetic and copies ran while one was open for 3% of the time, Pallas kernels for 7%

profile of v8, /device:TPU:1, one launch (start us, length us, event | category | flops | bytes accessed | tf_op | source)
XLA Modules:
  0.0 158.6 jit_solution(5725293749690146479)
XLA Ops:
  0.6 8.9 %collective-permute-start = (bf16[256,8192]{1,0:T(8,128)(2,1)}, bf16[256,8192]{1,0:T(8,128)(2,1)}, u32[]{:S(2)}, u32[]{:S(2)}) collective-permute-start(bf16[256,8192]{1,0:T(8,128)(2,1)} %bitcast.21), channel_id=1, source_target_pairs={{0,32},{32,0},{1,33},{33,1},{2,34},{34,2},{3,35},{35,3},{4,36},{36... | collective-permute-start | bytes 12582920 | tf_op jit(solution)/shard_map/ppermute | solution.py:291
  9.6 0.7 constant_dynamic-slice_fusion.1
  10.4 1.1 broadcast_in_dim.6
  11.5 3.7 %all-to-all-start = ((bf16[16,144,256]{2,1,0:T(8,128)(2,1)}), bf16[16,144,256]{2,1,0:T(8,128)(2,1)S(1)}, u32[]{:S(2)}, u32[]{:S(2)}) async-start(bf16[16,144,256]{2,1,0:T(8,128)(2,1)} %broadcast_in_dim.6), calls=%async_computation | async-start | bytes 2359296 | tf_op jit(solution)/shard_map/all_to_all | solution.py:183
  15.2 8.8 %collective-permute-start.1 = (bf16[144,512]{1,0:T(8,128)(2,1)S(1)}, bf16[144,512]{1,0:T(8,128)(2,1)S(1)}, u32[]{:S(2)}, u32[]{:S(2)}) collective-permute-start(bf16[144,512]{1,0:T(8,128)(2,1)S(1)} %pad_maximum_fusion), channel_id=1, source_target_pairs={{0,452},{1,453},{2,454},{3,455},{4,448},{5,449},{6,450},{7,451},{8... | collective-permute-start | bytes 442376 | tf_op jit(solution)/shard_map/ppermute | solution.py:288
  24.0 13.5 %collective-permute-done.1 = bf16[144,512]{1,0:T(8,128)(2,1)S(1)} collective-permute-done((bf16[144,512]{1,0:T(8,128)(2,1)S(1)}, bf16[144,512]{1,0:T(8,128)(2,1)S(1)}, u32[]{:S(2)}, u32[]{:S(2)}) %collective-permute-start.1) | collective-permute-done | bytes 147488 | tf_op jit(solution)/shard_map/ppermute | solution.py:288
  37.5 1.8 %broadcast_in_dim.7 = bf16[16,144,512]{2,1,0:T(8,128)(2,1)} broadcast(bf16[144,512]{1,0:T(8,128)(2,1)S(1)} %collective-permute-done.1), dimensions={1,2} | broadcast | bytes 2506752 | tf_op jit(solution)/shard_map/broadcast_in_dim | solution.py:183
  39.3 6.5 %all-to-all-start.1 = ((bf16[16,144,512]{2,1,0:T(8,128)(2,1)}), bf16[16,144,512]{2,1,0:T(8,128)(2,1)S(1)}, u32[]{:S(2)}, u32[]{:S(2)}) async-start(bf16[16,144,512]{2,1,0:T(8,128)(2,1)} %broadcast_in_dim.7), calls=%async_computation.1 | async-start | bytes 4718592 | tf_op jit(solution)/shard_map/all_to_all | solution.py:183
  45.9 1.9 %collective-permute-start.2 = (bf16[16,144,256]{2,1,0:T(8,128)(2,1)}, bf16[16,144,256]{2,1,0:T(8,128)(2,1)}, u32[]{:S(2)}, u32[]{:S(2)}) collective-permute-start(bf16[16,144,256]{2,1,0:T(8,128)(2,1)} %copy-done.7), channel_id=1, source_target_pairs={{0,64},{64,0},{128,192},{192,128},{256,320},{320,256},{384,448},{4... | collective-permute-start | bytes 3538952 | tf_op jit(solution)/shard_map/ppermute | solution.py:295
  47.9 6.9 %own.1 = (f32[256,640]{1,0:T(8,128)S(1)}, f32[256,640]{1,0:T(8,128)S(1)}, bf16[256,2048]{1,0:T(8,128)(2,1)S(1)}, bf16[256,2048]{1,0:T(8,128)(2,1)S(1)}, bf16[256...) custom-call(s32[3]{0:T(128)S(1)} %pad_add_fusion.where_ref, bf16[256,8192]{1,0:T(8,128)(2,1)} %bitcast.22, ...), custom_call_target="tpu_custom_call" | custom-call | tf_op jit(solution)/shard_map/own/pallas_call | solution.py:149
  54.7 19.6 %collective-permute-done.2.passed_ref = bf16[16,144,256]{2,1,0:T(8,128)(2,1)} collective-permute-done((bf16[16,144,256]{2,1,0:T(8,128)(2,1)}, bf16[16,144,256]{2,1,0:T(8,128)(2,1)}, u32[]{:S(2)}, u32[]{:S(2)}) %collective-permute-start.2) | collective-permute-done | bytes 1179680 | tf_op jit(solution)/shard_map/ppermute | solution.py:295
  74.4 2.6 %passed.1 = (f32[256,640]{1,0:T(8,128)S(1)}, f32[256,640]{1,0:T(8,128)S(1)}) custom-call(s32[3]{0:T(128)S(1)} %pad_add_fusion.where_ref, bf16[256,2048]{1,0:T(8,128)(2,1)S(1)} %get-tuple-element.19.mine_ref, bf16[256,2048]{1,0:T(8,128)(2,1)S(1)} %get-tuple-element.20.other_ref, bf16[16,144,256]{2,1,0:T(8,128)(2,1)} %collective-permute-done.2.passed_ref, ...), custom_call_target="tpu_custom_call" | custom-call | tf_op jit(solution)/shard_map/passed/pallas_call | solution.py:161
  77.0 0.8 copy-done.4
  77.8 1.2 copy-done.3
  79.1 1.1 copy-done.5
  80.2 1.8 %last.3 = f32[256,640]{1,0:T(8,128)} custom-call(bf16[256,2048]{1,0:T(8,128)(2,1)S(1)} %copy-done.3, bf16[16,144,512]{2,1,0:T(8,128)(2,1)S(1)} %all-to-all-done.1.weight_ref, f32[256,640]{1,0:T(8,128)S(1)} %copy-done.5), custom_call_target="tpu_custom_call" | custom-call | tf_op jit(solution)/shard_map/last/pallas_call | solution.py:172
  82.0 4.4 %collective-permute-start.3 = (f32[256,640]{1,0:T(8,128)}, f32[256,640]{1,0:T(8,128)}, u32[]{:S(2)}, u32[]{:S(2)}) collective-permute-start(f32[256,640]{1,0:T(8,128)} %last.3), channel_id=1, source_target_pairs={{0,32},{32,0},{1,33},{33,1},{2,34},{34,2},{3,35},{35,3},{4,36},{36... | collective-permute-start | bytes 1966088 | tf_op jit(solution)/shard_map/ppermute | solution.py:299
  86.4 0.1 copy.14.mask_ref
  86.5 1.2 copy-done.2
  87.8 1.0 last.2.mine_ref
  88.8 1.2 copy-done.1
  90.0 2.4 %middle.1 = bf16[16,144,256]{2,1,0:T(8,128)(2,1)S(1)} custom-call(f32[256,640]{1,0:T(8,128)S(1)} %last.2.mine_ref, f32[256,640]{1,0:T(8,128)} %collective-permute-done.3.other_ref, bf16[256,8192]{1,0:T(8,128)(2,1)S(1)} %bitcast.23, bf16[256,512]{1,0:T(8,128)(2,1)S(1)} %bitcast.24, f32[256,1]{1,0:T(8,128)S(1)} %copy.14.mask_ref, bf16[128,512]{1,0:T(8,128)(2,1)S(1)} %pad.4.up_ref), custom_call_target="tpu_custom_call" | custom-call | tf_op jit(solution)/shard_map/middle/pallas_call | solution.py:306
  92.4 24.1 %all_to_all.25.got_ref = bf16[16,144,256]{2,1,0:T(8,128)(2,1)S(1)} all-to-all(bf16[16,144,256]{2,1,0:T(8,128)(2,1)S(1)} %middle.1), channel_id=1, replica_groups=mesh['zl'=8,'core'=2,'x'=4,'zh'=2,'y'=4] {'x','y'}, dimensions={0} | all-to-all | bytes 2359296 | tf_op jit(solution)/shard_map/all_to_all | solution.py:314
  116.5 0.2 plane.1
  116.7 21.0 %all_to_all.26.got_ref = bf16[16,16,256]{2,1,0:T(8,128)(2,1)S(1)} all-to-all(bf16[16,16,256]{2,1,0:T(8,128)(2,1)S(1)} %plane.1), channel_id=1, replica_groups=mesh['zl'=8,'core'=2,'x'=4,'zh'=2,'y'=4] {'zl','zh'}, dimensions={0} | all-to-all | bytes 262144 | tf_op jit(solution)/shard_map/all_to_all | solution.py:323
  137.8 0.7 broadcast_in_dim.8
  138.5 6.3 %all-to-all-start.4 = ((f32[16,8,256]{2,1,0:T(8,128)}), f32[16,8,256]{2,1,0:T(8,128)S(1)}, u32[]{:S(2)}, u32[]{:S(2)}) async-start(f32[16,8,256]{2,1,0:T(8,128)} %broadcast_in_dim.8), calls=%async_computation.4 | async-start | bytes 262144 | tf_op jit(solution)/shard_map/all_to_all | solution.py:334
  144.7 0.5 fusion.2
  146.0 2.5 %psum.7 = f32[8,128]{1,0:T(8,128)S(1)} all-reduce(f32[8,128]{1,0:T(8,128)S(1)} %slice.13), channel_id=1, replica_groups=mesh['zl'=8,'core'=2,'x'=4,'zh'=2,'y'=4] {'core'}, use_global_device_ids=true, to_apply=%region_1.2 | all-reduce | flops 1024 | bytes 8192 | tf_op jit(solution)/shard_map/psum | solution.py:336
  148.6 0.6 pad_maximum_fusion.1
  149.2 7.7 %all-to-all-done.4 = f32[16,8,256]{2,1,0:T(8,128)S(1)} async-done(((f32[16,8,256]{2,1,0:T(8,128)}), f32[16,8,256]{2,1,0:T(8,128)S(1)}, u32[]{:S(2)}, u32[]{:S(2)}) %all-to-all-start.4) | async-done | bytes 131104 | tf_op jit(solution)/shard_map/all_to_all | solution.py:334
  156.8 0.6 bitcast_reduce_fusion
  (30 shorter events, 0.4 us)
Async XLA Ops:
  0.6 9.7 %copy-start = (bf16[256,512]{1,0:T(8,128)(2,1)S(1)}, bf16[256,512]{1,0:T(8,128)(2,1)}, u32[]{:S(2)}) copy-start(bf16[256,512]{1,0:T(8,128)(2,1)} %param.9) | copy-start | bytes 786436
  0.6 47.2 %collective-permute-start = (bf16[256,8192]{1,0:T(8,128)(2,1)}, bf16[256,8192]{1,0:T(8,128)(2,1)}, u32[]{:S(2)}, u32[]{:S(2)}) collective-permute-start(bf16[256,8192]{1,0:T(8,128)(2,1)} %bitcast.21), channel_id=1, source_target_pairs={{0,32},{32,0},{1,33},{33,1},{2,34},{34,2},{3,35},{35,3},{4,36},{36... | collective-permute-start | bytes 12582920 | tf_op jit(solution)/shard_map/ppermute | solution.py:291
  11.5 26.0 %all-to-all-start = ((bf16[16,144,256]{2,1,0:T(8,128)(2,1)}), bf16[16,144,256]{2,1,0:T(8,128)(2,1)S(1)}, u32[]{:S(2)}, u32[]{:S(2)}) async-start(bf16[16,144,256]{2,1,0:T(8,128)(2,1)} %broadcast_in_dim.6), calls=%async_computation | async-start | bytes 2359296 | tf_op jit(solution)/shard_map/all_to_all | solution.py:183
  15.2 22.3 %collective-permute-start.1 = (bf16[144,512]{1,0:T(8,128)(2,1)S(1)}, bf16[144,512]{1,0:T(8,128)(2,1)S(1)}, u32[]{:S(2)}, u32[]{:S(2)}) collective-permute-start(bf16[144,512]{1,0:T(8,128)(2,1)S(1)} %pad_maximum_fusion), channel_id=1, source_target_pairs={{0,452},{1,453},{2,454},{3,455},{4,448},{5,449},{6,450},{7,451},{8... | collective-permute-start | bytes 442376 | tf_op jit(solution)/shard_map/ppermute | solution.py:288
  37.5 1.8 %copy-start.7 = (bf16[16,144,256]{2,1,0:T(8,128)(2,1)}, bf16[16,144,256]{2,1,0:T(8,128)(2,1)S(1)}, u32[]{:S(2)}) copy-start(bf16[16,144,256]{2,1,0:T(8,128)(2,1)S(1)} %all-to-all-done.own_ref) | copy-start | bytes 3538948
  39.3 38.5 %all-to-all-start.1 = ((bf16[16,144,512]{2,1,0:T(8,128)(2,1)}), bf16[16,144,512]{2,1,0:T(8,128)(2,1)S(1)}, u32[]{:S(2)}, u32[]{:S(2)}) async-start(bf16[16,144,512]{2,1,0:T(8,128)(2,1)} %broadcast_in_dim.7), calls=%async_computation.1 | async-start | bytes 4718592 | tf_op jit(solution)/shard_map/all_to_all | solution.py:183
  45.9 28.5 %collective-permute-start.2 = (bf16[16,144,256]{2,1,0:T(8,128)(2,1)}, bf16[16,144,256]{2,1,0:T(8,128)(2,1)}, u32[]{:S(2)}, u32[]{:S(2)}) collective-permute-start(bf16[16,144,256]{2,1,0:T(8,128)(2,1)} %copy-done.7), channel_id=1, source_target_pairs={{0,64},{64,0},{128,192},{192,128},{256,320},{320,256},{384,448},{4... | collective-permute-start | bytes 3538952 | tf_op jit(solution)/shard_map/ppermute | solution.py:295
  77.0 0.8 copy-start.4
  77.8 1.2 copy-start.3
  79.1 1.1 copy-start.5
  80.2 6.2 %copy-start.9 = (s32[1,2,128]{2,1,0:T(2,128)S(1)}, s32[1,2,128]{2,1,0:T(2,128)}, u32[]{:S(2)}) copy-start(s32[1,2,128]{2,1,0:T(2,128)} %param.8) | copy-start | bytes 3076
  80.2 6.4 %copy-start.8 = (bf16[64,512]{1,0:T(8,128)(2,1)S(1)}, bf16[64,512]{1,0:T(8,128)(2,1)}, u32[]{:S(2)}) copy-start(bf16[64,512]{1,0:T(8,128)(2,1)} %param.11) | copy-start | bytes 196612
  82.0 6.8 %collective-permute-start.3 = (f32[256,640]{1,0:T(8,128)}, f32[256,640]{1,0:T(8,128)}, u32[]{:S(2)}, u32[]{:S(2)}) collective-permute-start(f32[256,640]{1,0:T(8,128)} %last.3), channel_id=1, source_target_pairs={{0,32},{32,0},{1,33},{33,1},{2,34},{34,2},{3,35},{35,3},{4,36},{36... | collective-permute-start | bytes 1966088 | tf_op jit(solution)/shard_map/ppermute | solution.py:299
  86.5 1.2 copy-start.2
  87.8 2.2 %copy-start.1 = (bf16[1,2,128,8192]{3,2,1,0:T(8,128)(2,1)S(1)}, bf16[1,2,128,8192]{3,2,1,0:T(8,128)(2,1)}, u32[]{:S(2)}) copy-start(bf16[1,2,128,8192]{3,2,1,0:T(8,128)(2,1)} %param.6) | copy-start | bytes 12582916
  87.8 2.2 %copy-start.6 = (bf16[1,2,128,512]{3,2,1,0:T(8,128)(2,1)S(1)}, bf16[1,2,128,512]{3,2,1,0:T(8,128)(2,1)}, u32[]{:S(2)}) copy-start(bf16[1,2,128,512]{3,2,1,0:T(8,128)(2,1)} %param.7) | copy-start | bytes 786436
  138.5 18.3 %all-to-all-start.4 = ((f32[16,8,256]{2,1,0:T(8,128)}), f32[16,8,256]{2,1,0:T(8,128)S(1)}, u32[]{:S(2)}, u32[]{:S(2)}) async-start(f32[16,8,256]{2,1,0:T(8,128)} %broadcast_in_dim.8), calls=%async_computation.4 | async-start | bytes 262144 | tf_op jit(solution)/shard_map/all_to_all | solution.py:334
